TPU v7x, 512 devices: a whole 4x4x16 slice. The times are simulated.
512 devices in a mesh: space: 32 (over z, y_lo), filt: 16 (over y_hi, x, core).
Axes of the slice: x: 4, y: 4 (y_hi: 2, y_lo: 2; y = y_hi * 2 + y_lo), z: 16, core: 2. Of those that a mesh axis runs over, the one named last changes fastest.
Arguments:
- volume: bfloat16 [32, 256, 2, 128], P('space', 'filt'), may hold values from -6 to 6
- first_weight: bfloat16 [128, 64, 256], P('filt'), may hold values from -0.125 to 0.125
- first_bias: bfloat16 [128], P('filt'), may hold values from -3 to 3
- second_weight: bfloat16 [128, 27, 128], P('filt'), may hold values from -0.109375 to 0.109375
- second_bias: bfloat16 [128], P('filt'), may hold values from -3 to 3
- cotangent: bfloat16 [64, 128, 4, 256], P('space', 'filt'), may hold values from -6 to 6
Outputs:
- result: bfloat16 [64, 128, 4, 256], P('space', 'filt')
- grad_volume: bfloat16 [32, 256, 2, 128], P('space', 'filt')
- grad_first: float32 [128, 64, 256], P('filt')
- grad_first_bias: float32 [128], P('filt')
- grad_second: float32 [128, 27, 128], P('filt')
- grad_second_bias: float32 [128], P('filt')
All inputs are finite; a program needn't handle non-finite values.
Results may differ from a plain program's by a relative error of at most 0.0085.
Values may be sent and summed in bfloat16 or wider, within the bound.
No kernel may reach another device: no remote copies, remote signals or barrier semaphores. Data moves between devices by JAX's collectives and lax.ppermute only.
A program may use at most 64 MiB of HBM per device.

v0:
```python
import math

import jax
import jax.numpy as jnp
from jax import lax
from jax.sharding import PartitionSpec as P

TAP_PLACE = ((1, 1), (0, 0), (1, 0), (0, -1))


def with_halo(block, sides, width):
    for axis, dim in sides:
        count = lax.axis_size(axis)
        forward = [(i, i + 1) for i in range(count - 1)]
        forward.append((count - 1, 0))
        backward = [(target, source) for source, target in forward]
        low = lax.ppermute(
            lax.slice_in_dim(block, block.shape[dim] - width, None, axis=dim), axis, forward
        )
        high = lax.ppermute(lax.slice_in_dim(block, 0, width, axis=dim), axis, backward)
        block = jnp.concatenate([low, block, high], axis=dim)
    return block


def widen(field):
    rimmed = with_halo(field, (("space", 0),), 1)
    return lax.all_gather(rimmed, "filt", axis=1, tiled=True)


def alternate(parts):
    stacked = jnp.stack(parts)
    planes, channels, extent_x, extent_y = stacked.shape[1:]
    stacked = stacked.reshape(2, 2, 2, planes, channels, extent_x, extent_y)
    return stacked.transpose(3, 0, 4, 5, 1, 6, 2).reshape(
        2 * planes, channels, 2 * extent_x, 2 * extent_y
    )


def lift(source_wide, weight, planes_in):
    parts = {}
    for tap_z in range(4):
        parity_z, offset_z = TAP_PLACE[tap_z]
        block = jnp.einsum(
            "dkc,zcxy->zkdxy",
            weight[:, tap_z * 16 : (tap_z + 1) * 16, :],
            source_wide,
            preferred_element_type=jnp.float32,
        )
        layer = block[1 + offset_z : 1 + offset_z + planes_in]
        for tap_x in range(4):
            parity_x, offset_x = TAP_PLACE[tap_x]
            for tap_y in range(4):
                parity_y, offset_y = TAP_PLACE[tap_y]
                term = jnp.roll(layer[:, tap_x * 4 + tap_y], (-offset_x, -offset_y), axis=(2, 3))
                place = (parity_z, parity_x, parity_y)
                parts[place] = parts[place] + term if place in parts else term
    return alternate(
        [
            parts[first, second, third]
            for first in range(2)
            for second in range(2)
            for third in range(2)
        ]
    )


def mix_forward(hidden_wide, weight, planes_out):
    total = None
    for shift_z in (-1, 0, 1):
        group = shift_z + 1
        layer = hidden_wide[1 + shift_z : 1 + shift_z + planes_out]
        block = jnp.einsum(
            "dkc,zcxy->zkdxy",
            weight[:, group * 9 : group * 9 + 9, :],
            layer,
            preferred_element_type=jnp.float32,
        )
        for shift_x in (-1, 0, 1):
            for shift_y in (-1, 0, 1):
                term = jnp.roll(
                    block[:, (shift_x + 1) * 3 + shift_y + 1], (-shift_x, -shift_y), axis=(2, 3)
                )
                total = term if total is None else total + term
    return total


def mix_backward(grad_wide, turned, planes_out):
    total = None
    for shift_z in (-1, 0, 1):
        group = shift_z + 1
        layer = grad_wide[1 - shift_z : 1 - shift_z + planes_out]
        block = jnp.einsum(
            "dkc,zdxy->zkcxy",
            turned[:, group * 9 : group * 9 + 9, :],
            layer,
            preferred_element_type=jnp.float32,
        )
        for shift_x in (-1, 0, 1):
            for shift_y in (-1, 0, 1):
                term = jnp.roll(
                    block[:, (shift_x + 1) * 3 + shift_y + 1], (shift_x, shift_y), axis=(2, 3)
                )
                total = term if total is None else total + term
    return total


def second_grad(hidden_wide, dpre, planes_out):
    pieces = []
    for shift_z in (-1, 0, 1):
        layer = hidden_wide[1 + shift_z : 1 + shift_z + planes_out]
        shifted = jnp.stack(
            [
                jnp.roll(dpre, (shift_x, shift_y), axis=(2, 3))
                for shift_x in (-1, 0, 1)
                for shift_y in (-1, 0, 1)
            ],
            axis=1,
        )
        pieces.append(
            jnp.einsum("zkdxy,zcxy->dkc", shifted, layer, preferred_element_type=jnp.float32)
        )
    return jnp.concatenate(pieces, axis=1)


def tap_columns(grad_wide, planes_in, tap_z):
    layer = grad_wide[tap_z : tap_z + 2 * planes_in : 2]
    columns = []
    for tap_x in range(4):
        parity_x = (tap_x - 1) % 2
        offset_x = (tap_x - 1) // 2
        for tap_y in range(4):
            parity_y = (tap_y - 1) % 2
            offset_y = (tap_y - 1) // 2
            picked = layer[:, :, parity_x::2, parity_y::2]
            columns.append(jnp.roll(picked, (-offset_x, -offset_y), axis=(2, 3)))
    return jnp.stack(columns, axis=1)


def per_device(volume, first_weight, first_bias, second_weight, second_bias, cotangent):
    planes_in = volume.shape[0]
    planes_out = 2 * planes_in
    source_wide = widen(volume)
    lifted = (
        lift(source_wide, first_weight, planes_in)
        + first_bias.astype(jnp.float32)[None, :, None, None]
    )
    hidden = lifted.astype(jnp.bfloat16)
    hidden_wide = widen(hidden)
    pre = (
        mix_forward(hidden_wide, second_weight, planes_out)
        + second_bias.astype(jnp.float32)[None, :, None, None]
    )
    sigma = jax.nn.sigmoid(pre)
    result = (pre * sigma).astype(jnp.bfloat16)
    dpre = (cotangent.astype(jnp.float32) * sigma * (1.0 + pre * (1.0 - sigma))).astype(
        jnp.bfloat16
    )
    dpre_wide = widen(dpre)
    turned = lax.all_to_all(second_weight, "filt", split_axis=2, concat_axis=0, tiled=True)
    dhidden = mix_backward(dpre_wide, turned, planes_out).astype(jnp.bfloat16)
    raw_second = second_grad(hidden_wide, dpre, planes_out)
    raw_second_bias = jnp.sum(dpre.astype(jnp.float32), axis=(0, 2, 3))
    raw_first_bias = jnp.sum(dhidden.astype(jnp.float32), axis=(0, 2, 3))
    source = source_wide[1 : 1 + planes_in]
    grad_wide = with_halo(dhidden, (("space", 0),), 1)
    own_columns = jnp.concatenate(
        [tap_columns(grad_wide, planes_in, tap_z) for tap_z in range(4)], axis=1
    )
    raw_first = jnp.einsum(
        "zkdxy,zcxy->dkc", own_columns, source, preferred_element_type=jnp.float32
    )
    partial_terms = jnp.einsum(
        "zkdxy,dkc->zcxy", own_columns, first_weight, preferred_element_type=jnp.float32
    )
    input_grad = lax.psum_scatter(partial_terms, "filt", scatter_dimension=1, tiled=True)
    summed = lax.psum((raw_first, raw_first_bias, raw_second, raw_second_bias), "space")
    total_cells = planes_out * cotangent.shape[2] * cotangent.shape[3] * lax.axis_size("space")
    scale = 1.0 / math.sqrt(total_cells)
    return (
        result,
        input_grad.astype(jnp.bfloat16),
        summed[0] * scale,
        summed[1] * scale,
        summed[2] * scale,
        summed[3] * scale,
    )


def solution(mesh):
    placed = (
        P("space", "filt", None, None),
        P("filt", None, None),
        P("filt"),
        P("filt", None, None),
        P("filt"),
        P("space", "filt", None, None),
    )
    return jax.shard_map(
        per_device,
        mesh=mesh,
        in_specs=placed,
        out_specs=(
            P("space", "filt", None, None),
            P("space", "filt", None, None),
            P("filt", None, None),
            P("filt"),
            P("filt", None, None),
            P("filt"),
        ),
        check_vma=False,
    )
```

profile of v0, /device:TPU:24, one launch (start us, length us, event | category | flops | bytes accessed | tf_op | source)
XLA Modules:
  0.0 556.2 jit_solution(6400131447909899114)
XLA Ops:
  7.2 0.7 copy.366
  7.9 4.1 collective-permute-start
  12.0 1.9 collective-permute-start.1
  14.0 1.0 slice_bitcast_fusion.45
  15.0 3.5 collective-permute-done.1
  18.5 23.1 %all_gather.9 = bf16[3,256,2,128]{3,1,2,0:T(8,128)(2,1)S(1)} all-gather(bf16[3,16,2,128]{3,1,2,0:T(8,128)(2,1)S(1)} %pad_maximum_fusion.29), channel_id=1, replica_groups=mesh['space'=32,'filt'=16] {'filt'}, dimensions={1}, use_global_device_ids=true | all-gather | bytes 417792 | tf_op jit(solution)/shard_map/all_gather | solution.py:27
  45.8 0.5 copy.405
  46.8 2.0 collective-permute-start.2
  48.8 7.2 %collective-permute-start.3 = (bf16[1,8,4,256]{3,1,2,0:T(8,128)(2,1)S(1)}, bf16[1,8,4,256]{3,1,2,0:T(8,128)(2,1)S(1)}, u32[]{:S(2)}, u32[]{:S(2)}) collective-permute-start(bf16[1,8,4,256]{3,1,2,0:T(8,128)(2,1)S(1)} %get-tuple-element.168), channel_id=1, source_target_pairs={{16,0},{32,16},{48,32},{64,48},{80,64},{96,80},{112,96},{128,112},... | collective-permute-start | bytes 49160 | tf_op jit(solution)/shard_map/ppermute | solution.py:20
  56.0 1.4 collective-permute-done.3
  57.4 0.6 pad_maximum_fusion.27
  58.1 0.8 copy-done.3
  59.1 1.1 reshape.884
  60.2 6.8 %all-to-all-start = ((bf16[16,2,864]{2,1,0:T(2,128)(2,1)}), bf16[16,2,864]{2,1,0:T(2,128)(2,1)S(1)}, u32[]{:S(2)}, u32[]{:S(2)}) async-start(bf16[16,2,864]{2,1,0:T(2,128)(2,1)} %reshape.884), calls=%async_computation | async-start | bytes 114688 | tf_op jit(solution)/shard_map/all_to_all | solution.py:159
  67.1 0.6 copy-done.7
  67.8 1.3 dynamic-slice
  69.7 2.2 all-to-all-done
  71.9 0.7 reshape.885
  73.5 44.6 %all-gather.3.cloned.1.call-done = bf16[4,128,4,256]{3,1,2,0:T(8,128)(2,1)} async-done(((bf16[4,8,4,256]{3,1,2,0:T(8,128)(2,1)}), bf16[4,128,4,256]{3,1,2,0:T(8,128)(2,1)}) %all-gather.3.cloned.1.call-update) | async-done | bytes 1048592 | tf_op jit(solution)/shard_map/all_gather | solution.py:27
  118.1 1.3 convolution_bitcast_fusion.1
  119.4 0.5 fusion.235
  120.1 0.6 copy-done
  123.1 0.7 copy-done.5
  123.8 0.4 convert_reduce_fusion
  124.5 2.8 collective-permute-start.4
  127.3 3.0 collective-permute-start.5
  130.5 0.6 copy.443
  131.2 2.7 collective-permute-done.5
  133.9 0.6 pad_maximum_fusion.28
  136.2 0.7 pad_maximum_fusion
  136.8 58.6 %all-gather.5.cloned.1.call-done = bf16[4,128,4,256]{3,1,2,0:T(8,128)(2,1)} async-done(((bf16[4,8,4,256]{3,1,2,0:T(8,128)(2,1)}), bf16[4,128,4,256]{3,1,2,0:T(8,128)(2,1)}) %all-gather.5.cloned.1.call-update) | async-done | bytes 1048592 | tf_op jit(solution)/shard_map/all_gather | solution.py:27
  195.5 1.3 convolution_bitcast_fusion
  196.8 0.5 fusion.234
  197.5 0.6 copy-done.1
  200.5 0.4 convert_reduce_fusion.1
  200.9 0.5 slice.2414
  201.5 0.4 slice.2411
  202.1 0.5 slice.2406
  202.6 0.5 slice.2401
  203.2 2.1 collective-permute-start.7
  205.3 0.5 slice.2386
  205.9 0.4 slice.2383
  206.4 0.5 slice.2378
  207.0 0.5 slice.2373
  207.5 65.4 %all-reduce.1 = (f32[8]{0:T(128)S(1)}, f32[8]{0:T(128)S(1)}) all-reduce(f32[8]{0:T(128)S(1)} %get-tuple-element.37, f32[8]{0:T(128)S(1)} %get-tuple-element.34), channel_id=1, replica_groups=mesh['space'=32,'filt'=16] {'space'}, use_global_device_ids=true, to_apply=%region_3.4 | all-reduce | flops 16 | bytes 128 | tf_op jit(solution)/shard_map/psum | solution.py:176
  272.9 0.5 broadcast_multiply_fusion.2
  273.5 1.9 collective-permute-start.6
  276.0 0.4 slice.2442
  276.6 0.4 slice.2439
  277.1 0.5 slice.2434
  277.7 0.5 slice.2429
  278.3 0.9 collective-permute-done.6
  279.1 0.4 slice.2357
  279.7 0.4 slice.2354
  280.2 0.5 slice.2349
  280.8 0.5 slice.2344
  284.9 1.1 convolution_bitcast_fusion.6
  286.0 0.5 broadcast_multiply_fusion.3
  286.5 0.4 copy-done.2
  287.4 67.3 %all-reduce.7 = bf16[1,256,2,128]{3,2,0,1:T(2,128)(2,1)S(1)} all-reduce(f32[1,256,2,128]{3,2,0,1:T(2,128)S(1)} %copy.438), channel_id=2, replica_groups=mesh['space'=32,'filt'=16] {'filt'}, use_global_device_ids=true, to_apply=%region_0.1.clone | all-reduce | flops 65536 | bytes 393216
  354.7 0.6 fusion.130
  355.3 191.7 %all-reduce.6.cloned.1.call-done = (f32[8,64,256]{2,1,0:T(8,128)}, f32[8,27,128]{2,1,0:T(8,128)}) async-done(((f32[8,64,256]{2,1,0:T(8,128)}, f32[8,27,128]{2,1,0:T(8,128)}), (f32[8,64,256]{2,1,0:T(8,128)}, f32[8,27,128]{2,1,0:T(8,128)})) %all-reduce.6.cloned.1.call-update) | async-done | bytes 634896 | tf_op jit(solution)/shard_map/psum | solution.py:176
  547.0 1.9 broadcast_multiply_fusion
  548.9 0.7 copy.445
  (406 shorter events, 18.1 us)
Async XLA Ops:
  7.2 110.9 %all-gather.3.cloned.1.call-start = ((), (), s32[]{:S(2)}) async-start(), calls=%async_computation.1 | async-start | bytes 1114112 | tf_op jit(solution)/shard_map/all_gather | solution.py:27
  7.9 7.0 %copy-start.6 = (bf16[8]{0:T(256)(128)(2,1)S(1)}, bf16[8]{0:T(256)(128)(2,1)}, u32[]{:S(2)}) copy-start(bf16[8]{0:T(256)(128)(2,1)} %param.8) | copy-start | bytes 52
  7.9 7.1 %collective-permute-start = (bf16[1,16,2,128]{3,1,2,0:T(8,128)(2,1)S(1)}, bf16[1,16,2,128]{3,1,2,0:T(8,128)(2,1)S(1)}, u32[]{:S(2)}, u32[]{:S(2)}) collective-permute-start(bf16[1,16,2,128]{3,1,2,0:T(8,128)(2,1)S(1)} %copy.366), channel_id=1, source_target_pairs={{0,16},{16,32},{32,48},{48,64},{64,80},{80,96},{96,112},{112,128},... | collective-permute-start | bytes 24584 | tf_op jit(solution)/shard_map/ppermute | solution.py:17
  12.0 6.4 %collective-permute-start.1 = (bf16[1,16,2,128]{3,1,2,0:T(8,128)(2,1)S(1)}, bf16[1,16,2,128]{3,1,2,0:T(8,128)(2,1)S(1)}, u32[]{:S(2)}, u32[]{:S(2)}) collective-permute-start(bf16[1,16,2,128]{3,1,2,0:T(8,128)(2,1)S(1)} %copy.366), channel_id=1, source_target_pairs={{16,0},{32,16},{48,32},{64,48},{80,64},{96,80},{112,96},{128,112},... | collective-permute-start | bytes 24584 | tf_op jit(solution)/shard_map/ppermute | solution.py:20
  46.8 9.2 %collective-permute-start.2 = (bf16[1,8,4,256]{3,1,2,0:T(8,128)(2,1)S(1)}, bf16[1,8,4,256]{3,1,2,0:T(8,128)(2,1)S(1)}, u32[]{:S(2)}, u32[]{:S(2)}) collective-permute-start(bf16[1,8,4,256]{3,1,2,0:T(8,128)(2,1)S(1)} %get-tuple-element.167), channel_id=1, source_target_pairs={{0,16},{16,32},{32,48},{48,64},{64,80},{80,96},{96,112},{112,128},... | collective-permute-start | bytes 49160 | tf_op jit(solution)/shard_map/ppermute | solution.py:17
  48.8 8.7 %collective-permute-start.3 = (bf16[1,8,4,256]{3,1,2,0:T(8,128)(2,1)S(1)}, bf16[1,8,4,256]{3,1,2,0:T(8,128)(2,1)S(1)}, u32[]{:S(2)}, u32[]{:S(2)}) collective-permute-start(bf16[1,8,4,256]{3,1,2,0:T(8,128)(2,1)S(1)} %get-tuple-element.168), channel_id=1, source_target_pairs={{16,0},{32,16},{48,32},{64,48},{80,64},{96,80},{112,96},{128,112},... | collective-permute-start | bytes 49160 | tf_op jit(solution)/shard_map/ppermute | solution.py:20
  58.1 0.8 copy-start.3
  60.2 11.7 %all-to-all-start = ((bf16[16,2,864]{2,1,0:T(2,128)(2,1)}), bf16[16,2,864]{2,1,0:T(2,128)(2,1)S(1)}, u32[]{:S(2)}, u32[]{:S(2)}) async-start(bf16[16,2,864]{2,1,0:T(2,128)(2,1)} %reshape.884), calls=%async_computation | async-start | bytes 114688 | tf_op jit(solution)/shard_map/all_to_all | solution.py:159
  67.0 128.5 %all-gather.5.cloned.1.call-start = ((), (), s32[]{:S(2)}) async-start(), calls=%async_computation.2 | async-start | bytes 1114112 | tf_op jit(solution)/shard_map/all_gather | solution.py:27
  67.1 0.7 copy-start.7
  119.4 1.2 copy-start
  123.0 0.8 copy-start.5
  124.5 6.7 %collective-permute-start.4 = (bf16[1,8,4,256]{3,1,2,0:T(8,128)(2,1)S(1)}, bf16[1,8,4,256]{3,1,2,0:T(8,128)(2,1)S(1)}, u32[]{:S(2)}, u32[]{:S(2)}) collective-permute-start(bf16[1,8,4,256]{3,1,2,0:T(8,128)(2,1)S(1)} %get-tuple-element.165), channel_id=1, source_target_pairs={{0,16},{16,32},{32,48},{48,64},{64,80},{80,96},{96,112},{112,128},... | collective-permute-start | bytes 49160 | tf_op jit(solution)/shard_map/ppermute | solution.py:17
  127.3 6.5 %collective-permute-start.5 = (bf16[1,8,4,256]{3,1,2,0:T(8,128)(2,1)S(1)}, bf16[1,8,4,256]{3,1,2,0:T(8,128)(2,1)S(1)}, u32[]{:S(2)}, u32[]{:S(2)}) collective-permute-start(bf16[1,8,4,256]{3,1,2,0:T(8,128)(2,1)S(1)} %get-tuple-element.166), channel_id=1, source_target_pairs={{16,0},{32,16},{48,32},{64,48},{80,64},{96,80},{112,96},{128,112},... | collective-permute-start | bytes 49160 | tf_op jit(solution)/shard_map/ppermute | solution.py:20
  134.5 412.5 %all-reduce.6.cloned.1.call-start = ((), (), s32[]{:S(2)}) async-start(), calls=%async_computation.3 | async-start | bytes 1310720 | tf_op jit(solution)/shard_map/psum | solution.py:176
  196.8 1.2 copy-start.1
  203.2 72.8 %collective-permute-start.7 = (bf16[1,8,4,256]{3,1,2,0:T(8,128)(2,1)S(1)}, bf16[1,8,4,256]{3,1,2,0:T(8,128)(2,1)S(1)}, u32[]{:S(2)}, u32[]{:S(2)}) collective-permute-start(bf16[1,8,4,256]{3,1,2,0:T(8,128)(2,1)S(1)} %get-tuple-element.163), channel_id=1, source_target_pairs={{16,0},{32,16},{48,32},{64,48},{80,64},{96,80},{112,96},{128,112},... | collective-permute-start | bytes 49160 | tf_op jit(solution)/shard_map/ppermute | solution.py:20
  273.5 5.6 %collective-permute-start.6 = (bf16[1,8,4,256]{3,1,2,0:T(8,128)(2,1)S(1)}, bf16[1,8,4,256]{3,1,2,0:T(8,128)(2,1)S(1)}, u32[]{:S(2)}, u32[]{:S(2)}) collective-permute-start(bf16[1,8,4,256]{3,1,2,0:T(8,128)(2,1)S(1)} %get-tuple-element.164), channel_id=1, source_target_pairs={{0,16},{16,32},{32,48},{48,64},{64,80},{80,96},{96,112},{112,128},... | collective-permute-start | bytes 49160 | tf_op jit(solution)/shard_map/ppermute | solution.py:17
  286.0 1.0 copy-start.2
  547.0 1.9 copy-start.4
Sparse Core Ops, SparseCore 0:
  58.2 59.8 all-gather.2
  134.6 60.7 all-gather.4
  286.1 260.8 all-reduce.5
where the time goes:
time: 558 us; the launch traced here: 556 us
  waiting for transfers between devices  306 us (55%)
  blocking collectives  156 us (28%)
  starting transfers between devices  32.1 us (6%)
  local copies, waits for them, and re-layouts  25.1 us (4%)
  between operations  16.1 us (3%)
  other arithmetic  14.7 us (3%)
  matrix products  6.88 us (1%)
    psum x1, waiting for transfers between devices, per_device(): lax.psum((raw_first, raw_first_bias, raw_second, raw_second_bias), 'space')  192 us
    all_gather x2, waiting for transfers between devices, widen(): return lax.all_gather(rimmed, 'filt', axis=1, tiled=True)  103 us
    unnamed x1, blocking collectives  67.3 us
    psum x1, blocking collectives, per_device(): lax.psum((raw_first, raw_first_bias, raw_second, raw_second_bias), 'space')  65.4 us
    all_gather x1, blocking collectives, widen(): return lax.all_gather(rimmed, 'filt', axis=1, tiled=True)  23.1 us
    ppermute x4, starting transfers between devices, with_halo(): lax.ppermute(lax.slice_in_dim(block, 0, width, axis=dim), axis, backward)  14.2 us
  transfers between devices with their start and end apart: 12, of which 8 were waited for; matrix products, arithmetic and copies ran while one was open for 3% of the time, Pallas kernels for 0%

commit v1 on v0

v1 whole, which is shorter than its diff:
```python
import math

import jax
import jax.numpy as jnp
from jax import lax
from jax.experimental import pallas as pl
from jax.experimental.pallas import tpu as pltpu
from jax.sharding import PartitionSpec as P

F32 = jnp.float32
BF16 = jnp.bfloat16
TAP_PLACE = ((1, 1), (0, 0), (1, 0), (0, -1))
LANE = 128
PLANE = 1024
NEAR = 8


def vmem_call(body, outs, scratch=(), limit=24 * 1024 * 1024):
    return pl.pallas_call(
        body,
        out_shape=outs,
        scratch_shapes=list(scratch),
        compiler_params=pltpu.CompilerParams(vmem_limit_bytes=limit),
    )


def ahead(value, step):
    extent = value.shape[-1]
    return value if step == 0 else pltpu.roll(value, (-step) % extent, value.ndim - 1)


def dot(a, b, dims=((1,), (0,))):
    return lax.dot_general(a, b, (dims, ((), ())), preferred_element_type=F32)


def hidden_kernel(weight, source, bias, out, taps):
    taps[...] = dot(weight[...], source[...])

    def tap(kz, kx, ky, plane, xi):
        row = (kz * 16 + kx * 4 + ky) * 8
        col = plane * 256 + xi * LANE
        return taps[row : row + 8, col : col + LANE]

    for plane in range(4):
        parity_z = (plane + 1) % 2
        base_z = (plane + 1) // 2
        along_z = [(k, base_z + off) for k, (par, off) in enumerate(TAP_PLACE) if par == parity_z]
        for x in range(4):
            along_x = [
                (k, (x // 2 + off) % 2) for k, (par, off) in enumerate(TAP_PLACE) if par == x % 2
            ]
            for parity_y in range(2):
                total = bias[...]
                for ky, (par, off) in enumerate(TAP_PLACE):
                    if par != parity_y:
                        continue
                    part = None
                    for kz, iz in along_z:
                        for kx, ix in along_x:
                            term = tap(kz, kx, ky, iz, ix)
                            part = term if part is None else part + term
                    total = total + ahead(part, off)
                col = plane * PLANE + x * 256 + parity_y * LANE
                out[:, col : col + LANE] = total.astype(BF16)


def spread_rows(rows, cols):
    natural = lax.broadcasted_iota(jnp.int32, (rows, cols), 0)
    split = lax.broadcasted_iota(jnp.int32, (rows, cols), 1)
    return jnp.where(natural == 2 * (split % LANE) + split // LANE, 1.0, 0.0).astype(BF16)


def split_kernel(field, out, rows):
    rows[...] = dot(field[...], spread_rows(256, 256))
    for z in range(2):
        for x in range(4):
            col = z * PLANE + x * 256
            for e in range(8):
                line = z * 32 + e * 4 + x
                out[e : e + 1, col : col + 256] = rows[line : line + 1, :]


def activate_kernel(hidden, weight, bias, cot, result, dpre, taps, rows):
    taps[...] = dot(weight[...], hidden[...])

    def column(plane, x, parity):
        return plane * PLANE + (x % 4) * 256 + parity * LANE

    for z in range(2):
        for x in range(4):
            halves = []
            for parity in range(2):
                pre = bias[...]
                for ty in (-1, 0, 1):
                    other = (parity + ty) % 2
                    step = (parity + ty) // 2
                    part = None
                    for tz in range(3):
                        for tx in range(3):
                            row = (tz * 9 + tx * 3 + ty + 1) * 8
                            col = column(z + tz, x + tx - 1, other)
                            term = taps[row : row + 8, col : col + LANE]
                            part = term if part is None else part + term
                    pre = pre + ahead(part, step)
                sigma = 1.0 / (1.0 + jnp.exp(-pre))
                halves.append((pre * sigma).astype(BF16))
                col = column(z, x, parity)
                slope = cot[:, col : col + LANE] * sigma * (1.0 + pre * (1.0 - sigma))
                dpre[:, col : col + LANE] = slope.astype(BF16)
            both = jnp.concatenate(halves, axis=1)
            natural = dot(both, spread_rows(256, 256), ((1,), (1,)))
            for e in range(8):
                line = z * 32 + e * 4 + x
                rows[line : line + 1, :] = natural[e : e + 1, :]
    result[...] = rows[...].astype(BF16)


def mix_back_kernel(low, dpre, high, hidden, weight, share, raw, cols, colb):
    planes = (
        low[...].astype(F32),
        dpre[:, :PLANE].astype(F32),
        dpre[:, PLANE:].astype(F32),
        high[...].astype(F32),
    )

    def cells(plane, x, parity):
        col = (x % 4) * 256 + parity * LANE
        return planes[plane][:, col : col + LANE]

    for z in range(2):
        for tz in range(3):
            for x in range(4):
                for parity in range(2):
                    for ty in (-1, 0, 1):
                        other = (parity - ty) % 2
                        step = (parity - ty) // 2
                        for tx in range(3):
                            value = ahead(cells(z + 2 - tz, x - (tx - 1), other), step)
                            row = (tz * 9 + tx * 3 + ty + 1) * 8
                            col = z * PLANE + x * 256 + parity * LANE
                            cols[row : row + 8, col : col + LANE] = value
    cols[216:256, :] = jnp.zeros((40, 2 * PLANE), F32)
    colb[...] = cols[...].astype(BF16)
    share[...] = dot(weight[...], colb[...]).astype(BF16)
    raw[...] = dot(colb[...], hidden[...], ((1,), (1,)))
    total = jnp.sum(planes[1] + planes[2], axis=1, keepdims=True)
    raw[216:224, :] = jnp.broadcast_to(total, (8, LANE))


def pick_columns(field, out, base):
    for kx in range(4):
        for ky in range(4):
            parity, step = (ky - 1) % 2, (ky - 1) // 2
            for xi in range(2):
                x = (2 * xi - 1 + kx) % 4
                col = x * 256 + parity * LANE
                row = base + (kx * 4 + ky) * 8
                out[row : row + 8, xi * LANE : (xi + 1) * LANE] = ahead(
                    field[:, col : col + LANE], step
                )


def lift_back_kernel(parts, source, raw_second, dhidden, message, cols, raw, second):
    total = parts[0].astype(F32)
    for f in range(1, 16):
        total = total + parts[f].astype(F32)
    rounded = total.astype(BF16)
    dhidden[...] = rounded
    total = rounded.astype(F32)
    pick_columns(total[:, :PLANE], cols, 0)
    pick_columns(total[:, PLANE:], cols, LANE)
    for kz, (plane, place) in enumerate(((1, 2), (0, 1), (1, 1), (0, 0))):
        raw[kz * LANE : (kz + 1) * LANE, :] = dot(
            cols[plane * LANE : (plane + 1) * LANE, :].astype(BF16),
            source[:, place * 256 : (place + 1) * 256],
            ((1,), (1,)),
        )
    second[...] = raw_second[...]
    sums = (second[216:224, :], jnp.broadcast_to(jnp.sum(total, axis=1, keepdims=True), (8, LANE)))
    for i, value in enumerate(sums):
        high = value.astype(BF16).astype(F32)
        second[216 + 16 * i : 224 + 16 * i, :] = high
        second[224 + 16 * i : 232 + 16 * i, :] = value - high
    for i in range(NEAR):
        block = raw[64 * i : 64 * (i + 1), :].astype(BF16)
        message[i, 0:64, :] = block[:, :LANE]
        message[i, 64:128, :] = block[:, LANE:]
        message[i, 128:160, :] = second[32 * i : 32 * (i + 1), :].astype(BF16)


def lift_input_kernel(low, dhidden, high, weight, share, cols):
    own = dhidden[...].astype(F32)
    pick_columns(low[...].astype(F32), cols, 0)
    pick_columns(own[:, :PLANE], cols, LANE)
    pick_columns(own[:, PLANE:], cols, 2 * LANE)
    pick_columns(high[...].astype(F32), cols, 3 * LANE)
    share[...] = dot(weight[...], cols[...].astype(BF16)).astype(BF16)


def sum_kernel(parts, out):
    total = parts[0].astype(F32)
    for i in range(1, parts.shape[0]):
        total = total + parts[i].astype(F32)
    out[...] = total.astype(out.dtype)


def finish_kernel(scale, parts, first, second, bias, left, right, rest):
    for i in range(NEAR):
        left[64 * i : 64 * (i + 1), :] = parts[i, 0:64, :].astype(F32) * scale
        right[64 * i : 64 * (i + 1), :] = parts[i, 64:128, :].astype(F32) * scale
        rest[32 * i : 32 * (i + 1), :] = parts[i, 128:160, :].astype(F32) * scale
    for d in range(8):
        first[d, :, :LANE] = left[pl.ds(d, 64, stride=8), :]
        first[d, :, LANE:] = right[pl.ds(d, 64, stride=8), :]
    second[...] = rest[0:216, :]
    bias[0:8, :] = rest[216:224, :] + rest[224:232, :]
    bias[8:16, :] = rest[232:240, :] + rest[240:248, :]


def shifted(value, step):
    count = lax.axis_size("space")
    return lax.ppermute(value, "space", [(i, (i + step) % count) for i in range(count)])


def gathered(value):
    copies = jnp.broadcast_to(value[None], (lax.axis_size("filt"),) + value.shape)
    return lax.all_to_all(copies, "filt", 0, 0, tiled=True)


def near_exchange(value):
    count = lax.axis_size("space")
    groups = [[g + i for i in range(NEAR)] for g in range(0, count, NEAR)]
    return lax.all_to_all(value, "space", 0, 0, axis_index_groups=groups, tiled=True)


def per_device(volume, first_weight, first_bias, second_weight, second_bias, cotangent):
    struct = jax.ShapeDtypeStruct
    wide = lambda bias: jnp.broadcast_to(bias.astype(F32)[:, None], (8, LANE))
    first_rows = first_weight.transpose(1, 0, 2).reshape(512, 256)
    first_turned = first_weight.transpose(2, 1, 0).reshape(256, 512)
    second_rows = second_weight.transpose(1, 0, 2).reshape(216, LANE)
    second_rows = jnp.pad(second_rows, ((0, 8), (0, 0)))
    second_turned = jnp.pad(second_weight.transpose(2, 1, 0).reshape(LANE, 216), ((0, 0), (0, 40)))

    own = volume.reshape(16, 256)
    source = jnp.concatenate([shifted(own, 1), own, shifted(own, -1)], axis=1)
    source = gathered(source).reshape(256, 768)
    cot = vmem_call(
        split_kernel, struct((8, 2 * PLANE), F32), [pltpu.VMEM((64, 256), F32)]
    )(cotangent.reshape(64, 256))
    hidden = vmem_call(
        hidden_kernel, struct((8, 4 * PLANE), BF16), [pltpu.VMEM((512, 768), F32)]
    )(first_rows, source, wide(first_bias))
    hidden = gathered(hidden).reshape(LANE, 4 * PLANE)

    result, dpre = vmem_call(
        activate_kernel,
        (struct((64, 256), BF16), struct((8, 2 * PLANE), BF16)),
        [pltpu.VMEM((224, 4 * PLANE), F32), pltpu.VMEM((64, 256), F32)],
    )(hidden, second_rows, wide(second_bias), cot)

    low = shifted(dpre[:, PLANE:], 1)
    high = shifted(dpre[:, :PLANE], -1)
    share, raw_second = vmem_call(
        mix_back_kernel,
        (struct((LANE, 2 * PLANE), BF16), struct((256, LANE), F32)),
        [pltpu.VMEM((256, 2 * PLANE), F32), pltpu.VMEM((256, 2 * PLANE), BF16)],
    )(low, dpre, high, hidden[:, PLANE : 3 * PLANE], second_turned)
    parts = lax.all_to_all(share.reshape(16, 8, 2 * PLANE), "filt", 0, 0, tiled=True)

    dhidden, message = vmem_call(
        lift_back_kernel,
        (struct((8, 2 * PLANE), BF16), struct((NEAR, 160, LANE), BF16)),
        [pltpu.VMEM((256, 256), F32), pltpu.VMEM((512, 256), F32), pltpu.VMEM((256, LANE), F32)],
    )(parts, source, raw_second)

    low = shifted(dhidden[:, PLANE:], 1)
    high = shifted(dhidden[:, :PLANE], -1)
    message = near_exchange(message)
    mine = vmem_call(sum_kernel, struct((160, LANE), BF16))(message)
    far = [shifted(mine, NEAR * i) for i in (1, 2, 3)]
    share = vmem_call(
        lift_input_kernel, struct((256, 256), BF16), [pltpu.VMEM((512, 256), F32)]
    )(low, dhidden, high, first_turned)
    share = lax.all_to_all(share.reshape(16, 16, 256), "filt", 0, 0, tiled=True)
    mine = mine.astype(F32)
    for other in far:
        mine = mine + other.astype(F32)
    message = near_exchange(jnp.broadcast_to(mine.astype(BF16)[None], (NEAR, 160, LANE)))
    grad_volume = vmem_call(sum_kernel, struct((16, 256), BF16))(share)

    total_cells = volume.shape[0] * lax.axis_size("space") * 8 * volume.shape[2] * volume.shape[3]
    scale = 1.0 / math.sqrt(total_cells)
    first, second, bias = vmem_call(
        lambda *refs: finish_kernel(scale, *refs),
        (struct((8, 64, 256), F32), struct((216, LANE), F32), struct((16, LANE), F32)),
        [pltpu.VMEM((512, LANE), F32), pltpu.VMEM((512, LANE), F32), pltpu.VMEM((256, LANE), F32)],
    )(message)
    return (
        result.reshape(2, 8, 4, 256),
        grad_volume.reshape(1, 16, 2, 128),
        first,
        bias[8:16, 0],
        second.reshape(27, 8, LANE).transpose(1, 0, 2),
        bias[0:8, 0],
    )


def solution(mesh):
    placed = (
        P("space", "filt", None, None),
        P("filt", None, None),
        P("filt"),
        P("filt", None, None),
        P("filt"),
        P("space", "filt", None, None),
    )
    return jax.shard_map(
        per_device,
        mesh=mesh,
        in_specs=placed,
        out_specs=(
            P("space", "filt", None, None),
            P("space", "filt", None, None),
            P("filt", None, None),
            P("filt"),
            P("filt", None, None),
            P("filt"),
        ),
        check_vma=False,
    )
```

time: 558 us -> 161 us (0.29)
  waiting for transfers between devices: 306 us -> 45.2 us
  blocking collectives: 156 us -> 33.6 us
  starting transfers between devices: 32.1 us -> 66.7 us
  local copies, waits for them, and re-layouts: 25.1 us -> 7.28 us
  between operations: 16.1 us -> 0.89 us
  other arithmetic: 14.7 us -> 0.03 us
  matrix products: 6.88 us -> 0 us
    psum x1 -> x0, waiting for transfers between devices: 192 us -> none  [per_device(): lax.psum((raw_first, raw_first_bias, raw_second, raw_second_bias), 'space')]
    all_gather x2 -> x0, waiting for transfers between devices: 103 us -> none  [widen(): return lax.all_gather(rimmed, 'filt', axis=1, tiled=True)]
    unnamed x1 -> x0, blocking collectives: 67.3 us -> none
    psum x1 -> x0, blocking collectives: 65.4 us -> none  [per_device(): lax.psum((raw_first, raw_first_bias, raw_second, raw_second_bias), 'space')]
    all_to_all x1 -> x4, waiting for transfers between devices: 2.19 us -> 35.8 us  [the longest x2 21.9 us: gathered(): return lax.all_to_all(copies, 'filt', 0, 0, tiled=True)]
    all_to_all x0 -> x2, blocking collectives: none -> 33.6 us  [the longest x1 18 us: near_exchange(): lax.all_to_all(value, 'space', 0, 0, axis_index_groups=groups, tiled=True)]
    all_gather x1 -> x0, blocking collectives: 23.1 us -> none  [widen(): return lax.all_gather(rimmed, 'filt', axis=1, tiled=True)]
    all_to_all x1 -> x4, starting transfers between devices: 6.84 us -> 24.7 us  [the longest x2 14 us: gathered(): return lax.all_to_all(copies, 'filt', 0, 0, tiled=True)]
  transfers between devices with their start and end apart: 12 -> 13, of which waited for: 8 -> 7; matrix products, arithmetic and copies ran while one was open for 3% -> 1% of each run, Pallas kernels for 0% -> 1%
where the time goes in v1:
time: 161 us; the launch traced here: 158 us
  starting transfers between devices  66.7 us (41%)
  waiting for transfers between devices  45.2 us (28%)
  blocking collectives  33.6 us (21%)
  local copies, waits for them, and re-layouts  7.28 us (5%)
  Pallas kernels  4.5 us (3%)
    ppermute x9, starting transfers between devices, shifted(): lax.ppermute(value, 'space', [(i, (i + step) % count) for i in range(coun...  41.9 us
    all_to_all x2, waiting for transfers between devices, gathered(): return lax.all_to_all(copies, 'filt', 0, 0, tiled=True)  21.9 us
    all_to_all x1, blocking collectives, near_exchange(): lax.all_to_all(value, 'space', 0, 0, axis_index_groups=groups, tiled=True)  18 us
    all_to_all x1, blocking collectives, per_device(): lax.all_to_all(share.reshape(16, 8, 2 * PLANE), 'filt', 0, 0, tiled=True)  15.6 us
    all_to_all x2, starting transfers between devices, gathered(): return lax.all_to_all(copies, 'filt', 0, 0, tiled=True)  14 us
    ppermute x9, waiting for transfers between devices, shifted(): lax.ppermute(value, 'space', [(i, (i + step) % count) for i in range(coun...  9.4 us
    all_to_all x1, waiting for transfers between devices, near_exchange(): lax.all_to_all(value, 'space', 0, 0, axis_index_groups=groups, tiled=True)  8.79 us
    all_to_all x1, starting transfers between devices, per_device(): share = lax.all_to_all(share.reshape(16, 16, 256), 'filt', 0, 0, tiled=True)  5.76 us
  transfers between devices with their start and end apart: 13, of which 7 were waited for; matrix products, arithmetic and copies ran while one was open for 1% of the time, Pallas kernels for 1%

profile of v1, /device:TPU:24, one launch (start us, length us, event | category | flops | bytes accessed | tf_op | source)
XLA Modules:
  0.0 158.2 jit_solution(15600808294343271276)
XLA Ops:
  0.6 0.7 copy.25
  1.3 4.0 %collective-permute-start = (bf16[16,256]{1,0:T(8,128)(2,1)S(1)}, bf16[16,256]{1,0:T(8,128)(2,1)S(1)}, u32[]{:S(2)}, u32[]{:S(2)}) collective-permute-start(bf16[16,256]{1,0:T(8,128)(2,1)S(1)} %bitcast.37), channel_id=1, source_target_pairs={{0,16},{16,32},{32,48},{48,64},{64,80},{80,96},{96,112},{112,128},... | collective-permute-start | bytes 24584 | tf_op jit(solution)/shard_map/ppermute | solution.py:222
  5.3 1.9 %collective-permute-start.1 = (bf16[16,256]{1,0:T(8,128)(2,1)S(1)}, bf16[16,256]{1,0:T(8,128)(2,1)S(1)}, u32[]{:S(2)}, u32[]{:S(2)}) collective-permute-start(bf16[16,256]{1,0:T(8,128)(2,1)S(1)} %bitcast.38), channel_id=1, source_target_pairs={{0,496},{16,0},{32,16},{48,32},{64,48},{80,64},{96,80},{112,96},{1... | collective-permute-start | bytes 24584 | tf_op jit(solution)/shard_map/ppermute | solution.py:222
  7.3 0.0 collective-permute-done
  7.3 4.5 %collective-permute-done.1 = bf16[16,256]{1,0:T(8,128)(2,1)S(1)} collective-permute-done((bf16[16,256]{1,0:T(8,128)(2,1)S(1)}, bf16[16,256]{1,0:T(8,128)(2,1)S(1)}, u32[]{:S(2)}, u32[]{:S(2)}) %collective-permute-start.1) | collective-permute-done | bytes 8224 | tf_op jit(solution)/shard_map/ppermute | solution.py:222
  11.8 0.8 broadcast_in_dim.10
  12.6 0.0 copy-start
  12.6 7.4 %all-to-all-start = ((bf16[16,16,768]{2,1,0:T(8,128)(2,1)}), bf16[16,16,768]{2,1,0:T(8,128)(2,1)S(1)}, u32[]{:S(2)}, u32[]{:S(2)}) async-start(bf16[16,16,768]{2,1,0:T(8,128)(2,1)} %broadcast_in_dim.10), calls=%async_computation | async-start | bytes 786432 | tf_op jit(solution)/shard_map/all_to_all | solution.py:227
  20.0 0.0 copy-done
  20.0 0.2 copy.24
  20.1 7.7 %all-to-all-done = bf16[16,16,768]{2,1,0:T(8,128)(2,1)S(1)} async-done(((bf16[16,16,768]{2,1,0:T(8,128)(2,1)}), bf16[16,16,768]{2,1,0:T(8,128)(2,1)S(1)}, u32[]{:S(2)}, u32[]{:S(2)}) %all-to-all-start) | async-done | bytes 393248 | tf_op jit(solution)/shard_map/all_to_all | solution.py:227
  27.8 0.0 copy-start.3
  27.8 0.7 copy-done.3
  28.5 0.1 broadcast_in_dim.11.bias
  28.5 0.4 shard_map.109
  29.0 1.1 broadcast_in_dim.12
  30.1 0.0 copy-start.2
  30.1 6.6 %all-to-all-start.1 = ((bf16[16,8,4096]{2,1,0:T(8,128)(2,1)}), bf16[16,8,4096]{2,1,0:T(8,128)(2,1)S(1)}, u32[]{:S(2)}, u32[]{:S(2)}) async-start(bf16[16,8,4096]{2,1,0:T(8,128)(2,1)} %broadcast_in_dim.12), calls=%async_computation.1 | async-start | bytes 2097152 | tf_op jit(solution)/shard_map/all_to_all | solution.py:227
  36.7 0.0 copy-done.2
  36.7 0.0 copy-start.1
  36.7 0.2 shard_map.110.cot
  36.9 0.6 copy-done.1
  37.5 0.0 copy-start.4
  37.5 14.2 %all-to-all-done.1 = bf16[16,8,4096]{2,1,0:T(8,128)(2,1)S(1)} async-done(((bf16[16,8,4096]{2,1,0:T(8,128)(2,1)}), bf16[16,8,4096]{2,1,0:T(8,128)(2,1)S(1)}, u32[]{:S(2)}, u32[]{:S(2)}) %all-to-all-start.1) | async-done | bytes 1048608 | tf_op jit(solution)/shard_map/all_to_all | solution.py:227
  51.8 0.0 copy-done.4
  51.8 0.1 broadcast_in_dim.13.bias
  51.8 0.9 shard_map.111
  52.8 2.4 %collective-permute-start.2 = (bf16[8,1024]{1,0:T(8,128)(2,1)S(1)}, bf16[8,1024]{1,0:T(8,128)(2,1)S(1)}, u32[]{:S(2)}, u32[]{:S(2)}) collective-permute-start(bf16[8,1024]{1,0:T(8,128)(2,1)S(1)} %get-tuple-element.29), channel_id=1, source_target_pairs={{0,16},{16,32},{32,48},{48,64},{64,80},{80,96},{96,112},{112,128},... | collective-permute-start | bytes 49160 | tf_op jit(solution)/shard_map/ppermute | solution.py:222
  55.2 7.1 %collective-permute-start.3 = (bf16[8,1024]{1,0:T(8,128)(2,1)S(1)}, bf16[8,1024]{1,0:T(8,128)(2,1)S(1)}, u32[]{:S(2)}, u32[]{:S(2)}) collective-permute-start(bf16[8,1024]{1,0:T(8,128)(2,1)S(1)} %get-tuple-element.28), channel_id=1, source_target_pairs={{0,496},{16,0},{32,16},{48,32},{64,48},{80,64},{96,80},{112,96},{1... | collective-permute-start | bytes 49160 | tf_op jit(solution)/shard_map/ppermute | solution.py:222
  62.3 0.1 copy.16
  62.5 0.0 collective-permute-done.2.low
  62.5 1.2 collective-permute-done.3.high
  63.7 0.7 shard_map.112
  64.4 15.6 %all_to_all.30.parts = bf16[16,8,2048]{2,1,0:T(8,128)(2,1)S(1)} all-to-all(bf16[16,8,2048]{2,1,0:T(8,128)(2,1)S(1)} %bitcast.32), channel_id=1, replica_groups=mesh['space'=32,'filt'=16] {'filt'}, dimensions={0} | all-to-all | bytes 1048576 | tf_op jit(solution)/shard_map/all_to_all | solution.py:269
  80.0 0.3 shard_map.113
  80.3 18.0 %all_to_all.31.parts = bf16[8,160,128]{2,1,0:T(8,128)(2,1)S(1)} all-to-all(bf16[8,160,128]{2,1,0:T(8,128)(2,1)S(1)} %get-tuple-element.20), channel_id=1, replica_groups={{0,16,32,48,64,80,96,112},{128,144,160,176,192,208,224,240},{256,272,28..., dimensions={0} | all-to-all | bytes 655360 | tf_op jit(solution)/shard_map/all_to_all | solution.py:233
  98.4 9.1 %collective-permute-start.6 = (bf16[160,128]{1,0:T(8,128)(2,1)S(1)}, bf16[160,128]{1,0:T(8,128)(2,1)S(1)}, u32[]{:S(2)}, u32[]{:S(2)}) collective-permute-start(bf16[160,128]{1,0:T(8,128)(2,1)S(1)} %shard_map.116), channel_id=1, source_target_pairs={{0,128},{16,144},{32,160},{48,176},{64,192},{80,208},{96,224},{112... | collective-permute-start | bytes 122888 | tf_op jit(solution)/shard_map/ppermute | solution.py:222
  107.5 4.9 %collective-permute-start.7 = (bf16[160,128]{1,0:T(8,128)(2,1)S(1)}, bf16[160,128]{1,0:T(8,128)(2,1)S(1)}, u32[]{:S(2)}, u32[]{:S(2)}) collective-permute-start(bf16[160,128]{1,0:T(8,128)(2,1)S(1)} %shard_map.116), channel_id=1, source_target_pairs={{0,256},{16,272},{32,288},{48,304},{64,320},{80,336},{96,352},{112... | collective-permute-start | bytes 122888 | tf_op jit(solution)/shard_map/ppermute | solution.py:222
  112.4 6.6 %collective-permute-start.8 = (bf16[160,128]{1,0:T(8,128)(2,1)S(1)}, bf16[160,128]{1,0:T(8,128)(2,1)S(1)}, u32[]{:S(2)}, u32[]{:S(2)}) collective-permute-start(bf16[160,128]{1,0:T(8,128)(2,1)S(1)} %shard_map.116), channel_id=1, source_target_pairs={{0,384},{16,400},{32,416},{48,432},{64,448},{80,464},{96,480},{112... | collective-permute-start | bytes 122888 | tf_op jit(solution)/shard_map/ppermute | solution.py:222
  119.1 3.3 %collective-permute-start.4 = (bf16[8,1024]{1,0:T(8,128)(2,1)S(1)}, bf16[8,1024]{1,0:T(8,128)(2,1)S(1)}, u32[]{:S(2)}, u32[]{:S(2)}) collective-permute-start(bf16[8,1024]{1,0:T(8,128)(2,1)S(1)} %get-tuple-element.27), channel_id=1, source_target_pairs={{0,16},{16,32},{32,48},{48,64},{64,80},{80,96},{96,112},{112,128},... | collective-permute-start | bytes 49160 | tf_op jit(solution)/shard_map/ppermute | solution.py:222
  122.4 2.6 %collective-permute-start.5 = (bf16[8,1024]{1,0:T(8,128)(2,1)S(1)}, bf16[8,1024]{1,0:T(8,128)(2,1)S(1)}, u32[]{:S(2)}, u32[]{:S(2)}) collective-permute-start(bf16[8,1024]{1,0:T(8,128)(2,1)S(1)} %get-tuple-element.26), channel_id=1, source_target_pairs={{0,496},{16,0},{32,16},{48,32},{64,48},{80,64},{96,80},{112,96},{1... | collective-permute-start | bytes 49160 | tf_op jit(solution)/shard_map/ppermute | solution.py:222
  124.9 0.2 copy.23
  125.1 0.1 copy.18.weight
  125.2 0.0 collective-permute-done.4.low
  125.2 3.6 %collective-permute-done.5.high = bf16[8,1024]{1,0:T(8,128)(2,1)S(1)} collective-permute-done((bf16[8,1024]{1,0:T(8,128)(2,1)S(1)}, bf16[8,1024]{1,0:T(8,128)(2,1)S(1)}, u32[]{:S(2)}, u32[]{:S(2)}) %collective-permute-start.5) | collective-permute-done | bytes 16416 | tf_op jit(solution)/shard_map/ppermute | solution.py:222
  128.9 1.0 shard_map.114
  129.8 5.8 %all-to-all-start.3 = ((bf16[16,16,256]{2,1,0:T(8,128)(2,1)}), bf16[16,16,256]{2,1,0:T(8,128)(2,1)S(1)}, u32[]{:S(2)}, u32[]{:S(2)}) async-start(bf16[16,16,256]{2,1,0:T(8,128)(2,1)} %bitcast.11), calls=%async_computation.3 | async-start | bytes 262144 | tf_op jit(solution)/shard_map/all_to_all | solution.py:285
  135.6 0.0 collective-permute-done.6
  135.6 0.0 collective-permute-done.7
  135.6 0.0 collective-permute-done.8
  135.7 5.1 %all-to-all-done.3.parts = bf16[16,16,256]{2,1,0:T(8,128)(2,1)S(1)} async-done(((bf16[16,16,256]{2,1,0:T(8,128)(2,1)}), bf16[16,16,256]{2,1,0:T(8,128)(2,1)S(1)}, u32[]{:S(2)}, u32[]{:S(2)}) %all-to-all-start.3) | async-done | bytes 131104 | tf_op jit(solution)/shard_map/all_to_all | solution.py:285
  140.8 0.8 broadcast_in_dim.14
  141.5 5.0 %all-to-all-start.5 = ((bf16[8,160,128]{2,1,0:T(8,128)(2,1)}), bf16[8,160,128]{2,1,0:T(8,128)(2,1)S(1)}, u32[]{:S(2)}, u32[]{:S(2)}) async-start(bf16[8,160,128]{2,1,0:T(8,128)(2,1)} %broadcast_in_dim.14), calls=%async_computation.5 | async-start | bytes 655360 | tf_op jit(solution)/shard_map/all_to_all | solution.py:233
  146.5 0.6 reshape.62
  147.2 0.6 reshape.67
  147.8 8.8 %all-to-all-done.5.refs_0_ = bf16[8,160,128]{2,1,0:T(8,128)(2,1)S(1)} async-done(((bf16[8,160,128]{2,1,0:T(8,128)(2,1)}), bf16[8,160,128]{2,1,0:T(8,128)(2,1)S(1)}, u32[]{:S(2)}, u32[]{:S(2)}) %all-to-all-start.5) | async-done | bytes 327712 | tf_op jit(solution)/shard_map/all_to_all | solution.py:233
  156.6 0.9 shard_map.117
  157.5 0.7 slice_reduce_fusion
  (10 shorter events, 0.2 us)
Async XLA Ops:
  1.3 5.9 %collective-permute-start = (bf16[16,256]{1,0:T(8,128)(2,1)S(1)}, bf16[16,256]{1,0:T(8,128)(2,1)S(1)}, u32[]{:S(2)}, u32[]{:S(2)}) collective-permute-start(bf16[16,256]{1,0:T(8,128)(2,1)S(1)} %bitcast.37), channel_id=1, source_target_pairs={{0,16},{16,32},{32,48},{48,64},{64,80},{80,96},{96,112},{112,128},... | collective-permute-start | bytes 24584 | tf_op jit(solution)/shard_map/ppermute | solution.py:222
  5.3 6.4 %collective-permute-start.1 = (bf16[16,256]{1,0:T(8,128)(2,1)S(1)}, bf16[16,256]{1,0:T(8,128)(2,1)S(1)}, u32[]{:S(2)}, u32[]{:S(2)}) collective-permute-start(bf16[16,256]{1,0:T(8,128)(2,1)S(1)} %bitcast.38), channel_id=1, source_target_pairs={{0,496},{16,0},{32,16},{48,32},{64,48},{80,64},{96,80},{112,96},{1... | collective-permute-start | bytes 24584 | tf_op jit(solution)/shard_map/ppermute | solution.py:222
  12.6 7.4 %copy-start = (bf16[8,64,256]{2,1,0:T(8,128)(2,1)S(1)}, bf16[8,64,256]{2,1,0:T(8,128)(2,1)}, u32[]{:S(2)}) copy-start(bf16[8,64,256]{2,1,0:T(8,128)(2,1)} %param.7) | copy-start | bytes 786436
  12.6 15.3 %all-to-all-start = ((bf16[16,16,768]{2,1,0:T(8,128)(2,1)}), bf16[16,16,768]{2,1,0:T(8,128)(2,1)S(1)}, u32[]{:S(2)}, u32[]{:S(2)}) async-start(bf16[16,16,768]{2,1,0:T(8,128)(2,1)} %broadcast_in_dim.10), calls=%async_computation | async-start | bytes 786432 | tf_op jit(solution)/shard_map/all_to_all | solution.py:227
  27.8 0.7 copy-start.3
  30.1 6.6 %copy-start.2 = (bf16[2,8,4,256]{3,2,1,0:T(4,128)(2,1)S(1)}, bf16[2,8,4,256]{3,2,1,0:T(4,128)(2,1)}, u32[]{:S(2)}) copy-start(bf16[2,8,4,256]{3,2,1,0:T(4,128)(2,1)} %param.11) | copy-start | bytes 98308
  30.1 21.7 %all-to-all-start.1 = ((bf16[16,8,4096]{2,1,0:T(8,128)(2,1)}), bf16[16,8,4096]{2,1,0:T(8,128)(2,1)S(1)}, u32[]{:S(2)}, u32[]{:S(2)}) async-start(bf16[16,8,4096]{2,1,0:T(8,128)(2,1)} %broadcast_in_dim.12), calls=%async_computation.1 | async-start | bytes 2097152 | tf_op jit(solution)/shard_map/all_to_all | solution.py:227
  36.7 0.8 copy-start.1
  37.5 14.2 %copy-start.4 = (bf16[8]{0:T(256)(128)(2,1)S(1)}, bf16[8]{0:T(256)(128)(2,1)}, u32[]{:S(2)}) copy-start(bf16[8]{0:T(256)(128)(2,1)} %param.10) | copy-start | bytes 52
  52.8 9.7 %collective-permute-start.2 = (bf16[8,1024]{1,0:T(8,128)(2,1)S(1)}, bf16[8,1024]{1,0:T(8,128)(2,1)S(1)}, u32[]{:S(2)}, u32[]{:S(2)}) collective-permute-start(bf16[8,1024]{1,0:T(8,128)(2,1)S(1)} %get-tuple-element.29), channel_id=1, source_target_pairs={{0,16},{16,32},{32,48},{48,64},{64,80},{80,96},{96,112},{112,128},... | collective-permute-start | bytes 49160 | tf_op jit(solution)/shard_map/ppermute | solution.py:222
  55.2 8.6 %collective-permute-start.3 = (bf16[8,1024]{1,0:T(8,128)(2,1)S(1)}, bf16[8,1024]{1,0:T(8,128)(2,1)S(1)}, u32[]{:S(2)}, u32[]{:S(2)}) collective-permute-start(bf16[8,1024]{1,0:T(8,128)(2,1)S(1)} %get-tuple-element.28), channel_id=1, source_target_pairs={{0,496},{16,0},{32,16},{48,32},{64,48},{80,64},{96,80},{112,96},{1... | collective-permute-start | bytes 49160 | tf_op jit(solution)/shard_map/ppermute | solution.py:222
  98.4 37.2 %collective-permute-start.6 = (bf16[160,128]{1,0:T(8,128)(2,1)S(1)}, bf16[160,128]{1,0:T(8,128)(2,1)S(1)}, u32[]{:S(2)}, u32[]{:S(2)}) collective-permute-start(bf16[160,128]{1,0:T(8,128)(2,1)S(1)} %shard_map.116), channel_id=1, source_target_pairs={{0,128},{16,144},{32,160},{48,176},{64,192},{80,208},{96,224},{112... | collective-permute-start | bytes 122888 | tf_op jit(solution)/shard_map/ppermute | solution.py:222
  107.5 28.1 %collective-permute-start.7 = (bf16[160,128]{1,0:T(8,128)(2,1)S(1)}, bf16[160,128]{1,0:T(8,128)(2,1)S(1)}, u32[]{:S(2)}, u32[]{:S(2)}) collective-permute-start(bf16[160,128]{1,0:T(8,128)(2,1)S(1)} %shard_map.116), channel_id=1, source_target_pairs={{0,256},{16,272},{32,288},{48,304},{64,320},{80,336},{96,352},{112... | collective-permute-start | bytes 122888 | tf_op jit(solution)/shard_map/ppermute | solution.py:222
  112.4 23.2 %collective-permute-start.8 = (bf16[160,128]{1,0:T(8,128)(2,1)S(1)}, bf16[160,128]{1,0:T(8,128)(2,1)S(1)}, u32[]{:S(2)}, u32[]{:S(2)}) collective-permute-start(bf16[160,128]{1,0:T(8,128)(2,1)S(1)} %shard_map.116), channel_id=1, source_target_pairs={{0,384},{16,400},{32,416},{48,432},{64,448},{80,464},{96,480},{112... | collective-permute-start | bytes 122888 | tf_op jit(solution)/shard_map/ppermute | solution.py:222
  119.1 6.2 %collective-permute-start.4 = (bf16[8,1024]{1,0:T(8,128)(2,1)S(1)}, bf16[8,1024]{1,0:T(8,128)(2,1)S(1)}, u32[]{:S(2)}, u32[]{:S(2)}) collective-permute-start(bf16[8,1024]{1,0:T(8,128)(2,1)S(1)} %get-tuple-element.27), channel_id=1, source_target_pairs={{0,16},{16,32},{32,48},{48,64},{64,80},{80,96},{96,112},{112,128},... | collective-permute-start | bytes 49160 | tf_op jit(solution)/shard_map/ppermute | solution.py:222
  122.4 6.5 %collective-permute-start.5 = (bf16[8,1024]{1,0:T(8,128)(2,1)S(1)}, bf16[8,1024]{1,0:T(8,128)(2,1)S(1)}, u32[]{:S(2)}, u32[]{:S(2)}) collective-permute-start(bf16[8,1024]{1,0:T(8,128)(2,1)S(1)} %get-tuple-element.26), channel_id=1, source_target_pairs={{0,496},{16,0},{32,16},{48,32},{64,48},{80,64},{96,80},{112,96},{1... | collective-permute-start | bytes 49160 | tf_op jit(solution)/shard_map/ppermute | solution.py:222
  129.8 10.9 %all-to-all-start.3 = ((bf16[16,16,256]{2,1,0:T(8,128)(2,1)}), bf16[16,16,256]{2,1,0:T(8,128)(2,1)S(1)}, u32[]{:S(2)}, u32[]{:S(2)}) async-start(bf16[16,16,256]{2,1,0:T(8,128)(2,1)} %bitcast.11), calls=%async_computation.3 | async-start | bytes 262144 | tf_op jit(solution)/shard_map/all_to_all | solution.py:285
  141.5 15.0 %all-to-all-start.5 = ((bf16[8,160,128]{2,1,0:T(8,128)(2,1)}), bf16[8,160,128]{2,1,0:T(8,128)(2,1)S(1)}, u32[]{:S(2)}, u32[]{:S(2)}) async-start(bf16[8,160,128]{2,1,0:T(8,128)(2,1)} %broadcast_in_dim.14), calls=%async_computation.5 | async-start | bytes 655360 | tf_op jit(solution)/shard_map/all_to_all | solution.py:233

commit v2 on v1

--- a/solution.py
+++ b/solution.py
@@ -61,7 +61,9 @@
                             part = term if part is None else part + term
                     total = total + ahead(part, off)
                 col = plane * PLANE + x * 256 + parity_y * LANE
-                out[:, col : col + LANE] = total.astype(BF16)
+                value = total.astype(BF16)
+                for copy in range(out.shape[0]):
+                    out[copy, :, col : col + LANE] = value
 
 
 def spread_rows(rows, cols):
@@ -204,7 +206,18 @@
     out[...] = total.astype(out.dtype)
 
 
-def finish_kernel(scale, parts, first, second, bias, left, right, rest):
+def pair_kernel(one, other, out):
+    total = (one[...].astype(F32) + other[...].astype(F32)).astype(BF16)
+    out[...] = jnp.broadcast_to(total, out.shape)
+
+
+def as_row(column):
+    here = lax.broadcasted_iota(jnp.int32, (8, LANE), 0)
+    lane = lax.broadcasted_iota(jnp.int32, (8, LANE), 1)
+    return jnp.sum(jnp.where(here == lane, column, 0.0), axis=0, keepdims=True)[:, :8]
+
+
+def finish_kernel(scale, parts, first, second, first_bias, second_bias, left, right, rest):
     for i in range(NEAR):
         left[64 * i : 64 * (i + 1), :] = parts[i, 0:64, :].astype(F32) * scale
         right[64 * i : 64 * (i + 1), :] = parts[i, 64:128, :].astype(F32) * scale
@@ -213,8 +226,8 @@
         first[d, :, :LANE] = left[pl.ds(d, 64, stride=8), :]
         first[d, :, LANE:] = right[pl.ds(d, 64, stride=8), :]
     second[...] = rest[0:216, :]
-    bias[0:8, :] = rest[216:224, :] + rest[224:232, :]
-    bias[8:16, :] = rest[232:240, :] + rest[240:248, :]
+    second_bias[...] = as_row(rest[216:224, :] + rest[224:232, :])
+    first_bias[...] = as_row(rest[232:240, :] + rest[240:248, :])
 
 
 def shifted(value, step):
@@ -225,6 +238,17 @@
 def gathered(value):
     copies = jnp.broadcast_to(value[None], (lax.axis_size("filt"),) + value.shape)
     return lax.all_to_all(copies, "filt", 0, 0, tiled=True)
+
+
+def partner(value, ends):
+    count = lax.axis_size("space")
+    groups = count // NEAR
+    pairs = []
+    for i in range(count):
+        group = i // NEAR
+        other = ((group + ends) ^ 1) - ends
+        pairs.append((i, other % groups * NEAR + i % NEAR))
+    return lax.ppermute(value, "space", pairs)
 
 
 def near_exchange(value):
@@ -235,6 +259,7 @@
 
 def per_device(volume, first_weight, first_bias, second_weight, second_bias, cotangent):
     struct = jax.ShapeDtypeStruct
+    count = lax.axis_size("filt")
     wide = lambda bias: jnp.broadcast_to(bias.astype(F32)[:, None], (8, LANE))
     first_rows = first_weight.transpose(1, 0, 2).reshape(512, 256)
     first_turned = first_weight.transpose(2, 1, 0).reshape(256, 512)
@@ -249,9 +274,9 @@
         split_kernel, struct((8, 2 * PLANE), F32), [pltpu.VMEM((64, 256), F32)]
     )(cotangent.reshape(64, 256))
     hidden = vmem_call(
-        hidden_kernel, struct((8, 4 * PLANE), BF16), [pltpu.VMEM((512, 768), F32)]
+        hidden_kernel, struct((count, 8, 4 * PLANE), BF16), [pltpu.VMEM((512, 768), F32)]
     )(first_rows, source, wide(first_bias))
-    hidden = gathered(hidden).reshape(LANE, 4 * PLANE)
+    hidden = lax.all_to_all(hidden, "filt", 0, 0, tiled=True).reshape(LANE, 4 * PLANE)
 
     result, dpre = vmem_call(
         activate_kernel,
@@ -277,32 +302,40 @@
     low = shifted(dhidden[:, PLANE:], 1)
     high = shifted(dhidden[:, :PLANE], -1)
     message = near_exchange(message)
+    message, low, high = lax.optimization_barrier((message, low, high))
     mine = vmem_call(sum_kernel, struct((160, LANE), BF16))(message)
-    far = [shifted(mine, NEAR * i) for i in (1, 2, 3)]
+    other = partner(mine, 0)
     share = vmem_call(
         lift_input_kernel, struct((256, 256), BF16), [pltpu.VMEM((512, 256), F32)]
     )(low, dhidden, high, first_turned)
+    mine = vmem_call(pair_kernel, struct((160, LANE), BF16))(mine, other)
+    mine, share = lax.optimization_barrier((mine, share))
+    other = partner(mine, 1)
     share = lax.all_to_all(share.reshape(16, 16, 256), "filt", 0, 0, tiled=True)
-    mine = mine.astype(F32)
-    for other in far:
-        mine = mine + other.astype(F32)
-    message = near_exchange(jnp.broadcast_to(mine.astype(BF16)[None], (NEAR, 160, LANE)))
+    other, share = lax.optimization_barrier((other, share))
+    message = vmem_call(pair_kernel, struct((NEAR, 160, LANE), BF16))(mine, other)
+    message = near_exchange(message)
     grad_volume = vmem_call(sum_kernel, struct((16, 256), BF16))(share)
 
     total_cells = volume.shape[0] * lax.axis_size("space") * 8 * volume.shape[2] * volume.shape[3]
     scale = 1.0 / math.sqrt(total_cells)
-    first, second, bias = vmem_call(
+    first, second, sum_first, sum_second = vmem_call(
         lambda *refs: finish_kernel(scale, *refs),
-        (struct((8, 64, 256), F32), struct((216, LANE), F32), struct((16, LANE), F32)),
+        (
+            struct((8, 64, 256), F32),
+            struct((216, LANE), F32),
+            struct((1, 8), F32),
+            struct((1, 8), F32),
+        ),
         [pltpu.VMEM((512, LANE), F32), pltpu.VMEM((512, LANE), F32), pltpu.VMEM((256, LANE), F32)],
     )(message)
     return (
         result.reshape(2, 8, 4, 256),
         grad_volume.reshape(1, 16, 2, 128),
         first,
-        bias[8:16, 0],
+        sum_first.reshape(8),
         second.reshape(27, 8, LANE).transpose(1, 0, 2),
-        bias[0:8, 0],
+        sum_second.reshape(8),
     )
 
 

time: 161 us -> 147 us (0.913)
  blocking collectives: 33.6 us -> 15.6 us
  starting transfers between devices: 66.7 us -> 72.5 us
  Pallas kernels: 4.5 us -> 7.1 us
  local copies, waits for them, and re-layouts: 7.28 us -> 4.75 us
    ppermute x9 -> x6, starting transfers between devices: 41.9 us -> 21.3 us  [shifted(): lax.ppermute(value, 'space', [(i, (i + step) % count) for i in range(coun...]
    all_to_all x1 -> x0, blocking collectives: 18 us -> none  [near_exchange(): lax.all_to_all(value, 'space', 0, 0, axis_index_groups=groups, tiled=True)]
    ppermute x0 -> x2, starting transfers between devices: none -> 14.7 us  [partner(): return lax.ppermute(value, 'space', pairs)]
    all_to_all x2 -> x1, waiting for transfers between devices: 21.9 us -> 7.68 us  [gathered(): return lax.all_to_all(copies, 'filt', 0, 0, tiled=True)]
    all_to_all x0 -> x1, waiting for transfers between devices: none -> 14.2 us  [per_device(): lax.all_to_all(hidden, 'filt', 0, 0, tiled=True).reshape(LANE, 4 * PLANE)]
    all_to_all x1 -> x2, starting transfers between devices: 4.98 us -> 16.6 us  [near_exchange(): lax.all_to_all(value, 'space', 0, 0, axis_index_groups=groups, tiled=True)]
    all_to_all x0 -> x1, starting transfers between devices: none -> 6.59 us  [per_device(): lax.all_to_all(hidden, 'filt', 0, 0, tiled=True).reshape(LANE, 4 * PLANE)]
    all_to_all x2 -> x1, starting transfers between devices: 14 us -> 7.41 us  [gathered(): return lax.all_to_all(copies, 'filt', 0, 0, tiled=True)]
  transfers between devices with their start and end apart: 13 -> 13, of which waited for: 7 -> 8; matrix products, arithmetic and copies ran while one was open for 1% -> 1% of each run, Pallas kernels for 1% -> 1%
where the time goes in v2:
time: 147 us; the launch traced here: 146 us
  starting transfers between devices  72.5 us (49%)
  waiting for transfers between devices  44.9 us (31%)
  blocking collectives  15.6 us (11%)
  Pallas kernels  7.1 us (5%)
  local copies, waits for them, and re-layouts  4.75 us (3%)
    ppermute x6, starting transfers between devices, shifted(): lax.ppermute(value, 'space', [(i, (i + step) % count) for i in range(coun...  21.3 us
    all_to_all x2, starting transfers between devices, near_exchange(): lax.all_to_all(value, 'space', 0, 0, axis_index_groups=groups, tiled=True)  16.6 us
    all_to_all x1, blocking collectives, per_device(): lax.all_to_all(share.reshape(16, 8, 2 * PLANE), 'filt', 0, 0, tiled=True)  15.6 us
    ppermute x2, starting transfers between devices, partner(): return lax.ppermute(value, 'space', pairs)  14.7 us
    all_to_all x1, waiting for transfers between devices, per_device(): lax.all_to_all(hidden, 'filt', 0, 0, tiled=True).reshape(LANE, 4 * PLANE)  14.2 us
    ppermute x6, waiting for transfers between devices, shifted(): lax.ppermute(value, 'space', [(i, (i + step) % count) for i in range(coun...  10.2 us
    all_to_all x2, waiting for transfers between devices, near_exchange(): lax.all_to_all(value, 'space', 0, 0, axis_index_groups=groups, tiled=True)  7.87 us
    all_to_all x1, waiting for transfers between devices, gathered(): return lax.all_to_all(copies, 'filt', 0, 0, tiled=True)  7.68 us
  transfers between devices with their start and end apart: 13, of which 8 were waited for; matrix products, arithmetic and copies ran while one was open for 1% of the time, Pallas kernels for 1%

profile of v2, /device:TPU:24, one launch (start us, length us, event | category | flops | bytes accessed | tf_op | source)
XLA Modules:
  0.0 145.7 jit_solution(17485478789964109114)
XLA Ops:
  0.6 0.7 copy.25
  1.3 4.0 %collective-permute-start = (bf16[16,256]{1,0:T(8,128)(2,1)S(1)}, bf16[16,256]{1,0:T(8,128)(2,1)S(1)}, u32[]{:S(2)}, u32[]{:S(2)}) collective-permute-start(bf16[16,256]{1,0:T(8,128)(2,1)S(1)} %bitcast.39), channel_id=1, source_target_pairs={{0,16},{16,32},{32,48},{48,64},{64,80},{80,96},{96,112},{112,128},... | collective-permute-start | bytes 24584 | tf_op jit(solution)/shard_map/ppermute | solution.py:235
  5.3 1.9 %collective-permute-start.1 = (bf16[16,256]{1,0:T(8,128)(2,1)S(1)}, bf16[16,256]{1,0:T(8,128)(2,1)S(1)}, u32[]{:S(2)}, u32[]{:S(2)}) collective-permute-start(bf16[16,256]{1,0:T(8,128)(2,1)S(1)} %bitcast.40), channel_id=1, source_target_pairs={{0,496},{16,0},{32,16},{48,32},{64,48},{80,64},{96,80},{112,96},{1... | collective-permute-start | bytes 24584 | tf_op jit(solution)/shard_map/ppermute | solution.py:235
  7.3 0.0 collective-permute-done
  7.3 4.5 %collective-permute-done.1 = bf16[16,256]{1,0:T(8,128)(2,1)S(1)} collective-permute-done((bf16[16,256]{1,0:T(8,128)(2,1)S(1)}, bf16[16,256]{1,0:T(8,128)(2,1)S(1)}, u32[]{:S(2)}, u32[]{:S(2)}) %collective-permute-start.1) | collective-permute-done | bytes 8224 | tf_op jit(solution)/shard_map/ppermute | solution.py:235
  11.8 0.8 broadcast_in_dim.6
  12.6 0.0 copy-start
  12.6 7.4 %all-to-all-start = ((bf16[16,16,768]{2,1,0:T(8,128)(2,1)}), bf16[16,16,768]{2,1,0:T(8,128)(2,1)S(1)}, u32[]{:S(2)}, u32[]{:S(2)}) async-start(bf16[16,16,768]{2,1,0:T(8,128)(2,1)} %broadcast_in_dim.6), calls=%async_computation | async-start | bytes 786432 | tf_op jit(solution)/shard_map/all_to_all | solution.py:240
  20.0 0.0 copy-done
  20.0 0.2 copy.24
  20.1 7.7 %all-to-all-done = bf16[16,16,768]{2,1,0:T(8,128)(2,1)S(1)} async-done(((bf16[16,16,768]{2,1,0:T(8,128)(2,1)}), bf16[16,16,768]{2,1,0:T(8,128)(2,1)S(1)}, u32[]{:S(2)}, u32[]{:S(2)}) %all-to-all-start) | async-done | bytes 393248 | tf_op jit(solution)/shard_map/all_to_all | solution.py:240
  27.8 0.0 copy-start.3
  27.8 0.7 copy-done.3
  28.5 0.1 broadcast_in_dim.7.bias
  28.5 1.5 %shard_map.109 = bf16[16,8,4096]{2,1,0:T(8,128)(2,1)} custom-call(bf16[512,256]{1,0:T(8,128)(2,1)S(1)} %bitcast.33, bf16[256,768]{1,0:T(8,128)(2,1)S(1)} %bitcast.31, f32[8,128]{1,0:T(8,128)S(1)} %broadcast_in_dim.7.bias), custom_call_target="tpu_custom_call" | custom-call | tf_op jit(solution)/shard_map/pallas_call | solution.py:276
  30.1 0.0 copy-start.2
  30.1 6.6 %all-to-all-start.1 = ((bf16[16,8,4096]{2,1,0:T(8,128)(2,1)}), bf16[16,8,4096]{2,1,0:T(8,128)(2,1)S(1)}, u32[]{:S(2)}, u32[]{:S(2)}) async-start(bf16[16,8,4096]{2,1,0:T(8,128)(2,1)} %shard_map.109), calls=%async_computation.1 | async-start | bytes 2097152 | tf_op jit(solution)/shard_map/all_to_all | solution.py:279
  36.7 0.0 copy-done.2
  36.7 0.0 copy-start.1
  36.7 0.2 shard_map.110.cot
  36.9 0.6 copy-done.1
  37.5 0.0 copy-start.4
  37.5 14.2 %all-to-all-done.1 = bf16[16,8,4096]{2,1,0:T(8,128)(2,1)S(1)} async-done(((bf16[16,8,4096]{2,1,0:T(8,128)(2,1)}), bf16[16,8,4096]{2,1,0:T(8,128)(2,1)S(1)}, u32[]{:S(2)}, u32[]{:S(2)}) %all-to-all-start.1) | async-done | bytes 1048608 | tf_op jit(solution)/shard_map/all_to_all | solution.py:279
  51.8 0.0 copy-done.4
  51.8 0.1 broadcast_in_dim.8.bias
  51.8 0.9 shard_map.111
  52.8 2.4 %collective-permute-start.2 = (bf16[8,1024]{1,0:T(8,128)(2,1)S(1)}, bf16[8,1024]{1,0:T(8,128)(2,1)S(1)}, u32[]{:S(2)}, u32[]{:S(2)}) collective-permute-start(bf16[8,1024]{1,0:T(8,128)(2,1)S(1)} %get-tuple-element.43), channel_id=1, source_target_pairs={{0,16},{16,32},{32,48},{48,64},{64,80},{80,96},{96,112},{112,128},... | collective-permute-start | bytes 49160 | tf_op jit(solution)/shard_map/ppermute | solution.py:235
  55.2 7.1 %collective-permute-start.3 = (bf16[8,1024]{1,0:T(8,128)(2,1)S(1)}, bf16[8,1024]{1,0:T(8,128)(2,1)S(1)}, u32[]{:S(2)}, u32[]{:S(2)}) collective-permute-start(bf16[8,1024]{1,0:T(8,128)(2,1)S(1)} %get-tuple-element.42), channel_id=1, source_target_pairs={{0,496},{16,0},{32,16},{48,32},{64,48},{80,64},{96,80},{112,96},{1... | collective-permute-start | bytes 49160 | tf_op jit(solution)/shard_map/ppermute | solution.py:235
  62.3 0.1 copy.16
  62.5 0.0 collective-permute-done.2.low
  62.5 1.2 collective-permute-done.3.high
  63.7 0.7 shard_map.112
  64.4 15.6 %all_to_all.30.parts = bf16[16,8,2048]{2,1,0:T(8,128)(2,1)S(1)} all-to-all(bf16[16,8,2048]{2,1,0:T(8,128)(2,1)S(1)} %bitcast.34), channel_id=1, replica_groups=mesh['space'=32,'filt'=16] {'filt'}, dimensions={0} | all-to-all | bytes 1048576 | tf_op jit(solution)/shard_map/all_to_all | solution.py:294
  80.0 1.1 shard_map.113
  81.0 8.2 %all-to-all-start.3 = ((bf16[8,160,128]{2,1,0:T(8,128)(2,1)}), bf16[8,160,128]{2,1,0:T(8,128)(2,1)S(1)}, u32[]{:S(2)}, u32[]{:S(2)}) async-start(bf16[8,160,128]{2,1,0:T(8,128)(2,1)} %get-tuple-element.27), calls=%async_computation.3 | async-start | bytes 655360 | tf_op jit(solution)/shard_map/all_to_all | solution.py:257
  89.3 3.4 %collective-permute-start.4 = (bf16[8,1024]{1,0:T(8,128)(2,1)S(1)}, bf16[8,1024]{1,0:T(8,128)(2,1)S(1)}, u32[]{:S(2)}, u32[]{:S(2)}) collective-permute-start(bf16[8,1024]{1,0:T(8,128)(2,1)S(1)} %get-tuple-element.41), channel_id=1, source_target_pairs={{0,16},{16,32},{32,48},{48,64},{64,80},{80,96},{96,112},{112,128},... | collective-permute-start | bytes 49160 | tf_op jit(solution)/shard_map/ppermute | solution.py:235
  92.7 2.5 %collective-permute-start.5 = (bf16[8,1024]{1,0:T(8,128)(2,1)S(1)}, bf16[8,1024]{1,0:T(8,128)(2,1)S(1)}, u32[]{:S(2)}, u32[]{:S(2)}) collective-permute-start(bf16[8,1024]{1,0:T(8,128)(2,1)S(1)} %get-tuple-element.40), channel_id=1, source_target_pairs={{0,496},{16,0},{32,16},{48,32},{64,48},{80,64},{96,80},{112,96},{1... | collective-permute-start | bytes 49160 | tf_op jit(solution)/shard_map/ppermute | solution.py:235
  95.1 0.0 collective-permute-done.4.low
  95.1 4.5 %collective-permute-done.5.high = bf16[8,1024]{1,0:T(8,128)(2,1)S(1)} collective-permute-done((bf16[8,1024]{1,0:T(8,128)(2,1)S(1)}, bf16[8,1024]{1,0:T(8,128)(2,1)S(1)}, u32[]{:S(2)}, u32[]{:S(2)}) %collective-permute-start.5) | collective-permute-done | bytes 16416 | tf_op jit(solution)/shard_map/ppermute | solution.py:235
  99.6 0.0 all-to-all-done.3.parts
  99.7 9.1 %collective-permute-start.6 = (bf16[160,128]{1,0:T(8,128)(2,1)S(1)}, bf16[160,128]{1,0:T(8,128)(2,1)S(1)}, u32[]{:S(2)}, u32[]{:S(2)}) collective-permute-start(bf16[160,128]{1,0:T(8,128)(2,1)S(1)} %shard_map.114.one), channel_id=1, source_target_pairs={{0,128},{16,144},{32,160},{48,176},{64,192},{80,208},{96,224},{112... | collective-permute-start | bytes 122888 | tf_op jit(solution)/shard_map/ppermute | solution.py:251
  108.8 0.2 copy.23
  108.9 0.1 copy.18.weight
  109.1 1.0 shard_map.116
  110.0 0.7 collective-permute-done.6.other
  110.7 6.0 %all-to-all-start.4 = ((bf16[16,16,256]{2,1,0:T(8,128)(2,1)}), bf16[16,16,256]{2,1,0:T(8,128)(2,1)S(1)}, u32[]{:S(2)}, u32[]{:S(2)}) async-start(bf16[16,16,256]{2,1,0:T(8,128)(2,1)} %bitcast.11), calls=%async_computation.4 | async-start | bytes 262144 | tf_op jit(solution)/shard_map/all_to_all | solution.py:314
  116.7 5.7 %collective-permute-start.7 = (bf16[160,128]{1,0:T(8,128)(2,1)S(1)}, bf16[160,128]{1,0:T(8,128)(2,1)S(1)}, u32[]{:S(2)}, u32[]{:S(2)}) collective-permute-start(bf16[160,128]{1,0:T(8,128)(2,1)S(1)} %shard_map.115.one), channel_id=1, source_target_pairs={{0,384},{16,400},{32,416},{48,432},{64,448},{80,464},{96,480},{112... | collective-permute-start | bytes 122888 | tf_op jit(solution)/shard_map/ppermute | solution.py:251
  122.4 4.2 %collective-permute-done.7.other = bf16[160,128]{1,0:T(8,128)(2,1)S(1)} collective-permute-done((bf16[160,128]{1,0:T(8,128)(2,1)S(1)}, bf16[160,128]{1,0:T(8,128)(2,1)S(1)}, u32[]{:S(2)}, u32[]{:S(2)}) %collective-permute-start.7) | collective-permute-done | bytes 40992 | tf_op jit(solution)/shard_map/ppermute | solution.py:251
  126.6 0.0 all-to-all-done.4.parts
  126.6 0.8 shard_map.118
  127.3 8.3 %all-to-all-start.5 = ((bf16[8,160,128]{2,1,0:T(8,128)(2,1)}), bf16[8,160,128]{2,1,0:T(8,128)(2,1)S(1)}, u32[]{:S(2)}, u32[]{:S(2)}) async-start(bf16[8,160,128]{2,1,0:T(8,128)(2,1)} %shard_map.118), calls=%async_computation.5 | async-start | bytes 655360 | tf_op jit(solution)/shard_map/all_to_all | solution.py:257
  135.7 0.6 reshape.66
  136.3 0.6 reshape.71
  136.9 7.9 %all-to-all-done.5.refs_0_ = bf16[8,160,128]{2,1,0:T(8,128)(2,1)S(1)} async-done(((bf16[8,160,128]{2,1,0:T(8,128)(2,1)}), bf16[8,160,128]{2,1,0:T(8,128)(2,1)S(1)}, u32[]{:S(2)}, u32[]{:S(2)}) %all-to-all-start.5) | async-done | bytes 327712 | tf_op jit(solution)/shard_map/all_to_all | solution.py:257
  144.8 0.9 shard_map.119
  (10 shorter events, 0.2 us)
Async XLA Ops:
  1.3 5.9 %collective-permute-start = (bf16[16,256]{1,0:T(8,128)(2,1)S(1)}, bf16[16,256]{1,0:T(8,128)(2,1)S(1)}, u32[]{:S(2)}, u32[]{:S(2)}) collective-permute-start(bf16[16,256]{1,0:T(8,128)(2,1)S(1)} %bitcast.39), channel_id=1, source_target_pairs={{0,16},{16,32},{32,48},{48,64},{64,80},{80,96},{96,112},{112,128},... | collective-permute-start | bytes 24584 | tf_op jit(solution)/shard_map/ppermute | solution.py:235
  5.3 6.4 %collective-permute-start.1 = (bf16[16,256]{1,0:T(8,128)(2,1)S(1)}, bf16[16,256]{1,0:T(8,128)(2,1)S(1)}, u32[]{:S(2)}, u32[]{:S(2)}) collective-permute-start(bf16[16,256]{1,0:T(8,128)(2,1)S(1)} %bitcast.40), channel_id=1, source_target_pairs={{0,496},{16,0},{32,16},{48,32},{64,48},{80,64},{96,80},{112,96},{1... | collective-permute-start | bytes 24584 | tf_op jit(solution)/shard_map/ppermute | solution.py:235
  12.6 7.4 %copy-start = (bf16[8,64,256]{2,1,0:T(8,128)(2,1)S(1)}, bf16[8,64,256]{2,1,0:T(8,128)(2,1)}, u32[]{:S(2)}) copy-start(bf16[8,64,256]{2,1,0:T(8,128)(2,1)} %param.7) | copy-start | bytes 786436
  12.6 15.3 %all-to-all-start = ((bf16[16,16,768]{2,1,0:T(8,128)(2,1)}), bf16[16,16,768]{2,1,0:T(8,128)(2,1)S(1)}, u32[]{:S(2)}, u32[]{:S(2)}) async-start(bf16[16,16,768]{2,1,0:T(8,128)(2,1)} %broadcast_in_dim.6), calls=%async_computation | async-start | bytes 786432 | tf_op jit(solution)/shard_map/all_to_all | solution.py:240
  27.8 0.7 copy-start.3
  30.1 6.6 %copy-start.2 = (bf16[2,8,4,256]{3,2,1,0:T(4,128)(2,1)S(1)}, bf16[2,8,4,256]{3,2,1,0:T(4,128)(2,1)}, u32[]{:S(2)}) copy-start(bf16[2,8,4,256]{3,2,1,0:T(4,128)(2,1)} %param.11) | copy-start | bytes 98308
  30.1 21.7 %all-to-all-start.1 = ((bf16[16,8,4096]{2,1,0:T(8,128)(2,1)}), bf16[16,8,4096]{2,1,0:T(8,128)(2,1)S(1)}, u32[]{:S(2)}, u32[]{:S(2)}) async-start(bf16[16,8,4096]{2,1,0:T(8,128)(2,1)} %shard_map.109), calls=%async_computation.1 | async-start | bytes 2097152 | tf_op jit(solution)/shard_map/all_to_all | solution.py:279
  36.7 0.8 copy-start.1
  37.5 14.2 %copy-start.4 = (bf16[8]{0:T(256)(128)(2,1)S(1)}, bf16[8]{0:T(256)(128)(2,1)}, u32[]{:S(2)}) copy-start(bf16[8]{0:T(256)(128)(2,1)} %param.10) | copy-start | bytes 52
  52.8 9.7 %collective-permute-start.2 = (bf16[8,1024]{1,0:T(8,128)(2,1)S(1)}, bf16[8,1024]{1,0:T(8,128)(2,1)S(1)}, u32[]{:S(2)}, u32[]{:S(2)}) collective-permute-start(bf16[8,1024]{1,0:T(8,128)(2,1)S(1)} %get-tuple-element.43), channel_id=1, source_target_pairs={{0,16},{16,32},{32,48},{48,64},{64,80},{80,96},{96,112},{112,128},... | collective-permute-start | bytes 49160 | tf_op jit(solution)/shard_map/ppermute | solution.py:235
  55.2 8.6 %collective-permute-start.3 = (bf16[8,1024]{1,0:T(8,128)(2,1)S(1)}, bf16[8,1024]{1,0:T(8,128)(2,1)S(1)}, u32[]{:S(2)}, u32[]{:S(2)}) collective-permute-start(bf16[8,1024]{1,0:T(8,128)(2,1)S(1)} %get-tuple-element.42), channel_id=1, source_target_pairs={{0,496},{16,0},{32,16},{48,32},{64,48},{80,64},{96,80},{112,96},{1... | collective-permute-start | bytes 49160 | tf_op jit(solution)/shard_map/ppermute | solution.py:235
  81.0 18.6 %all-to-all-start.3 = ((bf16[8,160,128]{2,1,0:T(8,128)(2,1)}), bf16[8,160,128]{2,1,0:T(8,128)(2,1)S(1)}, u32[]{:S(2)}, u32[]{:S(2)}) async-start(bf16[8,160,128]{2,1,0:T(8,128)(2,1)} %get-tuple-element.27), calls=%async_computation.3 | async-start | bytes 655360 | tf_op jit(solution)/shard_map/all_to_all | solution.py:257
  89.3 5.8 %collective-permute-start.4 = (bf16[8,1024]{1,0:T(8,128)(2,1)S(1)}, bf16[8,1024]{1,0:T(8,128)(2,1)S(1)}, u32[]{:S(2)}, u32[]{:S(2)}) collective-permute-start(bf16[8,1024]{1,0:T(8,128)(2,1)S(1)} %get-tuple-element.41), channel_id=1, source_target_pairs={{0,16},{16,32},{32,48},{48,64},{64,80},{80,96},{96,112},{112,128},... | collective-permute-start | bytes 49160 | tf_op jit(solution)/shard_map/ppermute | solution.py:235
  92.7 7.0 %collective-permute-start.5 = (bf16[8,1024]{1,0:T(8,128)(2,1)S(1)}, bf16[8,1024]{1,0:T(8,128)(2,1)S(1)}, u32[]{:S(2)}, u32[]{:S(2)}) collective-permute-start(bf16[8,1024]{1,0:T(8,128)(2,1)S(1)} %get-tuple-element.40), channel_id=1, source_target_pairs={{0,496},{16,0},{32,16},{48,32},{64,48},{80,64},{96,80},{112,96},{1... | collective-permute-start | bytes 49160 | tf_op jit(solution)/shard_map/ppermute | solution.py:235
  99.7 11.1 %collective-permute-start.6 = (bf16[160,128]{1,0:T(8,128)(2,1)S(1)}, bf16[160,128]{1,0:T(8,128)(2,1)S(1)}, u32[]{:S(2)}, u32[]{:S(2)}) collective-permute-start(bf16[160,128]{1,0:T(8,128)(2,1)S(1)} %shard_map.114.one), channel_id=1, source_target_pairs={{0,128},{16,144},{32,160},{48,176},{64,192},{80,208},{96,224},{112... | collective-permute-start | bytes 122888 | tf_op jit(solution)/shard_map/ppermute | solution.py:251
  110.7 15.8 %all-to-all-start.4 = ((bf16[16,16,256]{2,1,0:T(8,128)(2,1)}), bf16[16,16,256]{2,1,0:T(8,128)(2,1)S(1)}, u32[]{:S(2)}, u32[]{:S(2)}) async-start(bf16[16,16,256]{2,1,0:T(8,128)(2,1)} %bitcast.11), calls=%async_computation.4 | async-start | bytes 262144 | tf_op jit(solution)/shard_map/all_to_all | solution.py:314
  116.7 9.9 %collective-permute-start.7 = (bf16[160,128]{1,0:T(8,128)(2,1)S(1)}, bf16[160,128]{1,0:T(8,128)(2,1)S(1)}, u32[]{:S(2)}, u32[]{:S(2)}) collective-permute-start(bf16[160,128]{1,0:T(8,128)(2,1)S(1)} %shard_map.115.one), channel_id=1, source_target_pairs={{0,384},{16,400},{32,416},{48,432},{64,448},{80,464},{96,480},{112... | collective-permute-start | bytes 122888 | tf_op jit(solution)/shard_map/ppermute | solution.py:251
  127.3 17.5 %all-to-all-start.5 = ((bf16[8,160,128]{2,1,0:T(8,128)(2,1)}), bf16[8,160,128]{2,1,0:T(8,128)(2,1)S(1)}, u32[]{:S(2)}, u32[]{:S(2)}) async-start(bf16[8,160,128]{2,1,0:T(8,128)(2,1)} %shard_map.118), calls=%async_computation.5 | async-start | bytes 655360 | tf_op jit(solution)/shard_map/all_to_all | solution.py:257

commit v3 on v2

--- a/solution.py
+++ b/solution.py
@@ -82,7 +82,9 @@
                 out[e : e + 1, col : col + 256] = rows[line : line + 1, :]
 
 
-def activate_kernel(hidden, weight, bias, cot, result, dpre, taps, rows):
+def activate_kernel(
+    hidden, weight, bias, cot, turned, result, share, raw, taps, rows, dpre, cols
+):
     taps[...] = dot(weight[...], hidden[...])
 
     def column(plane, x, parity):
@@ -108,7 +110,7 @@
                 halves.append((pre * sigma).astype(BF16))
                 col = column(z, x, parity)
                 slope = cot[:, col : col + LANE] * sigma * (1.0 + pre * (1.0 - sigma))
-                dpre[:, col : col + LANE] = slope.astype(BF16)
+                dpre[:, col : col + LANE] = slope.astype(BF16).astype(F32)
             both = jnp.concatenate(halves, axis=1)
             natural = dot(both, spread_rows(256, 256), ((1,), (1,)))
             for e in range(8):
@@ -116,37 +118,32 @@
                 rows[line : line + 1, :] = natural[e : e + 1, :]
     result[...] = rows[...].astype(BF16)
 
-
-def mix_back_kernel(low, dpre, high, hidden, weight, share, raw, cols, colb):
-    planes = (
-        low[...].astype(F32),
-        dpre[:, :PLANE].astype(F32),
-        dpre[:, PLANE:].astype(F32),
-        high[...].astype(F32),
-    )
-
-    def cells(plane, x, parity):
-        col = (x % 4) * 256 + parity * LANE
-        return planes[plane][:, col : col + LANE]
-
     for z in range(2):
-        for tz in range(3):
-            for x in range(4):
-                for parity in range(2):
-                    for ty in (-1, 0, 1):
-                        other = (parity - ty) % 2
-                        step = (parity - ty) // 2
-                        for tx in range(3):
-                            value = ahead(cells(z + 2 - tz, x - (tx - 1), other), step)
-                            row = (tz * 9 + tx * 3 + ty + 1) * 8
-                            col = z * PLANE + x * 256 + parity * LANE
-                            cols[row : row + 8, col : col + LANE] = value
-    cols[216:256, :] = jnp.zeros((40, 2 * PLANE), F32)
-    colb[...] = cols[...].astype(BF16)
-    share[...] = dot(weight[...], colb[...]).astype(BF16)
-    raw[...] = dot(colb[...], hidden[...], ((1,), (1,)))
-    total = jnp.sum(planes[1] + planes[2], axis=1, keepdims=True)
+        cols[z * LANE + 72 : (z + 1) * LANE, :] = jnp.zeros((LANE - 72, PLANE), F32)
+        for x in range(4):
+            for parity in range(2):
+                for ty in (-1, 0, 1):
+                    other = (parity - ty) % 2
+                    step = (parity - ty) // 2
+                    for tx in range(3):
+                        col = column(z, x - (tx - 1), other)
+                        value = ahead(dpre[:, col : col + LANE], step)
+                        row = z * LANE + (tx * 3 + ty + 1) * 8
+                        col = column(0, x, parity)
+                        cols[row : row + 8, col : col + LANE] = value
+    moved = cols[...].astype(BF16)
+    lower, upper = moved[:LANE], moved[LANE:]
+    share[:, :PLANE] = dot(turned[:, 2 * LANE :], lower).astype(BF16)
+    share[:, PLANE : 2 * PLANE] = dot(turned[:, LANE:], moved).astype(BF16)
+    share[:, 2 * PLANE : 3 * PLANE] = dot(turned[:, : 2 * LANE], moved).astype(BF16)
+    share[:, 3 * PLANE :] = dot(turned[:, :LANE], upper).astype(BF16)
+    for tz in range(3):
+        one = dot(lower, hidden[:, tz * PLANE : (tz + 1) * PLANE], ((1,), (1,)))
+        two = dot(upper, hidden[:, (tz + 1) * PLANE : (tz + 2) * PLANE], ((1,), (1,)))
+        raw[tz * 72 : (tz + 1) * 72, :] = (one + two)[:72]
+    total = jnp.sum(dpre[...], axis=1, keepdims=True)
     raw[216:224, :] = jnp.broadcast_to(total, (8, LANE))
+    raw[224:256, :] = jnp.zeros((32, LANE), F32)
 
 
 def pick_columns(field, out, base):
@@ -162,21 +159,25 @@
                 )
 
 
-def lift_back_kernel(parts, source, raw_second, dhidden, message, cols, raw, second):
+def lift_back_kernel(parts, source, raw_second, low, high, message, cols, raw, second):
     total = parts[0].astype(F32)
-    for f in range(1, 16):
+    for f in range(1, parts.shape[0]):
         total = total + parts[f].astype(F32)
-    rounded = total.astype(BF16)
-    dhidden[...] = rounded
-    total = rounded.astype(F32)
-    pick_columns(total[:, :PLANE], cols, 0)
-    pick_columns(total[:, PLANE:], cols, LANE)
-    for kz, (plane, place) in enumerate(((1, 2), (0, 1), (1, 1), (0, 0))):
-        raw[kz * LANE : (kz + 1) * LANE, :] = dot(
-            cols[plane * LANE : (plane + 1) * LANE, :].astype(BF16),
-            source[:, place * 256 : (place + 1) * 256],
-            ((1,), (1,)),
-        )
+    low[...] = total[:, : 2 * PLANE]
+    high[...] = total[:, 2 * PLANE :]
+    for plane in range(4):
+        pick_columns(total[:, plane * PLANE : (plane + 1) * PLANE], cols, plane * LANE)
+    pairs = (((0, 1), (2, 2)), ((1, 1), (3, 2)), ((0, 0), (2, 1)), ((1, 0), (3, 1)))
+    for kz, met in enumerate(pairs):
+        part = None
+        for plane, place in met:
+            term = dot(
+                cols[plane * LANE : (plane + 1) * LANE, :].astype(BF16),
+                source[:, place * 256 : (place + 1) * 256],
+                ((1,), (1,)),
+            )
+            part = term if part is None else part + term
+        raw[kz * LANE : (kz + 1) * LANE, :] = part
     second[...] = raw_second[...]
     sums = (second[216:224, :], jnp.broadcast_to(jnp.sum(total, axis=1, keepdims=True), (8, LANE)))
     for i, value in enumerate(sums):
@@ -190,12 +191,11 @@
         message[i, 128:160, :] = second[32 * i : 32 * (i + 1), :].astype(BF16)
 
 
-def lift_input_kernel(low, dhidden, high, weight, share, cols):
-    own = dhidden[...].astype(F32)
-    pick_columns(low[...].astype(F32), cols, 0)
-    pick_columns(own[:, :PLANE], cols, LANE)
-    pick_columns(own[:, PLANE:], cols, 2 * LANE)
-    pick_columns(high[...].astype(F32), cols, 3 * LANE)
+def lift_input_kernel(low, low_other, high, high_other, weight, share, cols):
+    for half, (one, other) in enumerate(((low, low_other), (high, high_other))):
+        total = (one[...] + other[...]).astype(BF16).astype(F32)
+        pick_columns(total[:, :PLANE], cols, 2 * half * LANE)
+        pick_columns(total[:, PLANE:], cols, (2 * half + 1) * LANE)
     share[...] = dot(weight[...], cols[...].astype(BF16)).astype(BF16)
 
 
@@ -265,10 +265,11 @@
     first_turned = first_weight.transpose(2, 1, 0).reshape(256, 512)
     second_rows = second_weight.transpose(1, 0, 2).reshape(216, LANE)
     second_rows = jnp.pad(second_rows, ((0, 8), (0, 0)))
-    second_turned = jnp.pad(second_weight.transpose(2, 1, 0).reshape(LANE, 216), ((0, 0), (0, 40)))
-
-    own = volume.reshape(16, 256)
-    source = jnp.concatenate([shifted(own, 1), own, shifted(own, -1)], axis=1)
+    second_turned = second_weight.transpose(2, 1, 0).reshape(LANE, 3, 72)[:, ::-1]
+    second_turned = jnp.pad(second_turned, ((0, 0), (0, 0), (0, 56))).reshape(LANE, 384)
+
+    source = jnp.concatenate([shifted(volume, 1), volume, shifted(volume, -1)], axis=0)
+    source = source.transpose(1, 0, 2, 3).reshape(16, 768)
     source = gathered(source).reshape(256, 768)
     cot = vmem_call(
         split_kernel, struct((8, 2 * PLANE), F32), [pltpu.VMEM((64, 256), F32)]
@@ -278,36 +279,41 @@
     )(first_rows, source, wide(first_bias))
     hidden = lax.all_to_all(hidden, "filt", 0, 0, tiled=True).reshape(LANE, 4 * PLANE)
 
-    result, dpre = vmem_call(
+    result, share, raw_second = vmem_call(
         activate_kernel,
-        (struct((64, 256), BF16), struct((8, 2 * PLANE), BF16)),
-        [pltpu.VMEM((224, 4 * PLANE), F32), pltpu.VMEM((64, 256), F32)],
-    )(hidden, second_rows, wide(second_bias), cot)
-
-    low = shifted(dpre[:, PLANE:], 1)
-    high = shifted(dpre[:, :PLANE], -1)
-    share, raw_second = vmem_call(
-        mix_back_kernel,
-        (struct((LANE, 2 * PLANE), BF16), struct((256, LANE), F32)),
-        [pltpu.VMEM((256, 2 * PLANE), F32), pltpu.VMEM((256, 2 * PLANE), BF16)],
-    )(low, dpre, high, hidden[:, PLANE : 3 * PLANE], second_turned)
-    parts = lax.all_to_all(share.reshape(16, 8, 2 * PLANE), "filt", 0, 0, tiled=True)
-
-    dhidden, message = vmem_call(
+        (
+            struct((64, 256), BF16),
+            struct((LANE, 4 * PLANE), BF16),
+            struct((256, LANE), F32),
+        ),
+        [
+            pltpu.VMEM((224, 4 * PLANE), F32),
+            pltpu.VMEM((64, 256), F32),
+            pltpu.VMEM((8, 2 * PLANE), F32),
+            pltpu.VMEM((256, PLANE), F32),
+        ],
+    )(hidden, second_rows, wide(second_bias), cot, second_turned)
+    parts = lax.all_to_all(share.reshape(16, 8, 4 * PLANE), "filt", 0, 0, tiled=True)
+
+    low, high, message = vmem_call(
         lift_back_kernel,
-        (struct((8, 2 * PLANE), BF16), struct((NEAR, 160, LANE), BF16)),
-        [pltpu.VMEM((256, 256), F32), pltpu.VMEM((512, 256), F32), pltpu.VMEM((256, LANE), F32)],
+        (
+            struct((8, 2 * PLANE), F32),
+            struct((8, 2 * PLANE), F32),
+            struct((NEAR, 160, LANE), BF16),
+        ),
+        [pltpu.VMEM((512, 256), F32), pltpu.VMEM((512, 256), F32), pltpu.VMEM((256, LANE), F32)],
     )(parts, source, raw_second)
 
-    low = shifted(dhidden[:, PLANE:], 1)
-    high = shifted(dhidden[:, :PLANE], -1)
+    low_other = shifted(high, 1)
+    high_other = shifted(low, -1)
     message = near_exchange(message)
-    message, low, high = lax.optimization_barrier((message, low, high))
+    message, low_other, high_other = lax.optimization_barrier((message, low_other, high_other))
     mine = vmem_call(sum_kernel, struct((160, LANE), BF16))(message)
     other = partner(mine, 0)
     share = vmem_call(
         lift_input_kernel, struct((256, 256), BF16), [pltpu.VMEM((512, 256), F32)]
-    )(low, dhidden, high, first_turned)
+    )(low, low_other, high, high_other, first_turned)
     mine = vmem_call(pair_kernel, struct((160, LANE), BF16))(mine, other)
     mine, share = lax.optimization_barrier((mine, share))
     other = partner(mine, 1)

time: 147 us -> 143 us (0.973)
  starting transfers between devices: 72.5 us -> 64.6 us
  blocking collectives: 15.6 us -> 20.6 us
    ppermute x6 -> x4, starting transfers between devices: 21.3 us -> 11.8 us  [shifted(): lax.ppermute(value, 'space', [(i, (i + step) % count) for i in range(coun...]
    all_to_all x1, blocking collectives: 15.6 us -> 20.6 us  [per_device(): lax.all_to_all(share.reshape(16, 8, 4 * PLANE), 'filt', 0, 0, tiled=True)]
    ppermute x6 -> x4, waiting for transfers between devices: 10.2 us -> 9.82 us  [shifted(): lax.ppermute(value, 'space', [(i, (i + step) % count) for i in range(coun...]
    pallas_call x3 -> x2, Pallas kernels: 2.64 us -> 2.95 us  [the longest x1 1.74 us: per_device(): vmem_call(activate_kernel, (struct((64, 256), BF16), struct((LANE, 4 * PL...]
  transfers between devices with their start and end apart: 13 -> 11, of which waited for: 8 -> 8; matrix products, arithmetic and copies ran while one was open for 1% -> 1% of each run, Pallas kernels for 1% -> 1%
where the time goes in v3:
time: 143 us; the launch traced here: 142 us
  starting transfers between devices  64.6 us (45%)
  waiting for transfers between devices  44.2 us (31%)
  blocking collectives  20.6 us (14%)
  Pallas kernels  7.4 us (5%)
  local copies, waits for them, and re-layouts  4.09 us (3%)
    all_to_all x1, blocking collectives, per_device(): lax.all_to_all(share.reshape(16, 8, 4 * PLANE), 'filt', 0, 0, tiled=True)  20.6 us
    all_to_all x2, starting transfers between devices, near_exchange(): lax.all_to_all(value, 'space', 0, 0, axis_index_groups=groups, tiled=True)  17.9 us
    ppermute x2, starting transfers between devices, partner(): return lax.ppermute(value, 'space', pairs)  14.9 us
    all_to_all x1, waiting for transfers between devices, per_device(): lax.all_to_all(hidden, 'filt', 0, 0, tiled=True).reshape(LANE, 4 * PLANE)  14 us
    ppermute x4, starting transfers between devices, shifted(): lax.ppermute(value, 'space', [(i, (i + step) % count) for i in range(coun...  11.8 us
    ppermute x4, waiting for transfers between devices, shifted(): lax.ppermute(value, 'space', [(i, (i + step) % count) for i in range(coun...  9.82 us
    all_to_all x2, waiting for transfers between devices, near_exchange(): lax.all_to_all(value, 'space', 0, 0, axis_index_groups=groups, tiled=True)  7.89 us
    all_to_all x1, waiting for transfers between devices, gathered(): return lax.all_to_all(copies, 'filt', 0, 0, tiled=True)  7.68 us
  transfers between devices with their start and end apart: 11, of which 8 were waited for; matrix products, arithmetic and copies ran while one was open for 1% of the time, Pallas kernels for 1%

profile of v3, /device:TPU:24, one launch (start us, length us, event | category | flops | bytes accessed | tf_op | source)
XLA Modules:
  0.0 142.5 jit_solution(17611635960115829482)
XLA Ops:
  0.6 4.0 %collective-permute-start = (bf16[1,16,2,128]{3,2,1,0:T(2,128)(2,1)}, bf16[1,16,2,128]{3,2,1,0:T(2,128)(2,1)S(1)}, u32[]{:S(2)}, u32[]{:S(2)}) collective-permute-start(bf16[1,16,2,128]{3,2,1,0:T(2,128)(2,1)} %param.6), channel_id=1, source_target_pairs={{0,16},{16,32},{32,48},{48,64},{64,80},{80,96},{96,112},{112,128},... | collective-permute-start | bytes 24584 | tf_op jit(solution)/shard_map/ppermute | solution.py:235
  4.6 1.9 %collective-permute-start.1 = (bf16[1,16,2,128]{3,2,1,0:T(2,128)(2,1)}, bf16[1,16,2,128]{3,2,1,0:T(2,128)(2,1)S(1)}, u32[]{:S(2)}, u32[]{:S(2)}) collective-permute-start(bf16[1,16,2,128]{3,2,1,0:T(2,128)(2,1)} %param.6), channel_id=1, source_target_pairs={{0,496},{16,0},{32,16},{48,32},{64,48},{80,64},{96,80},{112,96},{1... | collective-permute-start | bytes 24584 | tf_op jit(solution)/shard_map/ppermute | solution.py:235
  6.6 0.0 collective-permute-done
  6.6 4.7 %collective-permute-done.1 = bf16[1,16,2,128]{3,2,1,0:T(2,128)(2,1)S(1)} collective-permute-done((bf16[1,16,2,128]{3,2,1,0:T(2,128)(2,1)}, bf16[1,16,2,128]{3,2,1,0:T(2,128)(2,1)S(1)}, u32[]{:S(2)}, u32[]{:S(2)}) %collective-permute-start.1) | collective-permute-done | bytes 8224 | tf_op jit(solution)/shard_map/ppermute | solution.py:235
  11.3 0.7 maximum_bitcast_fusion
  12.1 0.8 broadcast_in_dim.9
  12.9 0.0 copy-start
  12.9 7.4 %all-to-all-start = ((bf16[16,16,768]{2,1,0:T(8,128)(2,1)}), bf16[16,16,768]{2,1,0:T(8,128)(2,1)S(1)}, u32[]{:S(2)}, u32[]{:S(2)}) async-start(bf16[16,16,768]{2,1,0:T(8,128)(2,1)} %broadcast_in_dim.9), calls=%async_computation | async-start | bytes 786432 | tf_op jit(solution)/shard_map/all_to_all | solution.py:240
  20.3 0.0 copy-done
  20.3 0.2 copy.23
  20.4 7.7 %all-to-all-done = bf16[16,16,768]{2,1,0:T(8,128)(2,1)S(1)} async-done(((bf16[16,16,768]{2,1,0:T(8,128)(2,1)}), bf16[16,16,768]{2,1,0:T(8,128)(2,1)S(1)}, u32[]{:S(2)}, u32[]{:S(2)}) %all-to-all-start) | async-done | bytes 393248 | tf_op jit(solution)/shard_map/all_to_all | solution.py:240
  28.1 0.0 copy-start.3
  28.1 0.7 copy-done.3
  28.8 0.1 broadcast_in_dim.10.bias
  28.8 1.5 %shard_map.109 = bf16[16,8,4096]{2,1,0:T(8,128)(2,1)} custom-call(bf16[512,256]{1,0:T(8,128)(2,1)S(1)} %bitcast.31, bf16[256,768]{1,0:T(8,128)(2,1)S(1)} %bitcast.28, f32[8,128]{1,0:T(8,128)S(1)} %broadcast_in_dim.10.bias), custom_call_target="tpu_custom_call" | custom-call | tf_op jit(solution)/shard_map/pallas_call | solution.py:277
  30.4 0.0 copy-start.1
  30.4 6.6 %all-to-all-start.1 = ((bf16[16,8,4096]{2,1,0:T(8,128)(2,1)}), bf16[16,8,4096]{2,1,0:T(8,128)(2,1)S(1)}, u32[]{:S(2)}, u32[]{:S(2)}) async-start(bf16[16,8,4096]{2,1,0:T(8,128)(2,1)} %shard_map.109), calls=%async_computation.1 | async-start | bytes 2097152 | tf_op jit(solution)/shard_map/all_to_all | solution.py:280
  37.0 0.0 copy-done.1
  37.0 0.0 copy-start.2
  37.0 0.1 copy.17.turned
  37.1 0.6 copy-done.2
  37.8 0.2 shard_map.110.cot
  38.0 0.0 copy-start.4
  38.0 14.0 %all-to-all-done.1 = bf16[16,8,4096]{2,1,0:T(8,128)(2,1)S(1)} async-done(((bf16[16,8,4096]{2,1,0:T(8,128)(2,1)}), bf16[16,8,4096]{2,1,0:T(8,128)(2,1)S(1)}, u32[]{:S(2)}, u32[]{:S(2)}) %all-to-all-start.1) | async-done | bytes 1048608 | tf_op jit(solution)/shard_map/all_to_all | solution.py:280
  52.1 0.0 copy-done.4
  52.1 0.1 broadcast_in_dim.22.bias
  52.1 1.7 %shard_map.111 = (bf16[64,256]{1,0:T(8,128)(2,1)S(1)}, bf16[128,4096]{1,0:T(8,128)(2,1)S(1)}, f32[256,128]{1,0:T(8,128)S(1)}) custom-call(bf16[128,4096]{1,0:T(8,128)(2,1)S(1)} %bitcast.27, bf16[224,128]{1,0:T(8,128)(2,1)S(1)} %pad.8.weight, f32[8,128]{1,0:T(8,128)S(1)} %broadcast_in_dim.22.bias, f32[8,2048]{1,0:T(8,128)S(1)} %shard_map.110.cot, ...), custom_call_target="tpu_custom_call" | custom-call | tf_op jit(solution)/shard_map/pallas_call | solution.py:282
  53.9 20.6 %all_to_all.30.parts = bf16[16,8,4096]{2,1,0:T(8,128)(2,1)S(1)} all-to-all(bf16[16,8,4096]{2,1,0:T(8,128)(2,1)S(1)} %bitcast.30), channel_id=1, replica_groups=mesh['space'=32,'filt'=16] {'filt'}, dimensions={0} | all-to-all | bytes 2097152 | tf_op jit(solution)/shard_map/all_to_all | solution.py:296
  74.5 1.2 shard_map.112
  75.7 9.8 %all-to-all-start.3 = ((bf16[8,160,128]{2,1,0:T(8,128)(2,1)}), bf16[8,160,128]{2,1,0:T(8,128)(2,1)S(1)}, u32[]{:S(2)}, u32[]{:S(2)}) async-start(bf16[8,160,128]{2,1,0:T(8,128)(2,1)} %get-tuple-element.26), calls=%async_computation.3 | async-start | bytes 655360 | tf_op jit(solution)/shard_map/all_to_all | solution.py:257
  85.5 3.4 %collective-permute-start.2 = (f32[8,2048]{1,0:T(8,128)S(1)}, f32[8,2048]{1,0:T(8,128)S(1)}, u32[]{:S(2)}, u32[]{:S(2)}) collective-permute-start(f32[8,2048]{1,0:T(8,128)S(1)} %get-tuple-element.27.high), channel_id=1, source_target_pairs={{0,16},{16,32},{32,48},{48,64},{64,80},{80,96},{96,112},{112,128},... | collective-permute-start | bytes 196616 | tf_op jit(solution)/shard_map/ppermute | solution.py:235
  88.8 2.5 %collective-permute-start.3 = (f32[8,2048]{1,0:T(8,128)S(1)}, f32[8,2048]{1,0:T(8,128)S(1)}, u32[]{:S(2)}, u32[]{:S(2)}) collective-permute-start(f32[8,2048]{1,0:T(8,128)S(1)} %get-tuple-element.28.low), channel_id=1, source_target_pairs={{0,496},{16,0},{32,16},{48,32},{64,48},{80,64},{96,80},{112,96},{1... | collective-permute-start | bytes 196616 | tf_op jit(solution)/shard_map/ppermute | solution.py:235
  91.3 1.0 collective-permute-done.2.low_other
  92.3 4.1 %collective-permute-done.3.high_other = f32[8,2048]{1,0:T(8,128)S(1)} collective-permute-done((f32[8,2048]{1,0:T(8,128)S(1)}, f32[8,2048]{1,0:T(8,128)S(1)}, u32[]{:S(2)}, u32[]{:S(2)}) %collective-permute-start.3) | collective-permute-done | bytes 65568 | tf_op jit(solution)/shard_map/ppermute | solution.py:235
  96.4 0.0 all-to-all-done.3.parts
  96.5 9.1 %collective-permute-start.4 = (bf16[160,128]{1,0:T(8,128)(2,1)S(1)}, bf16[160,128]{1,0:T(8,128)(2,1)S(1)}, u32[]{:S(2)}, u32[]{:S(2)}) collective-permute-start(bf16[160,128]{1,0:T(8,128)(2,1)S(1)} %shard_map.113.one), channel_id=1, source_target_pairs={{0,128},{16,144},{32,160},{48,176},{64,192},{80,208},{96,224},{112... | collective-permute-start | bytes 122888 | tf_op jit(solution)/shard_map/ppermute | solution.py:251
  105.6 0.2 copy.22
  105.7 0.1 copy.19.weight
  105.9 1.0 shard_map.115
  106.9 0.7 collective-permute-done.4.other
  107.6 6.1 %all-to-all-start.4 = ((bf16[16,16,256]{2,1,0:T(8,128)(2,1)}), bf16[16,16,256]{2,1,0:T(8,128)(2,1)S(1)}, u32[]{:S(2)}, u32[]{:S(2)}) async-start(bf16[16,16,256]{2,1,0:T(8,128)(2,1)} %bitcast.13), calls=%async_computation.4 | async-start | bytes 262144 | tf_op jit(solution)/shard_map/all_to_all | solution.py:320
  113.6 5.8 %collective-permute-start.5 = (bf16[160,128]{1,0:T(8,128)(2,1)S(1)}, bf16[160,128]{1,0:T(8,128)(2,1)S(1)}, u32[]{:S(2)}, u32[]{:S(2)}) collective-permute-start(bf16[160,128]{1,0:T(8,128)(2,1)S(1)} %shard_map.114.one), channel_id=1, source_target_pairs={{0,384},{16,400},{32,416},{48,432},{64,448},{80,464},{96,480},{112... | collective-permute-start | bytes 122888 | tf_op jit(solution)/shard_map/ppermute | solution.py:251
  119.4 4.1 %collective-permute-done.5.other = bf16[160,128]{1,0:T(8,128)(2,1)S(1)} collective-permute-done((bf16[160,128]{1,0:T(8,128)(2,1)S(1)}, bf16[160,128]{1,0:T(8,128)(2,1)S(1)}, u32[]{:S(2)}, u32[]{:S(2)}) %collective-permute-start.5) | collective-permute-done | bytes 40992 | tf_op jit(solution)/shard_map/ppermute | solution.py:251
  123.5 0.0 all-to-all-done.4.parts
  123.5 0.8 shard_map.117
  124.3 8.1 %all-to-all-start.5 = ((bf16[8,160,128]{2,1,0:T(8,128)(2,1)}), bf16[8,160,128]{2,1,0:T(8,128)(2,1)S(1)}, u32[]{:S(2)}, u32[]{:S(2)}) async-start(bf16[8,160,128]{2,1,0:T(8,128)(2,1)} %shard_map.117), calls=%async_computation.5 | async-start | bytes 655360 | tf_op jit(solution)/shard_map/all_to_all | solution.py:257
  132.4 0.6 reshape.67
  133.0 0.6 reshape.71
  133.6 7.9 %all-to-all-done.5.refs_0_ = bf16[8,160,128]{2,1,0:T(8,128)(2,1)S(1)} async-done(((bf16[8,160,128]{2,1,0:T(8,128)(2,1)}), bf16[8,160,128]{2,1,0:T(8,128)(2,1)S(1)}, u32[]{:S(2)}, u32[]{:S(2)}) %all-to-all-start.5) | async-done | bytes 327712 | tf_op jit(solution)/shard_map/all_to_all | solution.py:257
  141.5 0.9 shard_map.118
  (9 shorter events, 0.2 us)
Async XLA Ops:
  0.6 5.9 %collective-permute-start = (bf16[1,16,2,128]{3,2,1,0:T(2,128)(2,1)}, bf16[1,16,2,128]{3,2,1,0:T(2,128)(2,1)S(1)}, u32[]{:S(2)}, u32[]{:S(2)}) collective-permute-start(bf16[1,16,2,128]{3,2,1,0:T(2,128)(2,1)} %param.6), channel_id=1, source_target_pairs={{0,16},{16,32},{32,48},{48,64},{64,80},{80,96},{96,112},{112,128},... | collective-permute-start | bytes 24584 | tf_op jit(solution)/shard_map/ppermute | solution.py:235
  4.6 6.7 %collective-permute-start.1 = (bf16[1,16,2,128]{3,2,1,0:T(2,128)(2,1)}, bf16[1,16,2,128]{3,2,1,0:T(2,128)(2,1)S(1)}, u32[]{:S(2)}, u32[]{:S(2)}) collective-permute-start(bf16[1,16,2,128]{3,2,1,0:T(2,128)(2,1)} %param.6), channel_id=1, source_target_pairs={{0,496},{16,0},{32,16},{48,32},{64,48},{80,64},{96,80},{112,96},{1... | collective-permute-start | bytes 24584 | tf_op jit(solution)/shard_map/ppermute | solution.py:235
  12.9 7.4 %copy-start = (bf16[8,64,256]{2,1,0:T(8,128)(2,1)S(1)}, bf16[8,64,256]{2,1,0:T(8,128)(2,1)}, u32[]{:S(2)}) copy-start(bf16[8,64,256]{2,1,0:T(8,128)(2,1)} %param.7) | copy-start | bytes 786436
  12.9 15.3 %all-to-all-start = ((bf16[16,16,768]{2,1,0:T(8,128)(2,1)}), bf16[16,16,768]{2,1,0:T(8,128)(2,1)S(1)}, u32[]{:S(2)}, u32[]{:S(2)}) async-start(bf16[16,16,768]{2,1,0:T(8,128)(2,1)} %broadcast_in_dim.9), calls=%async_computation | async-start | bytes 786432 | tf_op jit(solution)/shard_map/all_to_all | solution.py:240
  28.1 0.7 copy-start.3
  30.4 6.6 %copy-start.1 = (bf16[8,27,128]{2,0,1:T(8,128)(2,1)S(1)}, bf16[8,27,128]{2,0,1:T(8,128)(2,1)}, u32[]{:S(2)}) copy-start(bf16[8,27,128]{2,0,1:T(8,128)(2,1)} %param.9) | copy-start | bytes 165892
  30.4 21.7 %all-to-all-start.1 = ((bf16[16,8,4096]{2,1,0:T(8,128)(2,1)}), bf16[16,8,4096]{2,1,0:T(8,128)(2,1)S(1)}, u32[]{:S(2)}, u32[]{:S(2)}) async-start(bf16[16,8,4096]{2,1,0:T(8,128)(2,1)} %shard_map.109), calls=%async_computation.1 | async-start | bytes 2097152 | tf_op jit(solution)/shard_map/all_to_all | solution.py:280
  37.0 0.8 copy-start.2
  38.0 14.1 %copy-start.4 = (bf16[8]{0:T(256)(128)(2,1)S(1)}, bf16[8]{0:T(256)(128)(2,1)}, u32[]{:S(2)}) copy-start(bf16[8]{0:T(256)(128)(2,1)} %param.10) | copy-start | bytes 52
  75.7 20.7 %all-to-all-start.3 = ((bf16[8,160,128]{2,1,0:T(8,128)(2,1)}), bf16[8,160,128]{2,1,0:T(8,128)(2,1)S(1)}, u32[]{:S(2)}, u32[]{:S(2)}) async-start(bf16[8,160,128]{2,1,0:T(8,128)(2,1)} %get-tuple-element.26), calls=%async_computation.3 | async-start | bytes 655360 | tf_op jit(solution)/shard_map/all_to_all | solution.py:257
  85.5 6.8 %collective-permute-start.2 = (f32[8,2048]{1,0:T(8,128)S(1)}, f32[8,2048]{1,0:T(8,128)S(1)}, u32[]{:S(2)}, u32[]{:S(2)}) collective-permute-start(f32[8,2048]{1,0:T(8,128)S(1)} %get-tuple-element.27.high), channel_id=1, source_target_pairs={{0,16},{16,32},{32,48},{48,64},{64,80},{80,96},{96,112},{112,128},... | collective-permute-start | bytes 196616 | tf_op jit(solution)/shard_map/ppermute | solution.py:235
  88.8 7.6 %collective-permute-start.3 = (f32[8,2048]{1,0:T(8,128)S(1)}, f32[8,2048]{1,0:T(8,128)S(1)}, u32[]{:S(2)}, u32[]{:S(2)}) collective-permute-start(f32[8,2048]{1,0:T(8,128)S(1)} %get-tuple-element.28.low), channel_id=1, source_target_pairs={{0,496},{16,0},{32,16},{48,32},{64,48},{80,64},{96,80},{112,96},{1... | collective-permute-start | bytes 196616 | tf_op jit(solution)/shard_map/ppermute | solution.py:235
  96.5 11.1 %collective-permute-start.4 = (bf16[160,128]{1,0:T(8,128)(2,1)S(1)}, bf16[160,128]{1,0:T(8,128)(2,1)S(1)}, u32[]{:S(2)}, u32[]{:S(2)}) collective-permute-start(bf16[160,128]{1,0:T(8,128)(2,1)S(1)} %shard_map.113.one), channel_id=1, source_target_pairs={{0,128},{16,144},{32,160},{48,176},{64,192},{80,208},{96,224},{112... | collective-permute-start | bytes 122888 | tf_op jit(solution)/shard_map/ppermute | solution.py:251
  107.6 16.0 %all-to-all-start.4 = ((bf16[16,16,256]{2,1,0:T(8,128)(2,1)}), bf16[16,16,256]{2,1,0:T(8,128)(2,1)S(1)}, u32[]{:S(2)}, u32[]{:S(2)}) async-start(bf16[16,16,256]{2,1,0:T(8,128)(2,1)} %bitcast.13), calls=%async_computation.4 | async-start | bytes 262144 | tf_op jit(solution)/shard_map/all_to_all | solution.py:320
  113.6 9.9 %collective-permute-start.5 = (bf16[160,128]{1,0:T(8,128)(2,1)S(1)}, bf16[160,128]{1,0:T(8,128)(2,1)S(1)}, u32[]{:S(2)}, u32[]{:S(2)}) collective-permute-start(bf16[160,128]{1,0:T(8,128)(2,1)S(1)} %shard_map.114.one), channel_id=1, source_target_pairs={{0,384},{16,400},{32,416},{48,432},{64,448},{80,464},{96,480},{112... | collective-permute-start | bytes 122888 | tf_op jit(solution)/shard_map/ppermute | solution.py:251
  124.3 17.3 %all-to-all-start.5 = ((bf16[8,160,128]{2,1,0:T(8,128)(2,1)}), bf16[8,160,128]{2,1,0:T(8,128)(2,1)S(1)}, u32[]{:S(2)}, u32[]{:S(2)}) async-start(bf16[8,160,128]{2,1,0:T(8,128)(2,1)} %shard_map.117), calls=%async_computation.5 | async-start | bytes 655360 | tf_op jit(solution)/shard_map/all_to_all | solution.py:257

commit v4 on v3

--- a/solution.py
+++ b/solution.py
@@ -15,10 +15,11 @@
 NEAR = 8
 
 
-def vmem_call(body, outs, scratch=(), limit=24 * 1024 * 1024):
+def vmem_call(body, outs, scratch=(), specs=None, limit=24 * 1024 * 1024):
     return pl.pallas_call(
         body,
         out_shape=outs,
+        **({} if specs is None else {"in_specs": specs}),
         scratch_shapes=list(scratch),
         compiler_params=pltpu.CompilerParams(vmem_limit_bytes=limit),
     )
@@ -33,7 +34,19 @@
     return lax.dot_general(a, b, (dims, ((), ())), preferred_element_type=F32)
 
 
-def hidden_kernel(weight, source, bias, out, taps):
+def hidden_kernel(odd, weight, pair, outer, bias, source, out, taps):
+    @pl.when(odd[0] == 0)
+    def _():
+        source[:, :256] = outer[...]
+        source[:, 256:512] = pair[:256]
+        source[:, 512:] = pair[256:]
+
+    @pl.when(odd[0] == 1)
+    def _():
+        source[:, :256] = pair[:256]
+        source[:, 256:512] = pair[256:]
+        source[:, 512:] = outer[...]
+
     taps[...] = dot(weight[...], source[...])
 
     def tap(kz, kx, ky, plane, xi):
@@ -83,9 +96,10 @@
 
 
 def activate_kernel(
-    hidden, weight, bias, cot, turned, result, share, raw, taps, rows, dpre, cols
+    near, across, weight, bias, cot, turned, result, own, share, raw, taps, rows, dpre, cols
 ):
-    taps[...] = dot(weight[...], hidden[...])
+    hidden = jnp.concatenate([near[...], across[...]], axis=0)
+    taps[...] = dot(weight[...], hidden)
 
     def column(plane, x, parity):
         return plane * PLANE + (x % 4) * 256 + parity * LANE
@@ -133,10 +147,11 @@
                         cols[row : row + 8, col : col + LANE] = value
     moved = cols[...].astype(BF16)
     lower, upper = moved[:LANE], moved[LANE:]
-    share[:, :PLANE] = dot(turned[:, 2 * LANE :], lower).astype(BF16)
-    share[:, PLANE : 2 * PLANE] = dot(turned[:, LANE:], moved).astype(BF16)
-    share[:, 2 * PLANE : 3 * PLANE] = dot(turned[:, : 2 * LANE], moved).astype(BF16)
-    share[:, 3 * PLANE :] = dot(turned[:, :LANE], upper).astype(BF16)
+    for rows_of, out in ((slice(0, 64), own), (slice(64, 128), share)):
+        out[:, :PLANE] = dot(turned[rows_of, 2 * LANE :], lower).astype(BF16)
+        out[:, PLANE : 2 * PLANE] = dot(turned[rows_of, LANE:], moved).astype(BF16)
+        out[:, 2 * PLANE : 3 * PLANE] = dot(turned[rows_of, : 2 * LANE], moved).astype(BF16)
+        out[:, 3 * PLANE :] = dot(turned[rows_of, :LANE], upper).astype(BF16)
     for tz in range(3):
         one = dot(lower, hidden[:, tz * PLANE : (tz + 1) * PLANE], ((1,), (1,)))
         two = dot(upper, hidden[:, (tz + 1) * PLANE : (tz + 2) * PLANE], ((1,), (1,)))
@@ -217,17 +232,17 @@
     return jnp.sum(jnp.where(here == lane, column, 0.0), axis=0, keepdims=True)[:, :8]
 
 
-def finish_kernel(scale, parts, first, second, first_bias, second_bias, left, right, rest):
+def finish_kernel(scale, parts, order, first, second, first_bias, second_bias, left, right, rest):
     for i in range(NEAR):
         left[64 * i : 64 * (i + 1), :] = parts[i, 0:64, :].astype(F32) * scale
         right[64 * i : 64 * (i + 1), :] = parts[i, 64:128, :].astype(F32) * scale
-        rest[32 * i : 32 * (i + 1), :] = parts[i, 128:160, :].astype(F32) * scale
+        rest[32 * i : 32 * (i + 1), :] = parts[i, 128:160, :].astype(F32)
     for d in range(8):
         first[d, :, :LANE] = left[pl.ds(d, 64, stride=8), :]
         first[d, :, LANE:] = right[pl.ds(d, 64, stride=8), :]
-    second[...] = rest[0:216, :]
-    second_bias[...] = as_row(rest[216:224, :] + rest[224:232, :])
-    first_bias[...] = as_row(rest[232:240, :] + rest[240:248, :])
+    second[...] = dot(rest[...].astype(BF16), order[...])[0:216] * scale
+    second_bias[...] = as_row(rest[216:224, :] + rest[224:232, :]) * scale
+    first_bias[...] = as_row(rest[232:240, :] + rest[240:248, :]) * scale
 
 
 def shifted(value, step):
@@ -235,9 +250,36 @@
     return lax.ppermute(value, "space", [(i, (i + step) % count) for i in range(count)])
 
 
-def gathered(value):
-    copies = jnp.broadcast_to(value[None], (lax.axis_size("filt"),) + value.shape)
-    return lax.all_to_all(copies, "filt", 0, 0, tiled=True)
+def chip_exchange(value):
+    count = lax.axis_size("filt")
+    groups = [list(range(core, count, 2)) for core in range(2)]
+    return lax.all_to_all(value, "filt", 0, 0, axis_index_groups=groups, tiled=True)
+
+
+def other_core(value):
+    count = lax.axis_size("filt")
+    return lax.ppermute(value, "filt", [(i, i ^ 1) for i in range(count)])
+
+
+def pair_gather(value):
+    slabs, blocks = lax.axis_size("space"), lax.axis_size("filt")
+    groups = [
+        [s * blocks + f for s in (low, low + 1) for f in range(blocks)] for low in range(0, slabs, 2)
+    ]
+    copies = jnp.broadcast_to(value[None], (2 * blocks,) + value.shape)
+    return lax.all_to_all(copies, ("space", "filt"), 0, 0, axis_index_groups=groups, tiled=True)
+
+
+def outer_plane(value):
+    count = lax.axis_size("space")
+    pairs = [(i, (((i + 1) ^ 1) - 1) % count) for i in range(count)]
+    return lax.ppermute(value, "space", pairs)
+
+
+def by_core(weight, core):
+    split = weight.reshape(weight.shape[:-1] + (8, 2, 8))
+    split = jnp.where(core == 0, split, jnp.flip(split, -2))
+    return jnp.swapaxes(split, -3, -2).reshape(weight.shape)
 
 
 def partner(value, ends):
@@ -259,31 +301,38 @@
 
 def per_device(volume, first_weight, first_bias, second_weight, second_bias, cotangent):
     struct = jax.ShapeDtypeStruct
-    count = lax.axis_size("filt")
     wide = lambda bias: jnp.broadcast_to(bias.astype(F32)[:, None], (8, LANE))
+    core = lax.axis_index("filt") % 2
+    odd = lax.axis_index("space") % 2
     first_rows = first_weight.transpose(1, 0, 2).reshape(512, 256)
     first_turned = first_weight.transpose(2, 1, 0).reshape(256, 512)
-    second_rows = second_weight.transpose(1, 0, 2).reshape(216, LANE)
+    second = by_core(second_weight, core)
+    second_rows = second.transpose(1, 0, 2).reshape(216, LANE)
     second_rows = jnp.pad(second_rows, ((0, 8), (0, 0)))
-    second_turned = second_weight.transpose(2, 1, 0).reshape(LANE, 3, 72)[:, ::-1]
+    second_turned = second.transpose(2, 1, 0).reshape(LANE, 3, 72)[:, ::-1]
     second_turned = jnp.pad(second_turned, ((0, 0), (0, 0), (0, 56))).reshape(LANE, 384)
-
-    source = jnp.concatenate([shifted(volume, 1), volume, shifted(volume, -1)], axis=0)
-    source = source.transpose(1, 0, 2, 3).reshape(16, 768)
-    source = gathered(source).reshape(256, 768)
+    order = by_core(jnp.eye(LANE, dtype=BF16), core).T
+
+    pair = pair_gather(volume.reshape(16, 256)).reshape(2, 256, 256)
+    outer = outer_plane(lax.dynamic_index_in_dim(pair, odd, 0, keepdims=False))
     cot = vmem_call(
         split_kernel, struct((8, 2 * PLANE), F32), [pltpu.VMEM((64, 256), F32)]
     )(cotangent.reshape(64, 256))
-    hidden = vmem_call(
-        hidden_kernel, struct((count, 8, 4 * PLANE), BF16), [pltpu.VMEM((512, 768), F32)]
-    )(first_rows, source, wide(first_bias))
-    hidden = lax.all_to_all(hidden, "filt", 0, 0, tiled=True).reshape(LANE, 4 * PLANE)
-
-    result, share, raw_second = vmem_call(
+    whole = pl.BlockSpec(memory_space=pltpu.VMEM)
+    source, hidden = vmem_call(
+        hidden_kernel,
+        (struct((256, 768), BF16), struct((8, 8, 4 * PLANE), BF16)),
+        [pltpu.VMEM((512, 768), F32)],
+        [pl.BlockSpec(memory_space=pltpu.SMEM)] + [whole] * 4,
+    )(odd.reshape(1), first_rows, pair.reshape(512, 256), outer, wide(first_bias))
+    hidden = chip_exchange(hidden).reshape(64, 4 * PLANE)
+
+    result, own, share, raw_second = vmem_call(
         activate_kernel,
         (
             struct((64, 256), BF16),
-            struct((LANE, 4 * PLANE), BF16),
+            struct((64, 4 * PLANE), BF16),
+            struct((64, 4 * PLANE), BF16),
             struct((256, LANE), F32),
         ),
         [
@@ -292,8 +341,9 @@
             pltpu.VMEM((8, 2 * PLANE), F32),
             pltpu.VMEM((256, PLANE), F32),
         ],
-    )(hidden, second_rows, wide(second_bias), cot, second_turned)
-    parts = lax.all_to_all(share.reshape(16, 8, 4 * PLANE), "filt", 0, 0, tiled=True)
+    )(hidden, other_core(hidden), second_rows, wide(second_bias), cot, second_turned)
+    share = vmem_call(pair_kernel, struct((64, 4 * PLANE), BF16))(own, other_core(share))
+    parts = chip_exchange(share.reshape(8, 8, 4 * PLANE))
 
     low, high, message = vmem_call(
         lift_back_kernel,
@@ -334,7 +384,7 @@
             struct((1, 8), F32),
         ),
         [pltpu.VMEM((512, LANE), F32), pltpu.VMEM((512, LANE), F32), pltpu.VMEM((256, LANE), F32)],
-    )(message)
+    )(message, order)
     return (
         result.reshape(2, 8, 4, 256),
         grad_volume.reshape(1, 16, 2, 128),

time: 143 us -> 136 us (0.951)
  waiting for transfers between devices: 44.2 us -> 35.2 us
  blocking collectives: 20.6 us -> 29 us
  starting transfers between devices: 64.6 us -> 57.3 us
  local copies, waits for them, and re-layouts: 4.09 us -> 5.81 us
    all_to_all x2 -> x1, waiting for transfers between devices: 21.7 us -> 7.23 us  [pair_gather(): lax.all_to_all(copies, ('space', 'filt'), 0, 0, axis_index_groups=groups,...]
    all_to_all x1 -> x2, blocking collectives: 20.6 us -> 29 us  [chip_exchange(): lax.all_to_all(value, 'filt', 0, 0, axis_index_groups=groups, tiled=True)]
    ppermute x0 -> x3, waiting for transfers between devices: none -> 7.77 us  [the longest x1 6.21 us: outer_plane(): return lax.ppermute(value, 'space', pairs)]
    ppermute x0 -> x3, starting transfers between devices: none -> 6.23 us  [the longest x2 4.31 us: other_core(): return lax.ppermute(value, 'filt', [(i, i ^ 1) for i in range(count)])]
    ppermute x4 -> x2, starting transfers between devices: 11.8 us -> 5.83 us  [shifted(): lax.ppermute(value, 'space', [(i, (i + step) % count) for i in range(coun...]
    ppermute x4 -> x2, waiting for transfers between devices: 9.82 us -> 5.05 us  [shifted(): lax.ppermute(value, 'space', [(i, (i + step) % count) for i in range(coun...]
    all_to_all x2 -> x1, starting transfers between devices: 14 us -> 9.28 us  [pair_gather(): lax.all_to_all(copies, ('space', 'filt'), 0, 0, axis_index_groups=groups,...]
    ppermute x2, starting transfers between devices: 14.9 us -> 12.7 us  [partner(): return lax.ppermute(value, 'space', pairs)]
  transfers between devices with their start and end apart: 11 -> 11, of which waited for: 8 -> 8; matrix products, arithmetic and copies ran while one was open for 1% -> 2% of each run, Pallas kernels for 1% -> 1%
where the time goes in v4:
time: 136 us; the launch traced here: 135 us
  starting transfers between devices  57.3 us (42%)
  waiting for transfers between devices  35.2 us (26%)
  blocking collectives  29 us (21%)
  Pallas kernels  6.66 us (5%)
  local copies, waits for them, and re-layouts  5.81 us (4%)
    all_to_all x2, blocking collectives, chip_exchange(): lax.all_to_all(value, 'filt', 0, 0, axis_index_groups=groups, tiled=True)  29 us
    all_to_all x2, starting transfers between devices, near_exchange(): lax.all_to_all(value, 'space', 0, 0, axis_index_groups=groups, tiled=True)  17.2 us
    ppermute x2, starting transfers between devices, partner(): return lax.ppermute(value, 'space', pairs)  12.7 us
    all_to_all x1, starting transfers between devices, pair_gather(): lax.all_to_all(copies, ('space', 'filt'), 0, 0, axis_index_groups=groups,...  9.28 us
    all_to_all x2, waiting for transfers between devices, near_exchange(): lax.all_to_all(value, 'space', 0, 0, axis_index_groups=groups, tiled=True)  8.54 us
    all_to_all x1, waiting for transfers between devices, pair_gather(): lax.all_to_all(copies, ('space', 'filt'), 0, 0, axis_index_groups=groups,...  7.23 us
    ppermute x2, waiting for transfers between devices, partner(): return lax.ppermute(value, 'space', pairs)  6.65 us
    ppermute x1, waiting for transfers between devices, outer_plane(): return lax.ppermute(value, 'space', pairs)  6.21 us
  transfers between devices with their start and end apart: 11, of which 8 were waited for; matrix products, arithmetic and copies ran while one was open for 2% of the time, Pallas kernels for 1%

profile of v4, /device:TPU:24, one launch (start us, length us, event | category | flops | bytes accessed | tf_op | source)
XLA Modules:
  0.0 135.1 jit_solution(5811116167655276014)
XLA Ops:
  0.6 0.7 copy.30
  1.3 0.7 broadcast_in_dim.9
  2.1 9.3 %all-to-all-start = ((bf16[32,16,256]{2,1,0:T(8,128)(2,1)}), bf16[32,16,256]{2,1,0:T(8,128)(2,1)S(1)}, u32[]{:S(2)}, u32[]{:S(2)}) async-start(bf16[32,16,256]{2,1,0:T(8,128)(2,1)} %broadcast_in_dim.9), calls=%async_computation | async-start | bytes 524288 | tf_op jit(solution)/shard_map/all_to_all | solution.py:270
  11.3 0.0 copy-start
  11.4 7.2 %all-to-all-done = bf16[32,16,256]{2,1,0:T(8,128)(2,1)S(1)} async-done(((bf16[32,16,256]{2,1,0:T(8,128)(2,1)}), bf16[32,16,256]{2,1,0:T(8,128)(2,1)S(1)}, u32[]{:S(2)}, u32[]{:S(2)}) %all-to-all-start) | async-done | bytes 262176 | tf_op jit(solution)/shard_map/all_to_all | solution.py:270
  18.6 1.9 %collective-permute-start = (bf16[256,256]{1,0:T(8,128)(2,1)S(1)}, bf16[256,256]{1,0:T(8,128)(2,1)S(1)}, u32[]{:S(2)}, u32[]{:S(2)}) collective-permute-start(bf16[256,256]{1,0:T(8,128)(2,1)S(1)} %dynamic-slice_bitcast_fusion), channel_id=1, source_target_pairs={{0,496},{16,32},{32,16},{48,64},{64,48},{80,96},{96,80},{112,128},... | collective-permute-start | bytes 393224 | tf_op jit(solution)/shard_map/ppermute | solution.py:276
  20.5 0.0 copy-done
  20.6 0.2 copy.29
  20.7 6.2 %collective-permute-done.outer = bf16[256,256]{1,0:T(8,128)(2,1)S(1)} collective-permute-done((bf16[256,256]{1,0:T(8,128)(2,1)S(1)}, bf16[256,256]{1,0:T(8,128)(2,1)S(1)}, u32[]{:S(2)}, u32[]{:S(2)}) %collective-permute-start) | collective-permute-done | bytes 131104 | tf_op jit(solution)/shard_map/ppermute | solution.py:276
  26.9 0.0 copy-start.3
  26.9 0.7 copy-done.3
  27.6 0.1 broadcast_in_dim.10.bias
  27.7 0.5 shard_map.109
  28.1 0.0 copy-start.1
  28.1 14.2 %all_to_all.30 = bf16[8,8,4096]{2,1,0:T(8,128)(2,1)S(1)} all-to-all(bf16[8,8,4096]{2,1,0:T(8,128)(2,1)S(1)} %get-tuple-element.26), channel_id=1, replica_groups={{0,2,4,6,8,10,12,14},{1,3,5,7,9,11,13,15},{16,18,20,22,24,26,28,30},{17..., dimensions={0} | all-to-all | bytes 1048576 | tf_op jit(solution)/shard_map/all_to_all | solution.py:256
  42.3 1.9 %collective-permute-start.1 = (bf16[64,4096]{1,0:T(8,128)(2,1)S(1)}, bf16[64,4096]{1,0:T(8,128)(2,1)S(1)}, u32[]{:S(2)}, u32[]{:S(2)}) collective-permute-start(bf16[64,4096]{1,0:T(8,128)(2,1)S(1)} %bitcast.44), channel_id=1, source_target_pairs={{0,1},{1,0},{2,3},{3,2},{4,5},{5,4},{6,7},{7,6},{8,9},{9,8},{10,11... | collective-permute-start | bytes 1572872 | tf_op jit(solution)/shard_map/ppermute | solution.py:261
  44.3 0.0 copy-done.1
  44.3 0.2 copy.17
  44.5 0.1 fusion
  44.6 0.2 copy.20
  44.8 0.1 copy.21.turned
  44.9 0.2 copy.19
  45.1 0.0 copy-start.2
  45.1 0.7 copy-done.2
  45.9 0.0 copy-start.4
  45.9 0.2 shard_map.110.cot
  46.1 0.0 collective-permute-done.1.across
  46.1 0.4 copy-done.4
  46.5 0.1 broadcast_in_dim.22.bias
  46.6 1.9 %shard_map.111 = (bf16[64,256]{1,0:T(8,128)(2,1)S(1)}, bf16[64,4096]{1,0:T(8,128)(2,1)S(1)}, bf16[64,4096]{1,0:T(8,128)(2,1)S(1)}, f32[256,128]{1,0:T(8,128)S(1)}) custom-call(bf16[64,4096]{1,0:T(8,128)(2,1)S(1)} %bitcast.45, bf16[64,4096]{1,0:T(8,128)(2,1)S(1)} %collective-permute-done.1.across, bf16[224,128]{1,0:T(8,128)(2,1)S(1)} %pad.8.weight, ...), custom_call_target="tpu_custom_call" | custom-call | tf_op jit(solution)/shard_map/pallas_call | solution.py:330
  48.5 2.4 %collective-permute-start.2 = (bf16[64,4096]{1,0:T(8,128)(2,1)S(1)}, bf16[64,4096]{1,0:T(8,128)(2,1)S(1)}, u32[]{:S(2)}, u32[]{:S(2)}) collective-permute-start(bf16[64,4096]{1,0:T(8,128)(2,1)S(1)} %get-tuple-element.29), channel_id=1, source_target_pairs={{0,1},{1,0},{2,3},{3,2},{4,5},{5,4},{6,7},{7,6},{8,9},{9,8},{10,11... | collective-permute-start | bytes 1572872 | tf_op jit(solution)/shard_map/ppermute | solution.py:261
  50.9 1.5 %collective-permute-done.2.other = bf16[64,4096]{1,0:T(8,128)(2,1)S(1)} collective-permute-done((bf16[64,4096]{1,0:T(8,128)(2,1)S(1)}, bf16[64,4096]{1,0:T(8,128)(2,1)S(1)}, u32[]{:S(2)}, u32[]{:S(2)}) %collective-permute-start.2) | collective-permute-done | bytes 524320 | tf_op jit(solution)/shard_map/ppermute | solution.py:261
  52.4 0.1 shard_map.112
  52.5 14.8 %all_to_all.31.parts = bf16[8,8,4096]{2,1,0:T(8,128)(2,1)S(1)} all-to-all(bf16[8,8,4096]{2,1,0:T(8,128)(2,1)S(1)} %bitcast.43), channel_id=1, replica_groups={{0,2,4,6,8,10,12,14},{1,3,5,7,9,11,13,15},{16,18,20,22,24,26,28,30},{17..., dimensions={0} | all-to-all | bytes 1048576 | tf_op jit(solution)/shard_map/all_to_all | solution.py:256
  67.3 1.2 shard_map.113
  68.6 9.6 %all-to-all-start.3 = ((bf16[8,160,128]{2,1,0:T(8,128)(2,1)}), bf16[8,160,128]{2,1,0:T(8,128)(2,1)S(1)}, u32[]{:S(2)}, u32[]{:S(2)}) async-start(bf16[8,160,128]{2,1,0:T(8,128)(2,1)} %get-tuple-element.32), calls=%async_computation.3 | async-start | bytes 655360 | tf_op jit(solution)/shard_map/all_to_all | solution.py:299
  78.1 3.4 %collective-permute-start.3 = (f32[8,2048]{1,0:T(8,128)S(1)}, f32[8,2048]{1,0:T(8,128)S(1)}, u32[]{:S(2)}, u32[]{:S(2)}) collective-permute-start(f32[8,2048]{1,0:T(8,128)S(1)} %get-tuple-element.33.high), channel_id=1, source_target_pairs={{0,16},{16,32},{32,48},{48,64},{64,80},{80,96},{96,112},{112,128},... | collective-permute-start | bytes 196616 | tf_op jit(solution)/shard_map/ppermute | solution.py:250
  81.5 2.5 %collective-permute-start.4 = (f32[8,2048]{1,0:T(8,128)S(1)}, f32[8,2048]{1,0:T(8,128)S(1)}, u32[]{:S(2)}, u32[]{:S(2)}) collective-permute-start(f32[8,2048]{1,0:T(8,128)S(1)} %get-tuple-element.34.low), channel_id=1, source_target_pairs={{0,496},{16,0},{32,16},{48,32},{64,48},{80,64},{96,80},{112,96},{1... | collective-permute-start | bytes 196616 | tf_op jit(solution)/shard_map/ppermute | solution.py:250
  84.0 0.8 collective-permute-done.3.low_other
  84.8 4.2 %collective-permute-done.4.high_other = f32[8,2048]{1,0:T(8,128)S(1)} collective-permute-done((f32[8,2048]{1,0:T(8,128)S(1)}, f32[8,2048]{1,0:T(8,128)S(1)}, u32[]{:S(2)}, u32[]{:S(2)}) %collective-permute-start.4) | collective-permute-done | bytes 65568 | tf_op jit(solution)/shard_map/ppermute | solution.py:250
  89.0 0.0 all-to-all-done.3.parts
  89.1 6.1 %collective-permute-start.5 = (bf16[160,128]{1,0:T(8,128)(2,1)S(1)}, bf16[160,128]{1,0:T(8,128)(2,1)S(1)}, u32[]{:S(2)}, u32[]{:S(2)}) collective-permute-start(bf16[160,128]{1,0:T(8,128)(2,1)S(1)} %shard_map.114.one), channel_id=1, source_target_pairs={{0,128},{16,144},{32,160},{48,176},{64,192},{80,208},{96,224},{112... | collective-permute-start | bytes 122888 | tf_op jit(solution)/shard_map/ppermute | solution.py:293
  95.2 0.2 copy.28
  95.3 0.1 copy.23.weight
  95.5 1.0 shard_map.116
  96.4 3.3 %collective-permute-done.5.other = bf16[160,128]{1,0:T(8,128)(2,1)S(1)} collective-permute-done((bf16[160,128]{1,0:T(8,128)(2,1)S(1)}, bf16[160,128]{1,0:T(8,128)(2,1)S(1)}, u32[]{:S(2)}, u32[]{:S(2)}) %collective-permute-start.5) | collective-permute-done | bytes 40992 | tf_op jit(solution)/shard_map/ppermute | solution.py:293
  99.8 6.1 %all-to-all-start.4 = ((bf16[16,16,256]{2,1,0:T(8,128)(2,1)}), bf16[16,16,256]{2,1,0:T(8,128)(2,1)S(1)}, u32[]{:S(2)}, u32[]{:S(2)}) async-start(bf16[16,16,256]{2,1,0:T(8,128)(2,1)} %bitcast.18), calls=%async_computation.4 | async-start | bytes 262144 | tf_op jit(solution)/shard_map/all_to_all | solution.py:370
  105.8 6.7 %collective-permute-start.6 = (bf16[160,128]{1,0:T(8,128)(2,1)S(1)}, bf16[160,128]{1,0:T(8,128)(2,1)S(1)}, u32[]{:S(2)}, u32[]{:S(2)}) collective-permute-start(bf16[160,128]{1,0:T(8,128)(2,1)S(1)} %shard_map.115.one), channel_id=1, source_target_pairs={{0,384},{16,400},{32,416},{48,432},{64,448},{80,464},{96,480},{112... | collective-permute-start | bytes 122888 | tf_op jit(solution)/shard_map/ppermute | solution.py:293
  112.5 3.3 %collective-permute-done.6.other = bf16[160,128]{1,0:T(8,128)(2,1)S(1)} collective-permute-done((bf16[160,128]{1,0:T(8,128)(2,1)S(1)}, bf16[160,128]{1,0:T(8,128)(2,1)S(1)}, u32[]{:S(2)}, u32[]{:S(2)}) %collective-permute-start.6) | collective-permute-done | bytes 40992 | tf_op jit(solution)/shard_map/ppermute | solution.py:293
  115.8 0.0 all-to-all-done.4.parts
  115.8 0.8 shard_map.118
  116.6 7.6 %all-to-all-start.5 = ((bf16[8,160,128]{2,1,0:T(8,128)(2,1)}), bf16[8,160,128]{2,1,0:T(8,128)(2,1)S(1)}, u32[]{:S(2)}, u32[]{:S(2)}) async-start(bf16[8,160,128]{2,1,0:T(8,128)(2,1)} %shard_map.118), calls=%async_computation.5 | async-start | bytes 655360 | tf_op jit(solution)/shard_map/all_to_all | solution.py:299
  124.2 0.1 fusion.1
  124.3 0.6 reshape.97
  125.0 0.6 reshape.101
  125.6 8.5 %all-to-all-done.5.refs_0_ = bf16[8,160,128]{2,1,0:T(8,128)(2,1)S(1)} async-done(((bf16[8,160,128]{2,1,0:T(8,128)(2,1)}), bf16[8,160,128]{2,1,0:T(8,128)(2,1)S(1)}, u32[]{:S(2)}, u32[]{:S(2)}) %all-to-all-start.5) | async-done | bytes 327712 | tf_op jit(solution)/shard_map/all_to_all | solution.py:299
  134.1 1.0 shard_map.119
  (11 shorter events, 0.2 us)
Async XLA Ops:
  2.1 16.5 %all-to-all-start = ((bf16[32,16,256]{2,1,0:T(8,128)(2,1)}), bf16[32,16,256]{2,1,0:T(8,128)(2,1)S(1)}, u32[]{:S(2)}, u32[]{:S(2)}) async-start(bf16[32,16,256]{2,1,0:T(8,128)(2,1)} %broadcast_in_dim.9), calls=%async_computation | async-start | bytes 524288 | tf_op jit(solution)/shard_map/all_to_all | solution.py:270
  11.3 9.2 %copy-start = (bf16[8,64,256]{2,1,0:T(8,128)(2,1)S(1)}, bf16[8,64,256]{2,1,0:T(8,128)(2,1)}, u32[]{:S(2)}) copy-start(bf16[8,64,256]{2,1,0:T(8,128)(2,1)} %param.7) | copy-start | bytes 786436
  18.6 8.3 %collective-permute-start = (bf16[256,256]{1,0:T(8,128)(2,1)S(1)}, bf16[256,256]{1,0:T(8,128)(2,1)S(1)}, u32[]{:S(2)}, u32[]{:S(2)}) collective-permute-start(bf16[256,256]{1,0:T(8,128)(2,1)S(1)} %dynamic-slice_bitcast_fusion), channel_id=1, source_target_pairs={{0,496},{16,32},{32,16},{48,64},{64,48},{80,96},{96,80},{112,128},... | collective-permute-start | bytes 393224 | tf_op jit(solution)/shard_map/ppermute | solution.py:276
  26.9 0.7 copy-start.3
  28.1 16.1 %copy-start.1 = (bf16[8,27,128]{2,0,1:T(8,128)(2,1)S(1)}, bf16[8,27,128]{2,0,1:T(8,128)(2,1)}, u32[]{:S(2)}) copy-start(bf16[8,27,128]{2,0,1:T(8,128)(2,1)} %param.9) | copy-start | bytes 165892
  42.3 3.8 %collective-permute-start.1 = (bf16[64,4096]{1,0:T(8,128)(2,1)S(1)}, bf16[64,4096]{1,0:T(8,128)(2,1)S(1)}, u32[]{:S(2)}, u32[]{:S(2)}) collective-permute-start(bf16[64,4096]{1,0:T(8,128)(2,1)S(1)} %bitcast.44), channel_id=1, source_target_pairs={{0,1},{1,0},{2,3},{3,2},{4,5},{5,4},{6,7},{7,6},{8,9},{9,8},{10,11... | collective-permute-start | bytes 1572872 | tf_op jit(solution)/shard_map/ppermute | solution.py:261
  45.1 0.8 copy-start.2
  45.9 0.7 copy-start.4
  48.5 3.9 %collective-permute-start.2 = (bf16[64,4096]{1,0:T(8,128)(2,1)S(1)}, bf16[64,4096]{1,0:T(8,128)(2,1)S(1)}, u32[]{:S(2)}, u32[]{:S(2)}) collective-permute-start(bf16[64,4096]{1,0:T(8,128)(2,1)S(1)} %get-tuple-element.29), channel_id=1, source_target_pairs={{0,1},{1,0},{2,3},{3,2},{4,5},{5,4},{6,7},{7,6},{8,9},{9,8},{10,11... | collective-permute-start | bytes 1572872 | tf_op jit(solution)/shard_map/ppermute | solution.py:261
  68.6 20.5 %all-to-all-start.3 = ((bf16[8,160,128]{2,1,0:T(8,128)(2,1)}), bf16[8,160,128]{2,1,0:T(8,128)(2,1)S(1)}, u32[]{:S(2)}, u32[]{:S(2)}) async-start(bf16[8,160,128]{2,1,0:T(8,128)(2,1)} %get-tuple-element.32), calls=%async_computation.3 | async-start | bytes 655360 | tf_op jit(solution)/shard_map/all_to_all | solution.py:299
  78.1 6.7 %collective-permute-start.3 = (f32[8,2048]{1,0:T(8,128)S(1)}, f32[8,2048]{1,0:T(8,128)S(1)}, u32[]{:S(2)}, u32[]{:S(2)}) collective-permute-start(f32[8,2048]{1,0:T(8,128)S(1)} %get-tuple-element.33.high), channel_id=1, source_target_pairs={{0,16},{16,32},{32,48},{48,64},{64,80},{80,96},{96,112},{112,128},... | collective-permute-start | bytes 196616 | tf_op jit(solution)/shard_map/ppermute | solution.py:250
  81.5 7.5 %collective-permute-start.4 = (f32[8,2048]{1,0:T(8,128)S(1)}, f32[8,2048]{1,0:T(8,128)S(1)}, u32[]{:S(2)}, u32[]{:S(2)}) collective-permute-start(f32[8,2048]{1,0:T(8,128)S(1)} %get-tuple-element.34.low), channel_id=1, source_target_pairs={{0,496},{16,0},{32,16},{48,32},{64,48},{80,64},{96,80},{112,96},{1... | collective-permute-start | bytes 196616 | tf_op jit(solution)/shard_map/ppermute | solution.py:250
  89.1 10.7 %collective-permute-start.5 = (bf16[160,128]{1,0:T(8,128)(2,1)S(1)}, bf16[160,128]{1,0:T(8,128)(2,1)S(1)}, u32[]{:S(2)}, u32[]{:S(2)}) collective-permute-start(bf16[160,128]{1,0:T(8,128)(2,1)S(1)} %shard_map.114.one), channel_id=1, source_target_pairs={{0,128},{16,144},{32,160},{48,176},{64,192},{80,208},{96,224},{112... | collective-permute-start | bytes 122888 | tf_op jit(solution)/shard_map/ppermute | solution.py:293
  99.8 16.1 %all-to-all-start.4 = ((bf16[16,16,256]{2,1,0:T(8,128)(2,1)}), bf16[16,16,256]{2,1,0:T(8,128)(2,1)S(1)}, u32[]{:S(2)}, u32[]{:S(2)}) async-start(bf16[16,16,256]{2,1,0:T(8,128)(2,1)} %bitcast.18), calls=%async_computation.4 | async-start | bytes 262144 | tf_op jit(solution)/shard_map/all_to_all | solution.py:370
  105.8 10.0 %collective-permute-start.6 = (bf16[160,128]{1,0:T(8,128)(2,1)S(1)}, bf16[160,128]{1,0:T(8,128)(2,1)S(1)}, u32[]{:S(2)}, u32[]{:S(2)}) collective-permute-start(bf16[160,128]{1,0:T(8,128)(2,1)S(1)} %shard_map.115.one), channel_id=1, source_target_pairs={{0,384},{16,400},{32,416},{48,432},{64,448},{80,464},{96,480},{112... | collective-permute-start | bytes 122888 | tf_op jit(solution)/shard_map/ppermute | solution.py:293
  116.6 17.5 %all-to-all-start.5 = ((bf16[8,160,128]{2,1,0:T(8,128)(2,1)}), bf16[8,160,128]{2,1,0:T(8,128)(2,1)S(1)}, u32[]{:S(2)}, u32[]{:S(2)}) async-start(bf16[8,160,128]{2,1,0:T(8,128)(2,1)} %shard_map.118), calls=%async_computation.5 | async-start | bytes 655360 | tf_op jit(solution)/shard_map/all_to_all | solution.py:299

commit v5 on v4

--- a/solution.py
+++ b/solution.py
@@ -79,6 +79,13 @@
                     out[copy, :, col : col + LANE] = value
 
 
+def copies_kernel(field, out):
+    rows = field[...].astype(F32)
+    plane = jnp.concatenate([rows[:, 0, :], rows[:, 1, :]], axis=1).astype(BF16)
+    for i in range(out.shape[0]):
+        out[i] = plane
+
+
 def spread_rows(rows, cols):
     natural = lax.broadcasted_iota(jnp.int32, (rows, cols), 0)
     split = lax.broadcasted_iota(jnp.int32, (rows, cols), 1)
@@ -96,7 +103,7 @@
 
 
 def activate_kernel(
-    near, across, weight, bias, cot, turned, result, own, share, raw, taps, rows, dpre, cols
+    near, across, weight, bias, cot, turned, active, share, dpre, moved, taps, cols
 ):
     hidden = jnp.concatenate([near[...], across[...]], axis=0)
     taps[...] = dot(weight[...], hidden)
@@ -106,7 +113,6 @@
 
     for z in range(2):
         for x in range(4):
-            halves = []
             for parity in range(2):
                 pre = bias[...]
                 for ty in (-1, 0, 1):
@@ -121,16 +127,10 @@
                             part = term if part is None else part + term
                     pre = pre + ahead(part, step)
                 sigma = 1.0 / (1.0 + jnp.exp(-pre))
-                halves.append((pre * sigma).astype(BF16))
                 col = column(z, x, parity)
+                active[:, col : col + LANE] = pre * sigma
                 slope = cot[:, col : col + LANE] * sigma * (1.0 + pre * (1.0 - sigma))
                 dpre[:, col : col + LANE] = slope.astype(BF16).astype(F32)
-            both = jnp.concatenate(halves, axis=1)
-            natural = dot(both, spread_rows(256, 256), ((1,), (1,)))
-            for e in range(8):
-                line = z * 32 + e * 4 + x
-                rows[line : line + 1, :] = natural[e : e + 1, :]
-    result[...] = rows[...].astype(BF16)
 
     for z in range(2):
         cols[z * LANE + 72 : (z + 1) * LANE, :] = jnp.zeros((LANE - 72, PLANE), F32)
@@ -145,17 +145,36 @@
                         row = z * LANE + (tx * 3 + ty + 1) * 8
                         col = column(0, x, parity)
                         cols[row : row + 8, col : col + LANE] = value
-    moved = cols[...].astype(BF16)
-    lower, upper = moved[:LANE], moved[LANE:]
-    for rows_of, out in ((slice(0, 64), own), (slice(64, 128), share)):
-        out[:, :PLANE] = dot(turned[rows_of, 2 * LANE :], lower).astype(BF16)
-        out[:, PLANE : 2 * PLANE] = dot(turned[rows_of, LANE:], moved).astype(BF16)
-        out[:, 2 * PLANE : 3 * PLANE] = dot(turned[rows_of, : 2 * LANE], moved).astype(BF16)
-        out[:, 3 * PLANE :] = dot(turned[rows_of, :LANE], upper).astype(BF16)
+    moved[...] = cols[...].astype(BF16)
+    channel_sums(turned, moved, slice(64, 128), share)
+
+
+def channel_sums(turned, moved, rows, out):
+    out[:, :PLANE] = dot(turned[rows, 2 * LANE :], moved[:LANE]).astype(BF16)
+    out[:, PLANE : 2 * PLANE] = dot(turned[rows, LANE:], moved[...]).astype(BF16)
+    out[:, 2 * PLANE : 3 * PLANE] = dot(turned[rows, : 2 * LANE], moved[...]).astype(BF16)
+    out[:, 3 * PLANE :] = dot(turned[rows, :LANE], moved[LANE:]).astype(BF16)
+
+
+def mix_back_kernel(near, across, turned, active, dpre, moved, own, raw, result, rows):
+    channel_sums(turned, moved, slice(0, 64), own)
+    for z in range(2):
+        for x in range(4):
+            col = z * PLANE + x * 256
+            both = active[:, col : col + 256].astype(BF16)
+            natural = dot(both, spread_rows(256, 256), ((1,), (1,)))
+            for e in range(8):
+                line = z * 32 + e * 4 + x
+                rows[line : line + 1, :] = natural[e : e + 1, :]
+    for z in range(2):
+        for e in range(8):
+            line = z * 32 + e * 4
+            result[z, e] = rows[line : line + 4, :].astype(BF16)
     for tz in range(3):
-        one = dot(lower, hidden[:, tz * PLANE : (tz + 1) * PLANE], ((1,), (1,)))
-        two = dot(upper, hidden[:, (tz + 1) * PLANE : (tz + 2) * PLANE], ((1,), (1,)))
-        raw[tz * 72 : (tz + 1) * 72, :] = (one + two)[:72]
+        for block, columns in ((near, slice(0, 64)), (across, slice(64, 128))):
+            one = dot(moved[:LANE], block[:, tz * PLANE : (tz + 1) * PLANE], ((1,), (1,)))
+            two = dot(moved[LANE:], block[:, (tz + 1) * PLANE : (tz + 2) * PLANE], ((1,), (1,)))
+            raw[tz * 72 : (tz + 1) * 72, columns] = (one + two)[:72]
     total = jnp.sum(dpre[...], axis=1, keepdims=True)
     raw[216:224, :] = jnp.broadcast_to(total, (8, LANE))
     raw[224:256, :] = jnp.zeros((32, LANE), F32)
@@ -221,6 +240,14 @@
     out[...] = total.astype(out.dtype)
 
 
+def plane_kernel(parts, out):
+    total = parts[0].astype(F32)
+    for i in range(1, parts.shape[0]):
+        total = total + parts[i].astype(F32)
+    out[:, 0, :] = total[:, :LANE].astype(BF16)
+    out[:, 1, :] = total[:, LANE:].astype(BF16)
+
+
 def pair_kernel(one, other, out):
     total = (one[...].astype(F32) + other[...].astype(F32)).astype(BF16)
     out[...] = jnp.broadcast_to(total, out.shape)
@@ -261,12 +288,11 @@
     return lax.ppermute(value, "filt", [(i, i ^ 1) for i in range(count)])
 
 
-def pair_gather(value):
+def pair_gather(copies):
     slabs, blocks = lax.axis_size("space"), lax.axis_size("filt")
     groups = [
         [s * blocks + f for s in (low, low + 1) for f in range(blocks)] for low in range(0, slabs, 2)
     ]
-    copies = jnp.broadcast_to(value[None], (2 * blocks,) + value.shape)
     return lax.all_to_all(copies, ("space", "filt"), 0, 0, axis_index_groups=groups, tiled=True)
 
 
@@ -313,35 +339,46 @@
     second_turned = jnp.pad(second_turned, ((0, 0), (0, 0), (0, 56))).reshape(LANE, 384)
     order = by_core(jnp.eye(LANE, dtype=BF16), core).T
 
-    pair = pair_gather(volume.reshape(16, 256)).reshape(2, 256, 256)
-    outer = outer_plane(lax.dynamic_index_in_dim(pair, odd, 0, keepdims=False))
+    copies = vmem_call(copies_kernel, struct((32, 16, 256), BF16))(volume.reshape(16, 2, LANE))
+    pair = pair_gather(copies).reshape(2, 256, 256)
     cot = vmem_call(
         split_kernel, struct((8, 2 * PLANE), F32), [pltpu.VMEM((64, 256), F32)]
     )(cotangent.reshape(64, 256))
+    ready = (first_rows, first_turned, second_rows, second_turned, order)
+    ready += (wide(first_bias), wide(second_bias), cot)
+    pair, ready = lax.optimization_barrier((pair, ready))
+    first_rows, first_turned, second_rows, second_turned, order = ready[:5]
+    first_wide, second_wide, cot = ready[5:]
+    outer = outer_plane(lax.dynamic_index_in_dim(pair, odd, 0, keepdims=False))
     whole = pl.BlockSpec(memory_space=pltpu.VMEM)
     source, hidden = vmem_call(
         hidden_kernel,
         (struct((256, 768), BF16), struct((8, 8, 4 * PLANE), BF16)),
         [pltpu.VMEM((512, 768), F32)],
         [pl.BlockSpec(memory_space=pltpu.SMEM)] + [whole] * 4,
-    )(odd.reshape(1), first_rows, pair.reshape(512, 256), outer, wide(first_bias))
+    )(odd.reshape(1), first_rows, pair.reshape(512, 256), outer, first_wide)
     hidden = chip_exchange(hidden).reshape(64, 4 * PLANE)
 
-    result, own, share, raw_second = vmem_call(
+    across = other_core(hidden)
+    active, share, dpre, moved = vmem_call(
         activate_kernel,
         (
-            struct((64, 256), BF16),
+            struct((8, 2 * PLANE), F32),
             struct((64, 4 * PLANE), BF16),
+            struct((8, 2 * PLANE), F32),
+            struct((256, PLANE), BF16),
+        ),
+        [pltpu.VMEM((224, 4 * PLANE), F32), pltpu.VMEM((256, PLANE), F32)],
+    )(hidden, across, second_rows, second_wide, cot, second_turned)
+    own, raw_second, result = vmem_call(
+        mix_back_kernel,
+        (
             struct((64, 4 * PLANE), BF16),
             struct((256, LANE), F32),
+            struct((2, 8, 4, 256), BF16),
         ),
-        [
-            pltpu.VMEM((224, 4 * PLANE), F32),
-            pltpu.VMEM((64, 256), F32),
-            pltpu.VMEM((8, 2 * PLANE), F32),
-            pltpu.VMEM((256, PLANE), F32),
-        ],
-    )(hidden, other_core(hidden), second_rows, wide(second_bias), cot, second_turned)
+        [pltpu.VMEM((64, 256), F32)],
+    )(hidden, across, second_turned, active, dpre, moved)
     share = vmem_call(pair_kernel, struct((64, 4 * PLANE), BF16))(own, other_core(share))
     parts = chip_exchange(share.reshape(8, 8, 4 * PLANE))
 
@@ -359,19 +396,19 @@
     high_other = shifted(low, -1)
     message = near_exchange(message)
     message, low_other, high_other = lax.optimization_barrier((message, low_other, high_other))
-    mine = vmem_call(sum_kernel, struct((160, LANE), BF16))(message)
-    other = partner(mine, 0)
     share = vmem_call(
         lift_input_kernel, struct((256, 256), BF16), [pltpu.VMEM((512, 256), F32)]
     )(low, low_other, high, high_other, first_turned)
-    mine = vmem_call(pair_kernel, struct((160, LANE), BF16))(mine, other)
-    mine, share = lax.optimization_barrier((mine, share))
-    other = partner(mine, 1)
+    mine = vmem_call(sum_kernel, struct((160, LANE), BF16))(message)
+    share, mine = lax.optimization_barrier((share, mine))
+    other = partner(mine, 0)
     share = lax.all_to_all(share.reshape(16, 16, 256), "filt", 0, 0, tiled=True)
     other, share = lax.optimization_barrier((other, share))
+    mine = vmem_call(pair_kernel, struct((160, LANE), BF16))(mine, other)
+    other = partner(mine, 1)
     message = vmem_call(pair_kernel, struct((NEAR, 160, LANE), BF16))(mine, other)
     message = near_exchange(message)
-    grad_volume = vmem_call(sum_kernel, struct((16, 256), BF16))(share)
+    grad_volume = vmem_call(plane_kernel, struct((16, 2, LANE), BF16))(share)
 
     total_cells = volume.shape[0] * lax.axis_size("space") * 8 * volume.shape[2] * volume.shape[3]
     scale = 1.0 / math.sqrt(total_cells)
@@ -383,10 +420,10 @@
             struct((1, 8), F32),
             struct((1, 8), F32),
         ),
-        [pltpu.VMEM((512, LANE), F32), pltpu.VMEM((512, LANE), F32), pltpu.VMEM((256, LANE), F32)],
+        [pltpu.VMEM((520, LANE), F32), pltpu.VMEM((520, LANE), F32), pltpu.VMEM((256, LANE), F32)],
     )(message, order)
     return (
-        result.reshape(2, 8, 4, 256),
+        result,
         grad_volume.reshape(1, 16, 2, 128),
         first,
         sum_first.reshape(8),

time: 136 us -> 134 us (0.985)
  starting transfers between devices: 57.3 us -> 51.3 us
  waiting for transfers between devices: 35.2 us -> 38.8 us
  Pallas kernels: 6.66 us -> 9.24 us
  local copies, waits for them, and re-layouts: 5.81 us -> 3.43 us
    ppermute x2, waiting for transfers between devices: 6.65 us -> 13 us  [partner(): return lax.ppermute(value, 'space', pairs)]
    ppermute x2, starting transfers between devices: 12.7 us -> 7.82 us  [partner(): return lax.ppermute(value, 'space', pairs)]
    all_to_all x1, waiting for transfers between devices: 7.23 us -> 4.41 us  [pair_gather(): lax.all_to_all(copies, ('space', 'filt'), 0, 0, axis_index_groups=groups,...]
    pallas_call x2 -> x4, Pallas kernels: 1.88 us -> 4.46 us  [the longest x1 1.97 us: per_device(): vmem_call(mix_back_kernel, (struct((64, 4 * PLANE), BF16), struct((256, L...]
    all_to_all x2, starting transfers between devices: 17.2 us -> 15.1 us  [near_exchange(): lax.all_to_all(value, 'space', 0, 0, axis_index_groups=groups, tiled=True)]
    reshape x4 -> x0, local copies, waits for them, and re-layouts: 1.5 us -> none  [the longest x1 0.63 us: per_device(): result.reshape(2, 8, 4, 256)]
    unnamed x13 -> x14, local copies, waits for them, and re-layouts: 2.88 us -> 2.46 us
  transfers between devices with their start and end apart: 11 -> 11, of which waited for: 8 -> 8; matrix products, arithmetic and copies ran while one was open for 2% -> 1% of each run, Pallas kernels for 1% -> 2%
where the time goes in v5:
time: 134 us; the launch traced here: 133 us
  starting transfers between devices  51.3 us (38%)
  waiting for transfers between devices  38.8 us (29%)
  blocking collectives  28.9 us (22%)
  Pallas kernels  9.24 us (7%)
  local copies, waits for them, and re-layouts  3.43 us (3%)
    all_to_all x2, blocking collectives, chip_exchange(): lax.all_to_all(value, 'filt', 0, 0, axis_index_groups=groups, tiled=True)  28.9 us
    all_to_all x2, starting transfers between devices, near_exchange(): lax.all_to_all(value, 'space', 0, 0, axis_index_groups=groups, tiled=True)  15.1 us
    ppermute x2, waiting for transfers between devices, partner(): return lax.ppermute(value, 'space', pairs)  13 us
    all_to_all x1, starting transfers between devices, pair_gather(): lax.all_to_all(copies, ('space', 'filt'), 0, 0, axis_index_groups=groups,...  9.41 us
    ppermute x2, starting transfers between devices, partner(): return lax.ppermute(value, 'space', pairs)  7.82 us
    all_to_all x2, waiting for transfers between devices, near_exchange(): lax.all_to_all(value, 'space', 0, 0, axis_index_groups=groups, tiled=True)  7.43 us
    ppermute x2, starting transfers between devices, shifted(): lax.ppermute(value, 'space', [(i, (i + step) % count) for i in range(coun...  6.73 us
    ppermute x1, waiting for transfers between devices, outer_plane(): return lax.ppermute(value, 'space', pairs)  6.38 us
  transfers between devices with their start and end apart: 11, of which 8 were waited for; matrix products, arithmetic and copies ran while one was open for 1% of the time, Pallas kernels for 2%

profile of v5, /device:TPU:24, one launch (start us, length us, event | category | flops | bytes accessed | tf_op | source)
XLA Modules:
  0.0 132.8 jit_solution(14201594838761771671)
XLA Ops:
  0.6 0.0 copy-start
  0.6 0.7 copy-done
  1.3 0.7 shard_map.109
  2.1 0.0 copy-start.2
  2.1 9.4 %all-to-all-start = ((bf16[32,16,256]{2,1,0:T(8,128)(2,1)}), bf16[32,16,256]{2,1,0:T(8,128)(2,1)S(1)}, u32[]{:S(2)}, u32[]{:S(2)}) async-start(bf16[32,16,256]{2,1,0:T(8,128)(2,1)} %shard_map.109), calls=%async_computation | async-start | bytes 524288 | tf_op jit(solution)/shard_map/all_to_all | solution.py:296
  11.5 0.0 copy-done.2
  11.5 0.2 copy.18
  11.7 0.1 fusion
  11.8 0.0 copy-start.3
  11.8 0.1 fusion.1
  11.9 0.6 copy-done.3
  12.6 0.2 shard_map.110.cot
  12.9 0.2 copy.21
  13.0 0.0 copy-start.1
  13.0 0.2 copy.20
  13.2 0.8 copy-done.1
  14.0 0.1 copy.27
  14.1 0.2 copy.28
  14.3 0.0 copy-start.4
  14.3 0.0 copy-start.5
  14.3 4.4 %all-to-all-done = bf16[32,16,256]{2,1,0:T(8,128)(2,1)S(1)} async-done(((bf16[32,16,256]{2,1,0:T(8,128)(2,1)}), bf16[32,16,256]{2,1,0:T(8,128)(2,1)S(1)}, u32[]{:S(2)}, u32[]{:S(2)}) %all-to-all-start) | async-done | bytes 262176 | tf_op jit(solution)/shard_map/all_to_all | solution.py:296
  18.7 0.0 copy-done.4
  18.7 0.1 broadcast_in_dim.4.bias
  18.8 0.0 copy-done.5
  18.8 0.1 broadcast_in_dim.5.bias
  18.9 1.9 %collective-permute-start = (bf16[256,256]{1,0:T(8,128)(2,1)S(1)}, bf16[256,256]{1,0:T(8,128)(2,1)S(1)}, u32[]{:S(2)}, u32[]{:S(2)}) collective-permute-start(bf16[256,256]{1,0:T(8,128)(2,1)S(1)} %dynamic-slice_bitcast_fusion), channel_id=1, source_target_pairs={{0,496},{16,32},{32,16},{48,64},{64,48},{80,96},{96,80},{112,128},... | collective-permute-start | bytes 393224 | tf_op jit(solution)/shard_map/ppermute | solution.py:302
  20.8 6.4 %collective-permute-done.outer = bf16[256,256]{1,0:T(8,128)(2,1)S(1)} collective-permute-done((bf16[256,256]{1,0:T(8,128)(2,1)S(1)}, bf16[256,256]{1,0:T(8,128)(2,1)S(1)}, u32[]{:S(2)}, u32[]{:S(2)}) %collective-permute-start) | collective-permute-done | bytes 131104 | tf_op jit(solution)/shard_map/ppermute | solution.py:302
  27.2 0.5 shard_map.111
  27.7 14.1 %all_to_all.30 = bf16[8,8,4096]{2,1,0:T(8,128)(2,1)S(1)} all-to-all(bf16[8,8,4096]{2,1,0:T(8,128)(2,1)S(1)} %get-tuple-element.41), channel_id=1, replica_groups={{0,2,4,6,8,10,12,14},{1,3,5,7,9,11,13,15},{16,18,20,22,24,26,28,30},{17..., dimensions={0} | all-to-all | bytes 1048576 | tf_op jit(solution)/shard_map/all_to_all | solution.py:283
  41.7 1.9 %collective-permute-start.1 = (bf16[64,4096]{1,0:T(8,128)(2,1)S(1)}, bf16[64,4096]{1,0:T(8,128)(2,1)S(1)}, u32[]{:S(2)}, u32[]{:S(2)}) collective-permute-start(bf16[64,4096]{1,0:T(8,128)(2,1)S(1)} %bitcast.40), channel_id=1, source_target_pairs={{0,1},{1,0},{2,3},{3,2},{4,5},{5,4},{6,7},{7,6},{8,9},{9,8},{10,11... | collective-permute-start | bytes 1572872 | tf_op jit(solution)/shard_map/ppermute | solution.py:288
  43.7 0.1 copy.23.turned
  43.8 1.7 %collective-permute-done.1.across = bf16[64,4096]{1,0:T(8,128)(2,1)S(1)} collective-permute-done((bf16[64,4096]{1,0:T(8,128)(2,1)S(1)}, bf16[64,4096]{1,0:T(8,128)(2,1)S(1)}, u32[]{:S(2)}, u32[]{:S(2)}) %collective-permute-start.1) | collective-permute-done | bytes 524320 | tf_op jit(solution)/shard_map/ppermute | solution.py:288
  45.5 1.1 shard_map.112
  46.7 2.0 %collective-permute-start.2 = (bf16[64,4096]{1,0:T(8,128)(2,1)S(1)}, bf16[64,4096]{1,0:T(8,128)(2,1)S(1)}, u32[]{:S(2)}, u32[]{:S(2)}) collective-permute-start(bf16[64,4096]{1,0:T(8,128)(2,1)S(1)} %get-tuple-element.51), channel_id=1, source_target_pairs={{0,1},{1,0},{2,3},{3,2},{4,5},{5,4},{6,7},{7,6},{8,9},{9,8},{10,11... | collective-permute-start | bytes 1572872 | tf_op jit(solution)/shard_map/ppermute | solution.py:288
  48.7 2.0 %shard_map.113 = (bf16[64,4096]{1,0:T(8,128)(2,1)S(1)}, f32[256,128]{1,0:T(8,128)S(1)}, bf16[2,8,4,256]{3,2,1,0:T(4,128)(2,1)}) custom-call(bf16[64,4096]{1,0:T(8,128)(2,1)S(1)} %bitcast.42, bf16[64,4096]{1,0:T(8,128)(2,1)S(1)} %collective-permute-done.1.across, bf16[128,384]{1,0:T(8,128)(2,1)S(1)} %copy.23.turned, f32[8,2048]{1,0:T(8,128)S(1)} %get-tuple-element.46.active, ...), custom_call_target="tpu_custom_call" | custom-call | tf_op jit(solution)/shard_map/pallas_call | solution.py:373
  50.7 0.0 collective-permute-done.2.other
  50.7 0.1 shard_map.114
  50.8 14.8 %all_to_all.31.parts = bf16[8,8,4096]{2,1,0:T(8,128)(2,1)S(1)} all-to-all(bf16[8,8,4096]{2,1,0:T(8,128)(2,1)S(1)} %bitcast.43), channel_id=1, replica_groups={{0,2,4,6,8,10,12,14},{1,3,5,7,9,11,13,15},{16,18,20,22,24,26,28,30},{17..., dimensions={0} | all-to-all | bytes 1048576 | tf_op jit(solution)/shard_map/all_to_all | solution.py:283
  65.6 1.2 shard_map.115
  66.8 9.6 %all-to-all-start.3 = ((bf16[8,160,128]{2,1,0:T(8,128)(2,1)}), bf16[8,160,128]{2,1,0:T(8,128)(2,1)S(1)}, u32[]{:S(2)}, u32[]{:S(2)}) async-start(bf16[8,160,128]{2,1,0:T(8,128)(2,1)} %get-tuple-element.55), calls=%async_computation.3 | async-start | bytes 655360 | tf_op jit(solution)/shard_map/all_to_all | solution.py:325
  76.4 2.0 %collective-permute-start.4 = (f32[8,2048]{1,0:T(8,128)S(1)}, f32[8,2048]{1,0:T(8,128)S(1)}, u32[]{:S(2)}, u32[]{:S(2)}) collective-permute-start(f32[8,2048]{1,0:T(8,128)S(1)} %get-tuple-element.54.low), channel_id=1, source_target_pairs={{0,496},{16,0},{32,16},{48,32},{64,48},{80,64},{96,80},{112,96},{1... | collective-permute-start | bytes 196616 | tf_op jit(solution)/shard_map/ppermute | solution.py:277
  78.4 4.7 %collective-permute-start.3 = (f32[8,2048]{1,0:T(8,128)S(1)}, f32[8,2048]{1,0:T(8,128)S(1)}, u32[]{:S(2)}, u32[]{:S(2)}) collective-permute-start(f32[8,2048]{1,0:T(8,128)S(1)} %get-tuple-element.56.high), channel_id=1, source_target_pairs={{0,16},{16,32},{32,48},{48,64},{64,80},{80,96},{96,112},{112,128},... | collective-permute-start | bytes 196616 | tf_op jit(solution)/shard_map/ppermute | solution.py:277
  83.2 0.1 copy.24.weight
  83.3 0.8 collective-permute-done.4.high_other
  84.1 5.0 %collective-permute-done.3.low_other = f32[8,2048]{1,0:T(8,128)S(1)} collective-permute-done((f32[8,2048]{1,0:T(8,128)S(1)}, f32[8,2048]{1,0:T(8,128)S(1)}, u32[]{:S(2)}, u32[]{:S(2)}) %collective-permute-start.3) | collective-permute-done | bytes 65568 | tf_op jit(solution)/shard_map/ppermute | solution.py:277
  89.1 0.0 all-to-all-done.3.parts
  89.2 1.0 shard_map.116
  90.2 6.3 %all-to-all-start.4 = ((bf16[16,16,256]{2,1,0:T(8,128)(2,1)}), bf16[16,16,256]{2,1,0:T(8,128)(2,1)S(1)}, u32[]{:S(2)}, u32[]{:S(2)}) async-start(bf16[16,16,256]{2,1,0:T(8,128)(2,1)} %bitcast.22), calls=%async_computation.4 | async-start | bytes 262144 | tf_op jit(solution)/shard_map/all_to_all | solution.py:405
  96.5 3.6 %collective-permute-start.5 = (bf16[160,128]{1,0:T(8,128)(2,1)S(1)}, bf16[160,128]{1,0:T(8,128)(2,1)S(1)}, u32[]{:S(2)}, u32[]{:S(2)}) collective-permute-start(bf16[160,128]{1,0:T(8,128)(2,1)S(1)} %shard_map.117.one), channel_id=1, source_target_pairs={{0,128},{16,144},{32,160},{48,176},{64,192},{80,208},{96,224},{112... | collective-permute-start | bytes 122888 | tf_op jit(solution)/shard_map/ppermute | solution.py:319
  100.1 7.4 %collective-permute-done.5.other = bf16[160,128]{1,0:T(8,128)(2,1)S(1)} collective-permute-done((bf16[160,128]{1,0:T(8,128)(2,1)S(1)}, bf16[160,128]{1,0:T(8,128)(2,1)S(1)}, u32[]{:S(2)}, u32[]{:S(2)}) %collective-permute-start.5) | collective-permute-done | bytes 40992 | tf_op jit(solution)/shard_map/ppermute | solution.py:319
  107.6 0.0 all-to-all-done.4.parts
  107.6 4.2 %collective-permute-start.6 = (bf16[160,128]{1,0:T(8,128)(2,1)S(1)}, bf16[160,128]{1,0:T(8,128)(2,1)S(1)}, u32[]{:S(2)}, u32[]{:S(2)}) collective-permute-start(bf16[160,128]{1,0:T(8,128)(2,1)S(1)} %shard_map.119.one), channel_id=1, source_target_pairs={{0,384},{16,400},{32,416},{48,432},{64,448},{80,464},{96,480},{112... | collective-permute-start | bytes 122888 | tf_op jit(solution)/shard_map/ppermute | solution.py:319
  111.8 5.6 %collective-permute-done.6.other = bf16[160,128]{1,0:T(8,128)(2,1)S(1)} collective-permute-done((bf16[160,128]{1,0:T(8,128)(2,1)S(1)}, bf16[160,128]{1,0:T(8,128)(2,1)S(1)}, u32[]{:S(2)}, u32[]{:S(2)}) %collective-permute-start.6) | collective-permute-done | bytes 40992 | tf_op jit(solution)/shard_map/ppermute | solution.py:319
  117.4 0.7 shard_map.120
  118.1 5.6 %all-to-all-start.5 = ((bf16[8,160,128]{2,1,0:T(8,128)(2,1)}), bf16[8,160,128]{2,1,0:T(8,128)(2,1)S(1)}, u32[]{:S(2)}, u32[]{:S(2)}) async-start(bf16[8,160,128]{2,1,0:T(8,128)(2,1)} %shard_map.120), calls=%async_computation.5 | async-start | bytes 655360 | tf_op jit(solution)/shard_map/all_to_all | solution.py:325
  123.7 0.6 shard_map.118
  124.3 7.4 %all-to-all-done.5.refs_0_ = bf16[8,160,128]{2,1,0:T(8,128)(2,1)S(1)} async-done(((bf16[8,160,128]{2,1,0:T(8,128)(2,1)}), bf16[8,160,128]{2,1,0:T(8,128)(2,1)S(1)}, u32[]{:S(2)}, u32[]{:S(2)}) %all-to-all-start.5) | async-done | bytes 327712 | tf_op jit(solution)/shard_map/all_to_all | solution.py:325
  131.8 1.0 shard_map.121
  (10 shorter events, 0.2 us)
Async XLA Ops:
  0.6 0.7 copy-start
  2.1 9.5 %copy-start.2 = (bf16[8,27,128]{2,0,1:T(8,128)(2,1)S(1)}, bf16[8,27,128]{2,0,1:T(8,128)(2,1)}, u32[]{:S(2)}) copy-start(bf16[8,27,128]{2,0,1:T(8,128)(2,1)} %param.9) | copy-start | bytes 165892
  2.1 16.7 %all-to-all-start = ((bf16[32,16,256]{2,1,0:T(8,128)(2,1)}), bf16[32,16,256]{2,1,0:T(8,128)(2,1)S(1)}, u32[]{:S(2)}, u32[]{:S(2)}) async-start(bf16[32,16,256]{2,1,0:T(8,128)(2,1)} %shard_map.109), calls=%async_computation | async-start | bytes 524288 | tf_op jit(solution)/shard_map/all_to_all | solution.py:296
  11.8 0.8 copy-start.3
  13.0 1.0 copy-start.1
  14.3 4.5 %copy-start.4 = (bf16[8]{0:T(256)(128)(2,1)S(1)}, bf16[8]{0:T(256)(128)(2,1)}, u32[]{:S(2)}) copy-start(bf16[8]{0:T(256)(128)(2,1)} %param.8) | copy-start | bytes 52
  14.3 4.5 %copy-start.5 = (bf16[8]{0:T(256)(128)(2,1)S(1)}, bf16[8]{0:T(256)(128)(2,1)}, u32[]{:S(2)}) copy-start(bf16[8]{0:T(256)(128)(2,1)} %param.10) | copy-start | bytes 52
  18.9 8.3 %collective-permute-start = (bf16[256,256]{1,0:T(8,128)(2,1)S(1)}, bf16[256,256]{1,0:T(8,128)(2,1)S(1)}, u32[]{:S(2)}, u32[]{:S(2)}) collective-permute-start(bf16[256,256]{1,0:T(8,128)(2,1)S(1)} %dynamic-slice_bitcast_fusion), channel_id=1, source_target_pairs={{0,496},{16,32},{32,16},{48,64},{64,48},{80,96},{96,80},{112,128},... | collective-permute-start | bytes 393224 | tf_op jit(solution)/shard_map/ppermute | solution.py:302
  41.7 3.8 %collective-permute-start.1 = (bf16[64,4096]{1,0:T(8,128)(2,1)S(1)}, bf16[64,4096]{1,0:T(8,128)(2,1)S(1)}, u32[]{:S(2)}, u32[]{:S(2)}) collective-permute-start(bf16[64,4096]{1,0:T(8,128)(2,1)S(1)} %bitcast.40), channel_id=1, source_target_pairs={{0,1},{1,0},{2,3},{3,2},{4,5},{5,4},{6,7},{7,6},{8,9},{9,8},{10,11... | collective-permute-start | bytes 1572872 | tf_op jit(solution)/shard_map/ppermute | solution.py:288
  46.7 4.0 %collective-permute-start.2 = (bf16[64,4096]{1,0:T(8,128)(2,1)S(1)}, bf16[64,4096]{1,0:T(8,128)(2,1)S(1)}, u32[]{:S(2)}, u32[]{:S(2)}) collective-permute-start(bf16[64,4096]{1,0:T(8,128)(2,1)S(1)} %get-tuple-element.51), channel_id=1, source_target_pairs={{0,1},{1,0},{2,3},{3,2},{4,5},{5,4},{6,7},{7,6},{8,9},{9,8},{10,11... | collective-permute-start | bytes 1572872 | tf_op jit(solution)/shard_map/ppermute | solution.py:288
  66.8 22.3 %all-to-all-start.3 = ((bf16[8,160,128]{2,1,0:T(8,128)(2,1)}), bf16[8,160,128]{2,1,0:T(8,128)(2,1)S(1)}, u32[]{:S(2)}, u32[]{:S(2)}) async-start(bf16[8,160,128]{2,1,0:T(8,128)(2,1)} %get-tuple-element.55), calls=%async_computation.3 | async-start | bytes 655360 | tf_op jit(solution)/shard_map/all_to_all | solution.py:325
  76.4 7.7 %collective-permute-start.4 = (f32[8,2048]{1,0:T(8,128)S(1)}, f32[8,2048]{1,0:T(8,128)S(1)}, u32[]{:S(2)}, u32[]{:S(2)}) collective-permute-start(f32[8,2048]{1,0:T(8,128)S(1)} %get-tuple-element.54.low), channel_id=1, source_target_pairs={{0,496},{16,0},{32,16},{48,32},{64,48},{80,64},{96,80},{112,96},{1... | collective-permute-start | bytes 196616 | tf_op jit(solution)/shard_map/ppermute | solution.py:277
  78.4 10.7 %collective-permute-start.3 = (f32[8,2048]{1,0:T(8,128)S(1)}, f32[8,2048]{1,0:T(8,128)S(1)}, u32[]{:S(2)}, u32[]{:S(2)}) collective-permute-start(f32[8,2048]{1,0:T(8,128)S(1)} %get-tuple-element.56.high), channel_id=1, source_target_pairs={{0,16},{16,32},{32,48},{48,64},{64,80},{80,96},{96,112},{112,128},... | collective-permute-start | bytes 196616 | tf_op jit(solution)/shard_map/ppermute | solution.py:277
  90.2 17.4 %all-to-all-start.4 = ((bf16[16,16,256]{2,1,0:T(8,128)(2,1)}), bf16[16,16,256]{2,1,0:T(8,128)(2,1)S(1)}, u32[]{:S(2)}, u32[]{:S(2)}) async-start(bf16[16,16,256]{2,1,0:T(8,128)(2,1)} %bitcast.22), calls=%async_computation.4 | async-start | bytes 262144 | tf_op jit(solution)/shard_map/all_to_all | solution.py:405
  96.5 11.1 %collective-permute-start.5 = (bf16[160,128]{1,0:T(8,128)(2,1)S(1)}, bf16[160,128]{1,0:T(8,128)(2,1)S(1)}, u32[]{:S(2)}, u32[]{:S(2)}) collective-permute-start(bf16[160,128]{1,0:T(8,128)(2,1)S(1)} %shard_map.117.one), channel_id=1, source_target_pairs={{0,128},{16,144},{32,160},{48,176},{64,192},{80,208},{96,224},{112... | collective-permute-start | bytes 122888 | tf_op jit(solution)/shard_map/ppermute | solution.py:319
  107.6 9.8 %collective-permute-start.6 = (bf16[160,128]{1,0:T(8,128)(2,1)S(1)}, bf16[160,128]{1,0:T(8,128)(2,1)S(1)}, u32[]{:S(2)}, u32[]{:S(2)}) collective-permute-start(bf16[160,128]{1,0:T(8,128)(2,1)S(1)} %shard_map.119.one), channel_id=1, source_target_pairs={{0,384},{16,400},{32,416},{48,432},{64,448},{80,464},{96,480},{112... | collective-permute-start | bytes 122888 | tf_op jit(solution)/shard_map/ppermute | solution.py:319
  118.1 13.6 %all-to-all-start.5 = ((bf16[8,160,128]{2,1,0:T(8,128)(2,1)}), bf16[8,160,128]{2,1,0:T(8,128)(2,1)S(1)}, u32[]{:S(2)}, u32[]{:S(2)}) async-start(bf16[8,160,128]{2,1,0:T(8,128)(2,1)} %shard_map.120), calls=%async_computation.5 | async-start | bytes 655360 | tf_op jit(solution)/shard_map/all_to_all | solution.py:325

commit v6 on v5

--- a/solution.py
+++ b/solution.py
@@ -156,8 +156,7 @@
     out[:, 3 * PLANE :] = dot(turned[rows, :LANE], moved[LANE:]).astype(BF16)
 
 
-def mix_back_kernel(near, across, turned, active, dpre, moved, own, raw, result, rows):
-    channel_sums(turned, moved, slice(0, 64), own)
+def result_kernel(active, result, rows):
     for z in range(2):
         for x in range(4):
             col = z * PLANE + x * 256
@@ -170,6 +169,10 @@
         for e in range(8):
             line = z * 32 + e * 4
             result[z, e] = rows[line : line + 4, :].astype(BF16)
+
+
+def mix_back_kernel(near, across, turned, dpre, moved, own, raw):
+    channel_sums(turned, moved, slice(0, 64), own)
     for tz in range(3):
         for block, columns in ((near, slice(0, 64)), (across, slice(64, 128))):
             one = dot(moved[:LANE], block[:, tz * PLANE : (tz + 1) * PLANE], ((1,), (1,)))
@@ -197,8 +200,8 @@
     total = parts[0].astype(F32)
     for f in range(1, parts.shape[0]):
         total = total + parts[f].astype(F32)
-    low[...] = total[:, : 2 * PLANE]
-    high[...] = total[:, 2 * PLANE :]
+    low[...] = total[:, : 2 * PLANE].astype(BF16)
+    high[...] = total[:, 2 * PLANE :].astype(BF16)
     for plane in range(4):
         pick_columns(total[:, plane * PLANE : (plane + 1) * PLANE], cols, plane * LANE)
     pairs = (((0, 1), (2, 2)), ((1, 1), (3, 2)), ((0, 0), (2, 1)), ((1, 0), (3, 1)))
@@ -227,7 +230,7 @@
 
 def lift_input_kernel(low, low_other, high, high_other, weight, share, cols):
     for half, (one, other) in enumerate(((low, low_other), (high, high_other))):
-        total = (one[...] + other[...]).astype(BF16).astype(F32)
+        total = (one[...].astype(F32) + other[...].astype(F32)).astype(BF16).astype(F32)
         pick_columns(total[:, :PLANE], cols, 2 * half * LANE)
         pick_columns(total[:, PLANE:], cols, (2 * half + 1) * LANE)
     share[...] = dot(weight[...], cols[...].astype(BF16)).astype(BF16)
@@ -330,6 +333,11 @@
     wide = lambda bias: jnp.broadcast_to(bias.astype(F32)[:, None], (8, LANE))
     core = lax.axis_index("filt") % 2
     odd = lax.axis_index("space") % 2
+    copies = vmem_call(copies_kernel, struct((32, 16, 256), BF16))(volume.reshape(16, 2, LANE))
+    pair = pair_gather(copies).reshape(2, 256, 256)
+    given = (first_weight, wide(first_bias), second_weight, wide(second_bias), cotangent)
+    pair, given = lax.optimization_barrier((pair, given))
+    first_weight, first_wide, second_weight, second_wide, cotangent = given
     first_rows = first_weight.transpose(1, 0, 2).reshape(512, 256)
     first_turned = first_weight.transpose(2, 1, 0).reshape(256, 512)
     second = by_core(second_weight, core)
@@ -338,18 +346,13 @@
     second_turned = second.transpose(2, 1, 0).reshape(LANE, 3, 72)[:, ::-1]
     second_turned = jnp.pad(second_turned, ((0, 0), (0, 0), (0, 56))).reshape(LANE, 384)
     order = by_core(jnp.eye(LANE, dtype=BF16), core).T
-
-    copies = vmem_call(copies_kernel, struct((32, 16, 256), BF16))(volume.reshape(16, 2, LANE))
-    pair = pair_gather(copies).reshape(2, 256, 256)
     cot = vmem_call(
         split_kernel, struct((8, 2 * PLANE), F32), [pltpu.VMEM((64, 256), F32)]
     )(cotangent.reshape(64, 256))
-    ready = (first_rows, first_turned, second_rows, second_turned, order)
-    ready += (wide(first_bias), wide(second_bias), cot)
-    pair, ready = lax.optimization_barrier((pair, ready))
-    first_rows, first_turned, second_rows, second_turned, order = ready[:5]
-    first_wide, second_wide, cot = ready[5:]
     outer = outer_plane(lax.dynamic_index_in_dim(pair, odd, 0, keepdims=False))
+    ready = (first_rows, first_turned, second_rows, second_turned, order, cot)
+    outer, ready = lax.optimization_barrier((outer, ready))
+    first_rows, first_turned, second_rows, second_turned, order, cot = ready
     whole = pl.BlockSpec(memory_space=pltpu.VMEM)
     source, hidden = vmem_call(
         hidden_kernel,
@@ -370,23 +373,17 @@
         ),
         [pltpu.VMEM((224, 4 * PLANE), F32), pltpu.VMEM((256, PLANE), F32)],
     )(hidden, across, second_rows, second_wide, cot, second_turned)
-    own, raw_second, result = vmem_call(
-        mix_back_kernel,
-        (
-            struct((64, 4 * PLANE), BF16),
-            struct((256, LANE), F32),
-            struct((2, 8, 4, 256), BF16),
-        ),
-        [pltpu.VMEM((64, 256), F32)],
-    )(hidden, across, second_turned, active, dpre, moved)
+    own, raw_second = vmem_call(
+        mix_back_kernel, (struct((64, 4 * PLANE), BF16), struct((256, LANE), F32))
+    )(hidden, across, second_turned, dpre, moved)
     share = vmem_call(pair_kernel, struct((64, 4 * PLANE), BF16))(own, other_core(share))
     parts = chip_exchange(share.reshape(8, 8, 4 * PLANE))
 
     low, high, message = vmem_call(
         lift_back_kernel,
         (
-            struct((8, 2 * PLANE), F32),
-            struct((8, 2 * PLANE), F32),
+            struct((8, 2 * PLANE), BF16),
+            struct((8, 2 * PLANE), BF16),
             struct((NEAR, 160, LANE), BF16),
         ),
         [pltpu.VMEM((512, 256), F32), pltpu.VMEM((512, 256), F32), pltpu.VMEM((256, LANE), F32)],
@@ -395,7 +392,12 @@
     low_other = shifted(high, 1)
     high_other = shifted(low, -1)
     message = near_exchange(message)
-    message, low_other, high_other = lax.optimization_barrier((message, low_other, high_other))
+    result = vmem_call(
+        result_kernel, struct((2, 8, 4, 256), BF16), [pltpu.VMEM((64, 256), F32)]
+    )(active)
+    message, low_other, high_other, result = lax.optimization_barrier(
+        (message, low_other, high_other, result)
+    )
     share = vmem_call(
         lift_input_kernel, struct((256, 256), BF16), [pltpu.VMEM((512, 256), F32)]
     )(low, low_other, high, high_other, first_turned)
@@ -406,9 +408,10 @@
     other, share = lax.optimization_barrier((other, share))
     mine = vmem_call(pair_kernel, struct((160, LANE), BF16))(mine, other)
     other = partner(mine, 1)
+    grad_volume = vmem_call(plane_kernel, struct((16, 2, LANE), BF16))(share)
+    other, grad_volume = lax.optimization_barrier((other, grad_volume))
     message = vmem_call(pair_kernel, struct((NEAR, 160, LANE), BF16))(mine, other)
     message = near_exchange(message)
-    grad_volume = vmem_call(plane_kernel, struct((16, 2, LANE), BF16))(share)
 
     total_cells = volume.shape[0] * lax.axis_size("space") * 8 * volume.shape[2] * volume.shape[3]
     scale = 1.0 / math.sqrt(total_cells)

time: 134 us -> 131 us (0.978)
  blocking collectives: 28.9 us -> 41.7 us
  waiting for transfers between devices: 38.8 us -> 28.1 us
  starting transfers between devices: 51.3 us -> 47.6 us
    all_to_all x0 -> x1, blocking collectives: none -> 13.1 us  [near_exchange(): lax.all_to_all(value, 'space', 0, 0, axis_index_groups=groups, tiled=True)]
    all_to_all x2 -> x1, waiting for transfers between devices: 7.43 us -> 0.01 us  [near_exchange(): lax.all_to_all(value, 'space', 0, 0, axis_index_groups=groups, tiled=True)]
    all_to_all x2 -> x1, starting transfers between devices: 15.1 us -> 9.57 us  [near_exchange(): lax.all_to_all(value, 'space', 0, 0, axis_index_groups=groups, tiled=True)]
    all_to_all x1, waiting for transfers between devices: 4.41 us -> 7.08 us  [pair_gather(): lax.all_to_all(copies, ('space', 'filt'), 0, 0, axis_index_groups=groups,...]
    ppermute x2, waiting for transfers between devices: 13 us -> 10.7 us  [partner(): return lax.ppermute(value, 'space', pairs)]
    ppermute x2, waiting for transfers between devices: 5.83 us -> 3.52 us  [shifted(): lax.ppermute(value, 'space', [(i, (i + step) % count) for i in range(coun...]
    ppermute x2, starting transfers between devices: 7.82 us -> 10.1 us  [partner(): return lax.ppermute(value, 'space', pairs)]
    ppermute x1, waiting for transfers between devices: 6.38 us -> 4.59 us  [outer_plane(): return lax.ppermute(value, 'space', pairs)]
  transfers between devices with their start and end apart: 11 -> 10, of which waited for: 8 -> 7; matrix products, arithmetic and copies ran while one was open for 1% -> 1% of each run, Pallas kernels for 2% -> 2%
where the time goes in v6:
time: 131 us; the launch traced here: 130 us
  starting transfers between devices  47.6 us (36%)
  blocking collectives  41.7 us (32%)
  waiting for transfers between devices  28.1 us (21%)
  Pallas kernels  8.83 us (7%)
  local copies, waits for them, and re-layouts  2.8 us (2%)
    all_to_all x2, blocking collectives, chip_exchange(): lax.all_to_all(value, 'filt', 0, 0, axis_index_groups=groups, tiled=True)  28.6 us
    all_to_all x1, blocking collectives, near_exchange(): lax.all_to_all(value, 'space', 0, 0, axis_index_groups=groups, tiled=True)  13.1 us
    ppermute x2, waiting for transfers between devices, partner(): return lax.ppermute(value, 'space', pairs)  10.7 us
    ppermute x2, starting transfers between devices, partner(): return lax.ppermute(value, 'space', pairs)  10.1 us
    all_to_all x1, starting transfers between devices, near_exchange(): lax.all_to_all(value, 'space', 0, 0, axis_index_groups=groups, tiled=True)  9.57 us
    all_to_all x1, starting transfers between devices, pair_gather(): lax.all_to_all(copies, ('space', 'filt'), 0, 0, axis_index_groups=groups,...  9.28 us
    all_to_all x1, waiting for transfers between devices, pair_gather(): lax.all_to_all(copies, ('space', 'filt'), 0, 0, axis_index_groups=groups,...  7.08 us
    all_to_all x1, starting transfers between devices, per_device(): share = lax.all_to_all(share.reshape(16, 16, 256), 'filt', 0, 0, tiled=True)  6.93 us
  transfers between devices with their start and end apart: 10, of which 7 were waited for; matrix products, arithmetic and copies ran while one was open for 1% of the time, Pallas kernels for 2%

profile of v6, /device:TPU:24, one launch (start us, length us, event | category | flops | bytes accessed | tf_op | source)
XLA Modules:
  0.0 130.1 jit_solution(3101141996131366077)
XLA Ops:
  0.6 0.0 copy-start
  0.6 0.7 copy-done
  1.3 0.7 shard_map.109
  2.1 9.3 %all-to-all-start = ((bf16[32,16,256]{2,1,0:T(8,128)(2,1)}), bf16[32,16,256]{2,1,0:T(8,128)(2,1)S(1)}, u32[]{:S(2)}, u32[]{:S(2)}) async-start(bf16[32,16,256]{2,1,0:T(8,128)(2,1)} %shard_map.109), calls=%async_computation | async-start | bytes 524288 | tf_op jit(solution)/shard_map/all_to_all | solution.py:299
  11.4 0.1 fusion.1
  11.5 0.0 copy-start.4
  11.5 0.0 copy-start.3
  11.5 0.0 copy-start.5
  11.5 7.1 %all-to-all-done = bf16[32,16,256]{2,1,0:T(8,128)(2,1)S(1)} async-done(((bf16[32,16,256]{2,1,0:T(8,128)(2,1)}), bf16[32,16,256]{2,1,0:T(8,128)(2,1)S(1)}, u32[]{:S(2)}, u32[]{:S(2)}) %all-to-all-start) | async-done | bytes 262176 | tf_op jit(solution)/shard_map/all_to_all | solution.py:299
  18.6 0.0 copy-done.4
  18.6 0.1 broadcast_in_dim.4.bias
  18.7 0.0 copy-done.5
  18.7 0.1 broadcast_in_dim.5.bias
  18.8 0.0 copy-done.3
  18.8 0.2 shard_map.110.cot
  19.0 0.0 copy-start.2
  19.0 1.9 %collective-permute-start = (bf16[256,256]{1,0:T(8,128)(2,1)S(1)}, bf16[256,256]{1,0:T(8,128)(2,1)S(1)}, u32[]{:S(2)}, u32[]{:S(2)}) collective-permute-start(bf16[256,256]{1,0:T(8,128)(2,1)S(1)} %dynamic-slice_bitcast_fusion), channel_id=1, source_target_pairs={{0,496},{16,32},{32,16},{48,64},{64,48},{80,96},{96,80},{112,128},... | collective-permute-start | bytes 393224 | tf_op jit(solution)/shard_map/ppermute | solution.py:305
  20.9 0.0 copy-done.2
  21.0 0.2 copy.18
  21.2 0.1 fusion
  21.3 0.2 copy.21
  21.5 0.0 copy-start.1
  21.5 0.2 copy.20
  21.7 0.8 copy-done.1
  22.4 0.1 copy.27
  22.6 0.2 copy.28
  22.7 4.6 %collective-permute-done.outer = bf16[256,256]{1,0:T(8,128)(2,1)S(1)} collective-permute-done((bf16[256,256]{1,0:T(8,128)(2,1)S(1)}, bf16[256,256]{1,0:T(8,128)(2,1)S(1)}, u32[]{:S(2)}, u32[]{:S(2)}) %collective-permute-start) | collective-permute-done | bytes 131104 | tf_op jit(solution)/shard_map/ppermute | solution.py:305
  27.3 0.5 shard_map.111
  27.8 14.1 %all_to_all.30 = bf16[8,8,4096]{2,1,0:T(8,128)(2,1)S(1)} all-to-all(bf16[8,8,4096]{2,1,0:T(8,128)(2,1)S(1)} %get-tuple-element.51), channel_id=1, replica_groups={{0,2,4,6,8,10,12,14},{1,3,5,7,9,11,13,15},{16,18,20,22,24,26,28,30},{17..., dimensions={0} | all-to-all | bytes 1048576 | tf_op jit(solution)/shard_map/all_to_all | solution.py:286
  41.9 1.9 %collective-permute-start.1 = (bf16[64,4096]{1,0:T(8,128)(2,1)S(1)}, bf16[64,4096]{1,0:T(8,128)(2,1)S(1)}, u32[]{:S(2)}, u32[]{:S(2)}) collective-permute-start(bf16[64,4096]{1,0:T(8,128)(2,1)S(1)} %bitcast.40), channel_id=1, source_target_pairs={{0,1},{1,0},{2,3},{3,2},{4,5},{5,4},{6,7},{7,6},{8,9},{9,8},{10,11... | collective-permute-start | bytes 1572872 | tf_op jit(solution)/shard_map/ppermute | solution.py:291
  43.8 0.1 copy.23.turned
  43.9 1.7 %collective-permute-done.1.across = bf16[64,4096]{1,0:T(8,128)(2,1)S(1)} collective-permute-done((bf16[64,4096]{1,0:T(8,128)(2,1)S(1)}, bf16[64,4096]{1,0:T(8,128)(2,1)S(1)}, u32[]{:S(2)}, u32[]{:S(2)}) %collective-permute-start.1) | collective-permute-done | bytes 524320 | tf_op jit(solution)/shard_map/ppermute | solution.py:291
  45.7 1.1 shard_map.112
  46.8 2.0 %collective-permute-start.2 = (bf16[64,4096]{1,0:T(8,128)(2,1)S(1)}, bf16[64,4096]{1,0:T(8,128)(2,1)S(1)}, u32[]{:S(2)}, u32[]{:S(2)}) collective-permute-start(bf16[64,4096]{1,0:T(8,128)(2,1)S(1)} %get-tuple-element.59), channel_id=1, source_target_pairs={{0,1},{1,0},{2,3},{3,2},{4,5},{5,4},{6,7},{7,6},{8,9},{9,8},{10,11... | collective-permute-start | bytes 1572872 | tf_op jit(solution)/shard_map/ppermute | solution.py:291
  48.8 1.3 shard_map.113
  50.1 0.5 collective-permute-done.2.other
  50.6 0.1 shard_map.114
  50.7 14.6 %all_to_all.31.parts = bf16[8,8,4096]{2,1,0:T(8,128)(2,1)S(1)} all-to-all(bf16[8,8,4096]{2,1,0:T(8,128)(2,1)S(1)} %bitcast.43), channel_id=1, replica_groups={{0,2,4,6,8,10,12,14},{1,3,5,7,9,11,13,15},{16,18,20,22,24,26,28,30},{17..., dimensions={0} | all-to-all | bytes 1048576 | tf_op jit(solution)/shard_map/all_to_all | solution.py:286
  65.3 1.2 shard_map.115
  66.5 9.6 %all-to-all-start.3 = ((bf16[8,160,128]{2,1,0:T(8,128)(2,1)}), bf16[8,160,128]{2,1,0:T(8,128)(2,1)S(1)}, u32[]{:S(2)}, u32[]{:S(2)}) async-start(bf16[8,160,128]{2,1,0:T(8,128)(2,1)} %get-tuple-element.62), calls=%async_computation.3 | async-start | bytes 655360 | tf_op jit(solution)/shard_map/all_to_all | solution.py:328
  76.1 3.4 %collective-permute-start.3 = (bf16[8,2048]{1,0:T(8,128)(2,1)S(1)}, bf16[8,2048]{1,0:T(8,128)(2,1)S(1)}, u32[]{:S(2)}, u32[]{:S(2)}) collective-permute-start(bf16[8,2048]{1,0:T(8,128)(2,1)S(1)} %get-tuple-element.63.high), channel_id=1, source_target_pairs={{0,16},{16,32},{32,48},{48,64},{64,80},{80,96},{96,112},{112,128},... | collective-permute-start | bytes 98312 | tf_op jit(solution)/shard_map/ppermute | solution.py:280
  79.4 2.5 %collective-permute-start.4 = (bf16[8,2048]{1,0:T(8,128)(2,1)S(1)}, bf16[8,2048]{1,0:T(8,128)(2,1)S(1)}, u32[]{:S(2)}, u32[]{:S(2)}) collective-permute-start(bf16[8,2048]{1,0:T(8,128)(2,1)S(1)} %get-tuple-element.64.low), channel_id=1, source_target_pairs={{0,496},{16,0},{32,16},{48,32},{64,48},{80,64},{96,80},{112,96},{1... | collective-permute-start | bytes 98312 | tf_op jit(solution)/shard_map/ppermute | solution.py:280
  81.9 0.1 copy.24.weight
  82.1 1.0 shard_map.116
  83.1 0.0 collective-permute-done.3.low_other
  83.1 3.5 %collective-permute-done.4.high_other = bf16[8,2048]{1,0:T(8,128)(2,1)S(1)} collective-permute-done((bf16[8,2048]{1,0:T(8,128)(2,1)S(1)}, bf16[8,2048]{1,0:T(8,128)(2,1)S(1)}, u32[]{:S(2)}, u32[]{:S(2)}) %collective-permute-start.4) | collective-permute-done | bytes 32800 | tf_op jit(solution)/shard_map/ppermute | solution.py:280
  86.6 0.0 all-to-all-done.3.parts
  86.7 1.0 shard_map.117
  87.6 6.9 %all-to-all-start.4 = ((bf16[16,16,256]{2,1,0:T(8,128)(2,1)}), bf16[16,16,256]{2,1,0:T(8,128)(2,1)S(1)}, u32[]{:S(2)}, u32[]{:S(2)}) async-start(bf16[16,16,256]{2,1,0:T(8,128)(2,1)} %bitcast.22), calls=%async_computation.4 | async-start | bytes 262144 | tf_op jit(solution)/shard_map/all_to_all | solution.py:407
  94.6 5.3 %collective-permute-start.5 = (bf16[160,128]{1,0:T(8,128)(2,1)S(1)}, bf16[160,128]{1,0:T(8,128)(2,1)S(1)}, u32[]{:S(2)}, u32[]{:S(2)}) collective-permute-start(bf16[160,128]{1,0:T(8,128)(2,1)S(1)} %shard_map.118.one), channel_id=1, source_target_pairs={{0,128},{16,144},{32,160},{48,176},{64,192},{80,208},{96,224},{112... | collective-permute-start | bytes 122888 | tf_op jit(solution)/shard_map/ppermute | solution.py:322
  99.9 6.3 %collective-permute-done.5.other = bf16[160,128]{1,0:T(8,128)(2,1)S(1)} collective-permute-done((bf16[160,128]{1,0:T(8,128)(2,1)S(1)}, bf16[160,128]{1,0:T(8,128)(2,1)S(1)}, u32[]{:S(2)}, u32[]{:S(2)}) %collective-permute-start.5) | collective-permute-done | bytes 40992 | tf_op jit(solution)/shard_map/ppermute | solution.py:322
  106.2 0.0 all-to-all-done.4.parts
  106.2 4.7 %collective-permute-start.6 = (bf16[160,128]{1,0:T(8,128)(2,1)S(1)}, bf16[160,128]{1,0:T(8,128)(2,1)S(1)}, u32[]{:S(2)}, u32[]{:S(2)}) collective-permute-start(bf16[160,128]{1,0:T(8,128)(2,1)S(1)} %shard_map.119.one), channel_id=1, source_target_pairs={{0,384},{16,400},{32,416},{48,432},{64,448},{80,464},{96,480},{112... | collective-permute-start | bytes 122888 | tf_op jit(solution)/shard_map/ppermute | solution.py:322
  111.0 0.6 shard_map.120
  111.6 4.4 %collective-permute-done.6.other = bf16[160,128]{1,0:T(8,128)(2,1)S(1)} collective-permute-done((bf16[160,128]{1,0:T(8,128)(2,1)S(1)}, bf16[160,128]{1,0:T(8,128)(2,1)S(1)}, u32[]{:S(2)}, u32[]{:S(2)}) %collective-permute-start.6) | collective-permute-done | bytes 40992 | tf_op jit(solution)/shard_map/ppermute | solution.py:322
  116.0 13.1 %all_to_all.32.refs_0_ = bf16[8,160,128]{2,1,0:T(8,128)(2,1)S(1)} all-to-all(bf16[8,160,128]{2,1,0:T(8,128)(2,1)S(1)} %shard_map.121), channel_id=1, replica_groups={{0,16,32,48,64,80,96,112},{128,144,160,176,192,208,224,240},{256,272,28..., dimensions={0} | all-to-all | bytes 655360 | tf_op jit(solution)/shard_map/all_to_all | solution.py:328
  129.1 1.0 shard_map.122
  (11 shorter events, 0.2 us)
Async XLA Ops:
  0.6 0.7 copy-start
  2.1 16.5 %all-to-all-start = ((bf16[32,16,256]{2,1,0:T(8,128)(2,1)}), bf16[32,16,256]{2,1,0:T(8,128)(2,1)S(1)}, u32[]{:S(2)}, u32[]{:S(2)}) async-start(bf16[32,16,256]{2,1,0:T(8,128)(2,1)} %shard_map.109), calls=%async_computation | async-start | bytes 524288 | tf_op jit(solution)/shard_map/all_to_all | solution.py:299
  11.5 7.1 %copy-start.4 = (bf16[8]{0:T(256)(128)(2,1)S(1)}, bf16[8]{0:T(256)(128)(2,1)}, u32[]{:S(2)}) copy-start(bf16[8]{0:T(256)(128)(2,1)} %param.8) | copy-start | bytes 52
  11.5 7.3 %copy-start.3 = (bf16[2,8,4,256]{3,2,1,0:T(4,128)(2,1)S(1)}, bf16[2,8,4,256]{3,2,1,0:T(4,128)(2,1)}, u32[]{:S(2)}) copy-start(bf16[2,8,4,256]{3,2,1,0:T(4,128)(2,1)} %param.11) | copy-start | bytes 98308
  11.5 7.2 %copy-start.5 = (bf16[8]{0:T(256)(128)(2,1)S(1)}, bf16[8]{0:T(256)(128)(2,1)}, u32[]{:S(2)}) copy-start(bf16[8]{0:T(256)(128)(2,1)} %param.10) | copy-start | bytes 52
  19.0 2.0 %copy-start.2 = (bf16[8,27,128]{2,0,1:T(8,128)(2,1)S(1)}, bf16[8,27,128]{2,0,1:T(8,128)(2,1)}, u32[]{:S(2)}) copy-start(bf16[8,27,128]{2,0,1:T(8,128)(2,1)} %param.9) | copy-start | bytes 165892
  19.0 8.3 %collective-permute-start = (bf16[256,256]{1,0:T(8,128)(2,1)S(1)}, bf16[256,256]{1,0:T(8,128)(2,1)S(1)}, u32[]{:S(2)}, u32[]{:S(2)}) collective-permute-start(bf16[256,256]{1,0:T(8,128)(2,1)S(1)} %dynamic-slice_bitcast_fusion), channel_id=1, source_target_pairs={{0,496},{16,32},{32,16},{48,64},{64,48},{80,96},{96,80},{112,128},... | collective-permute-start | bytes 393224 | tf_op jit(solution)/shard_map/ppermute | solution.py:305
  21.5 1.0 copy-start.1
  41.9 3.8 %collective-permute-start.1 = (bf16[64,4096]{1,0:T(8,128)(2,1)S(1)}, bf16[64,4096]{1,0:T(8,128)(2,1)S(1)}, u32[]{:S(2)}, u32[]{:S(2)}) collective-permute-start(bf16[64,4096]{1,0:T(8,128)(2,1)S(1)} %bitcast.40), channel_id=1, source_target_pairs={{0,1},{1,0},{2,3},{3,2},{4,5},{5,4},{6,7},{7,6},{8,9},{9,8},{10,11... | collective-permute-start | bytes 1572872 | tf_op jit(solution)/shard_map/ppermute | solution.py:291
  46.8 3.8 %collective-permute-start.2 = (bf16[64,4096]{1,0:T(8,128)(2,1)S(1)}, bf16[64,4096]{1,0:T(8,128)(2,1)S(1)}, u32[]{:S(2)}, u32[]{:S(2)}) collective-permute-start(bf16[64,4096]{1,0:T(8,128)(2,1)S(1)} %get-tuple-element.59), channel_id=1, source_target_pairs={{0,1},{1,0},{2,3},{3,2},{4,5},{5,4},{6,7},{7,6},{8,9},{9,8},{10,11... | collective-permute-start | bytes 1572872 | tf_op jit(solution)/shard_map/ppermute | solution.py:291
  66.5 20.1 %all-to-all-start.3 = ((bf16[8,160,128]{2,1,0:T(8,128)(2,1)}), bf16[8,160,128]{2,1,0:T(8,128)(2,1)S(1)}, u32[]{:S(2)}, u32[]{:S(2)}) async-start(bf16[8,160,128]{2,1,0:T(8,128)(2,1)} %get-tuple-element.62), calls=%async_computation.3 | async-start | bytes 655360 | tf_op jit(solution)/shard_map/all_to_all | solution.py:328
  76.1 7.0 %collective-permute-start.3 = (bf16[8,2048]{1,0:T(8,128)(2,1)S(1)}, bf16[8,2048]{1,0:T(8,128)(2,1)S(1)}, u32[]{:S(2)}, u32[]{:S(2)}) collective-permute-start(bf16[8,2048]{1,0:T(8,128)(2,1)S(1)} %get-tuple-element.63.high), channel_id=1, source_target_pairs={{0,16},{16,32},{32,48},{48,64},{64,80},{80,96},{96,112},{112,128},... | collective-permute-start | bytes 98312 | tf_op jit(solution)/shard_map/ppermute | solution.py:280
  79.4 7.2 %collective-permute-start.4 = (bf16[8,2048]{1,0:T(8,128)(2,1)S(1)}, bf16[8,2048]{1,0:T(8,128)(2,1)S(1)}, u32[]{:S(2)}, u32[]{:S(2)}) collective-permute-start(bf16[8,2048]{1,0:T(8,128)(2,1)S(1)} %get-tuple-element.64.low), channel_id=1, source_target_pairs={{0,496},{16,0},{32,16},{48,32},{64,48},{80,64},{96,80},{112,96},{1... | collective-permute-start | bytes 98312 | tf_op jit(solution)/shard_map/ppermute | solution.py:280
  87.6 18.6 %all-to-all-start.4 = ((bf16[16,16,256]{2,1,0:T(8,128)(2,1)}), bf16[16,16,256]{2,1,0:T(8,128)(2,1)S(1)}, u32[]{:S(2)}, u32[]{:S(2)}) async-start(bf16[16,16,256]{2,1,0:T(8,128)(2,1)} %bitcast.22), calls=%async_computation.4 | async-start | bytes 262144 | tf_op jit(solution)/shard_map/all_to_all | solution.py:407
  94.6 11.6 %collective-permute-start.5 = (bf16[160,128]{1,0:T(8,128)(2,1)S(1)}, bf16[160,128]{1,0:T(8,128)(2,1)S(1)}, u32[]{:S(2)}, u32[]{:S(2)}) collective-permute-start(bf16[160,128]{1,0:T(8,128)(2,1)S(1)} %shard_map.118.one), channel_id=1, source_target_pairs={{0,128},{16,144},{32,160},{48,176},{64,192},{80,208},{96,224},{112... | collective-permute-start | bytes 122888 | tf_op jit(solution)/shard_map/ppermute | solution.py:322
  106.2 9.8 %collective-permute-start.6 = (bf16[160,128]{1,0:T(8,128)(2,1)S(1)}, bf16[160,128]{1,0:T(8,128)(2,1)S(1)}, u32[]{:S(2)}, u32[]{:S(2)}) collective-permute-start(bf16[160,128]{1,0:T(8,128)(2,1)S(1)} %shard_map.119.one), channel_id=1, source_target_pairs={{0,384},{16,400},{32,416},{48,432},{64,448},{80,464},{96,480},{112... | collective-permute-start | bytes 122888 | tf_op jit(solution)/shard_map/ppermute | solution.py:322

commit v7 on v6

--- a/solution.py
+++ b/solution.py
@@ -311,15 +311,16 @@
     return jnp.swapaxes(split, -3, -2).reshape(weight.shape)
 
 
-def partner(value, ends):
-    count = lax.axis_size("space")
-    groups = count // NEAR
+def partner(value, turn):
+    slabs, blocks = lax.axis_size("space"), lax.axis_size("filt")
+    groups = slabs // NEAR
     pairs = []
-    for i in range(count):
-        group = i // NEAR
-        other = ((group + ends) ^ 1) - ends
-        pairs.append((i, other % groups * NEAR + i % NEAR))
-    return lax.ppermute(value, "space", pairs)
+    for s in range(slabs):
+        for f in range(blocks):
+            ends = (turn + f) % 2
+            other = (((s // NEAR + ends) ^ 1) - ends) % groups * NEAR + s % NEAR
+            pairs.append((s * blocks + f, other * blocks + f))
+    return lax.ppermute(value, ("space", "filt"), pairs)
 
 
 def near_exchange(value):

time: 131 us -> 131 us (level)
  waiting for transfers between devices: 28.1 us -> 24.7 us
  starting transfers between devices: 47.6 us -> 49.4 us
    ppermute x2, waiting for transfers between devices: 10.7 us -> 7.31 us  [partner(): return lax.ppermute(value, ('space', 'filt'), pairs)]
    ppermute x2, starting transfers between devices: 10.1 us -> 11.9 us  [partner(): return lax.ppermute(value, ('space', 'filt'), pairs)]
    all_to_all x1, blocking collectives: 13.1 us -> 14.4 us  [near_exchange(): lax.all_to_all(value, 'space', 0, 0, axis_index_groups=groups, tiled=True)]
where the time goes in v7:
time: 131 us; the launch traced here: 130 us
  starting transfers between devices  49.4 us (38%)
  blocking collectives  43 us (33%)
  waiting for transfers between devices  24.7 us (19%)
  Pallas kernels  8.83 us (7%)
  local copies, waits for them, and re-layouts  2.8 us (2%)
    all_to_all x2, blocking collectives, chip_exchange(): lax.all_to_all(value, 'filt', 0, 0, axis_index_groups=groups, tiled=True)  28.6 us
    all_to_all x1, blocking collectives, near_exchange(): lax.all_to_all(value, 'space', 0, 0, axis_index_groups=groups, tiled=True)  14.4 us
    ppermute x2, starting transfers between devices, partner(): return lax.ppermute(value, ('space', 'filt'), pairs)  11.9 us
    all_to_all x1, starting transfers between devices, near_exchange(): lax.all_to_all(value, 'space', 0, 0, axis_index_groups=groups, tiled=True)  9.57 us
    all_to_all x1, starting transfers between devices, pair_gather(): lax.all_to_all(copies, ('space', 'filt'), 0, 0, axis_index_groups=groups,...  9.28 us
    ppermute x2, waiting for transfers between devices, partner(): return lax.ppermute(value, ('space', 'filt'), pairs)  7.31 us
    all_to_all x1, waiting for transfers between devices, pair_gather(): lax.all_to_all(copies, ('space', 'filt'), 0, 0, axis_index_groups=groups,...  7.08 us
    all_to_all x1, starting transfers between devices, per_device(): share = lax.all_to_all(share.reshape(16, 16, 256), 'filt', 0, 0, tiled=True)  6.93 us
  transfers between devices with their start and end apart: 10, of which 7 were waited for; matrix products, arithmetic and copies ran while one was open for 1% of the time, Pallas kernels for 2%

profile of v7, /device:TPU:24, one launch (start us, length us, event | category | flops | bytes accessed | tf_op | source)
XLA Modules:
  0.0 129.9 jit_solution(15639758832972008113)
XLA Ops:
  0.6 0.0 copy-start
  0.6 0.7 copy-done
  1.3 0.7 shard_map.109
  2.1 9.3 %all-to-all-start = ((bf16[32,16,256]{2,1,0:T(8,128)(2,1)}), bf16[32,16,256]{2,1,0:T(8,128)(2,1)S(1)}, u32[]{:S(2)}, u32[]{:S(2)}) async-start(bf16[32,16,256]{2,1,0:T(8,128)(2,1)} %shard_map.109), calls=%async_computation | async-start | bytes 524288 | tf_op jit(solution)/shard_map/all_to_all | solution.py:299
  11.4 0.1 fusion.1
  11.5 0.0 copy-start.4
  11.5 0.0 copy-start.3
  11.5 0.0 copy-start.5
  11.5 7.1 %all-to-all-done = bf16[32,16,256]{2,1,0:T(8,128)(2,1)S(1)} async-done(((bf16[32,16,256]{2,1,0:T(8,128)(2,1)}), bf16[32,16,256]{2,1,0:T(8,128)(2,1)S(1)}, u32[]{:S(2)}, u32[]{:S(2)}) %all-to-all-start) | async-done | bytes 262176 | tf_op jit(solution)/shard_map/all_to_all | solution.py:299
  18.6 0.0 copy-done.4
  18.6 0.1 broadcast_in_dim.4.bias
  18.7 0.0 copy-done.5
  18.7 0.1 broadcast_in_dim.5.bias
  18.8 0.0 copy-done.3
  18.8 0.2 shard_map.110.cot
  19.0 0.0 copy-start.2
  19.0 1.9 %collective-permute-start = (bf16[256,256]{1,0:T(8,128)(2,1)S(1)}, bf16[256,256]{1,0:T(8,128)(2,1)S(1)}, u32[]{:S(2)}, u32[]{:S(2)}) collective-permute-start(bf16[256,256]{1,0:T(8,128)(2,1)S(1)} %dynamic-slice_bitcast_fusion), channel_id=1, source_target_pairs={{0,496},{16,32},{32,16},{48,64},{64,48},{80,96},{96,80},{112,128},... | collective-permute-start | bytes 393224 | tf_op jit(solution)/shard_map/ppermute | solution.py:305
  20.9 0.0 copy-done.2
  21.0 0.2 copy.18
  21.2 0.1 fusion
  21.3 0.2 copy.21
  21.5 0.0 copy-start.1
  21.5 0.2 copy.20
  21.7 0.8 copy-done.1
  22.4 0.1 copy.27
  22.6 0.2 copy.28
  22.7 4.6 %collective-permute-done.outer = bf16[256,256]{1,0:T(8,128)(2,1)S(1)} collective-permute-done((bf16[256,256]{1,0:T(8,128)(2,1)S(1)}, bf16[256,256]{1,0:T(8,128)(2,1)S(1)}, u32[]{:S(2)}, u32[]{:S(2)}) %collective-permute-start) | collective-permute-done | bytes 131104 | tf_op jit(solution)/shard_map/ppermute | solution.py:305
  27.3 0.5 shard_map.111
  27.8 14.1 %all_to_all.30 = bf16[8,8,4096]{2,1,0:T(8,128)(2,1)S(1)} all-to-all(bf16[8,8,4096]{2,1,0:T(8,128)(2,1)S(1)} %get-tuple-element.51), channel_id=1, replica_groups={{0,2,4,6,8,10,12,14},{1,3,5,7,9,11,13,15},{16,18,20,22,24,26,28,30},{17..., dimensions={0} | all-to-all | bytes 1048576 | tf_op jit(solution)/shard_map/all_to_all | solution.py:286
  41.9 1.9 %collective-permute-start.1 = (bf16[64,4096]{1,0:T(8,128)(2,1)S(1)}, bf16[64,4096]{1,0:T(8,128)(2,1)S(1)}, u32[]{:S(2)}, u32[]{:S(2)}) collective-permute-start(bf16[64,4096]{1,0:T(8,128)(2,1)S(1)} %bitcast.40), channel_id=1, source_target_pairs={{0,1},{1,0},{2,3},{3,2},{4,5},{5,4},{6,7},{7,6},{8,9},{9,8},{10,11... | collective-permute-start | bytes 1572872 | tf_op jit(solution)/shard_map/ppermute | solution.py:291
  43.8 0.1 copy.23.turned
  43.9 1.7 %collective-permute-done.1.across = bf16[64,4096]{1,0:T(8,128)(2,1)S(1)} collective-permute-done((bf16[64,4096]{1,0:T(8,128)(2,1)S(1)}, bf16[64,4096]{1,0:T(8,128)(2,1)S(1)}, u32[]{:S(2)}, u32[]{:S(2)}) %collective-permute-start.1) | collective-permute-done | bytes 524320 | tf_op jit(solution)/shard_map/ppermute | solution.py:291
  45.7 1.1 shard_map.112
  46.8 2.0 %collective-permute-start.2 = (bf16[64,4096]{1,0:T(8,128)(2,1)S(1)}, bf16[64,4096]{1,0:T(8,128)(2,1)S(1)}, u32[]{:S(2)}, u32[]{:S(2)}) collective-permute-start(bf16[64,4096]{1,0:T(8,128)(2,1)S(1)} %get-tuple-element.59), channel_id=1, source_target_pairs={{0,1},{1,0},{2,3},{3,2},{4,5},{5,4},{6,7},{7,6},{8,9},{9,8},{10,11... | collective-permute-start | bytes 1572872 | tf_op jit(solution)/shard_map/ppermute | solution.py:291
  48.8 1.3 shard_map.113
  50.1 0.5 collective-permute-done.2.other
  50.6 0.1 shard_map.114
  50.7 14.6 %all_to_all.31.parts = bf16[8,8,4096]{2,1,0:T(8,128)(2,1)S(1)} all-to-all(bf16[8,8,4096]{2,1,0:T(8,128)(2,1)S(1)} %bitcast.43), channel_id=1, replica_groups={{0,2,4,6,8,10,12,14},{1,3,5,7,9,11,13,15},{16,18,20,22,24,26,28,30},{17..., dimensions={0} | all-to-all | bytes 1048576 | tf_op jit(solution)/shard_map/all_to_all | solution.py:286
  65.3 1.2 shard_map.115
  66.5 9.6 %all-to-all-start.3 = ((bf16[8,160,128]{2,1,0:T(8,128)(2,1)}), bf16[8,160,128]{2,1,0:T(8,128)(2,1)S(1)}, u32[]{:S(2)}, u32[]{:S(2)}) async-start(bf16[8,160,128]{2,1,0:T(8,128)(2,1)} %get-tuple-element.62), calls=%async_computation.3 | async-start | bytes 655360 | tf_op jit(solution)/shard_map/all_to_all | solution.py:329
  76.1 3.4 %collective-permute-start.3 = (bf16[8,2048]{1,0:T(8,128)(2,1)S(1)}, bf16[8,2048]{1,0:T(8,128)(2,1)S(1)}, u32[]{:S(2)}, u32[]{:S(2)}) collective-permute-start(bf16[8,2048]{1,0:T(8,128)(2,1)S(1)} %get-tuple-element.63.high), channel_id=1, source_target_pairs={{0,16},{16,32},{32,48},{48,64},{64,80},{80,96},{96,112},{112,128},... | collective-permute-start | bytes 98312 | tf_op jit(solution)/shard_map/ppermute | solution.py:280
  79.4 2.5 %collective-permute-start.4 = (bf16[8,2048]{1,0:T(8,128)(2,1)S(1)}, bf16[8,2048]{1,0:T(8,128)(2,1)S(1)}, u32[]{:S(2)}, u32[]{:S(2)}) collective-permute-start(bf16[8,2048]{1,0:T(8,128)(2,1)S(1)} %get-tuple-element.64.low), channel_id=1, source_target_pairs={{0,496},{16,0},{32,16},{48,32},{64,48},{80,64},{96,80},{112,96},{1... | collective-permute-start | bytes 98312 | tf_op jit(solution)/shard_map/ppermute | solution.py:280
  81.9 0.1 copy.24.weight
  82.1 1.0 shard_map.116
  83.1 0.0 collective-permute-done.3.low_other
  83.1 3.5 %collective-permute-done.4.high_other = bf16[8,2048]{1,0:T(8,128)(2,1)S(1)} collective-permute-done((bf16[8,2048]{1,0:T(8,128)(2,1)S(1)}, bf16[8,2048]{1,0:T(8,128)(2,1)S(1)}, u32[]{:S(2)}, u32[]{:S(2)}) %collective-permute-start.4) | collective-permute-done | bytes 32800 | tf_op jit(solution)/shard_map/ppermute | solution.py:280
  86.6 0.0 all-to-all-done.3.parts
  86.7 1.0 shard_map.117
  87.6 6.9 %all-to-all-start.4 = ((bf16[16,16,256]{2,1,0:T(8,128)(2,1)}), bf16[16,16,256]{2,1,0:T(8,128)(2,1)S(1)}, u32[]{:S(2)}, u32[]{:S(2)}) async-start(bf16[16,16,256]{2,1,0:T(8,128)(2,1)} %bitcast.22), calls=%async_computation.4 | async-start | bytes 262144 | tf_op jit(solution)/shard_map/all_to_all | solution.py:408
  94.6 5.3 %collective-permute-start.5 = (bf16[160,128]{1,0:T(8,128)(2,1)S(1)}, bf16[160,128]{1,0:T(8,128)(2,1)S(1)}, u32[]{:S(2)}, u32[]{:S(2)}) collective-permute-start(bf16[160,128]{1,0:T(8,128)(2,1)S(1)} %shard_map.118.one), channel_id=1, source_target_pairs={{0,128},{1,385},{2,130},{3,387},{4,132},{5,389},{6,134},{7,391},{8... | collective-permute-start | bytes 122888 | tf_op jit(solution)/shard_map/ppermute | solution.py:323
  99.9 4.5 %collective-permute-done.5.other = bf16[160,128]{1,0:T(8,128)(2,1)S(1)} collective-permute-done((bf16[160,128]{1,0:T(8,128)(2,1)S(1)}, bf16[160,128]{1,0:T(8,128)(2,1)S(1)}, u32[]{:S(2)}, u32[]{:S(2)}) %collective-permute-start.5) | collective-permute-done | bytes 40992 | tf_op jit(solution)/shard_map/ppermute | solution.py:323
  104.5 0.0 all-to-all-done.4.parts
  104.5 6.6 %collective-permute-start.6 = (bf16[160,128]{1,0:T(8,128)(2,1)S(1)}, bf16[160,128]{1,0:T(8,128)(2,1)S(1)}, u32[]{:S(2)}, u32[]{:S(2)}) collective-permute-start(bf16[160,128]{1,0:T(8,128)(2,1)S(1)} %shard_map.119.one), channel_id=1, source_target_pairs={{0,384},{1,129},{2,386},{3,131},{4,388},{5,133},{6,390},{7,135},{8... | collective-permute-start | bytes 122888 | tf_op jit(solution)/shard_map/ppermute | solution.py:323
  111.0 0.6 shard_map.120
  111.7 2.8 %collective-permute-done.6.other = bf16[160,128]{1,0:T(8,128)(2,1)S(1)} collective-permute-done((bf16[160,128]{1,0:T(8,128)(2,1)S(1)}, bf16[160,128]{1,0:T(8,128)(2,1)S(1)}, u32[]{:S(2)}, u32[]{:S(2)}) %collective-permute-start.6) | collective-permute-done | bytes 40992 | tf_op jit(solution)/shard_map/ppermute | solution.py:323
  114.5 14.4 %all_to_all.32.refs_0_ = bf16[8,160,128]{2,1,0:T(8,128)(2,1)S(1)} all-to-all(bf16[8,160,128]{2,1,0:T(8,128)(2,1)S(1)} %shard_map.121), channel_id=1, replica_groups={{0,16,32,48,64,80,96,112},{128,144,160,176,192,208,224,240},{256,272,28..., dimensions={0} | all-to-all | bytes 655360 | tf_op jit(solution)/shard_map/all_to_all | solution.py:329
  128.9 1.0 shard_map.122
  (11 shorter events, 0.2 us)
Async XLA Ops:
  0.6 0.7 copy-start
  2.1 16.5 %all-to-all-start = ((bf16[32,16,256]{2,1,0:T(8,128)(2,1)}), bf16[32,16,256]{2,1,0:T(8,128)(2,1)S(1)}, u32[]{:S(2)}, u32[]{:S(2)}) async-start(bf16[32,16,256]{2,1,0:T(8,128)(2,1)} %shard_map.109), calls=%async_computation | async-start | bytes 524288 | tf_op jit(solution)/shard_map/all_to_all | solution.py:299
  11.5 7.1 %copy-start.4 = (bf16[8]{0:T(256)(128)(2,1)S(1)}, bf16[8]{0:T(256)(128)(2,1)}, u32[]{:S(2)}) copy-start(bf16[8]{0:T(256)(128)(2,1)} %param.8) | copy-start | bytes 52
  11.5 7.3 %copy-start.3 = (bf16[2,8,4,256]{3,2,1,0:T(4,128)(2,1)S(1)}, bf16[2,8,4,256]{3,2,1,0:T(4,128)(2,1)}, u32[]{:S(2)}) copy-start(bf16[2,8,4,256]{3,2,1,0:T(4,128)(2,1)} %param.11) | copy-start | bytes 98308
  11.5 7.2 %copy-start.5 = (bf16[8]{0:T(256)(128)(2,1)S(1)}, bf16[8]{0:T(256)(128)(2,1)}, u32[]{:S(2)}) copy-start(bf16[8]{0:T(256)(128)(2,1)} %param.10) | copy-start | bytes 52
  19.0 2.0 %copy-start.2 = (bf16[8,27,128]{2,0,1:T(8,128)(2,1)S(1)}, bf16[8,27,128]{2,0,1:T(8,128)(2,1)}, u32[]{:S(2)}) copy-start(bf16[8,27,128]{2,0,1:T(8,128)(2,1)} %param.9) | copy-start | bytes 165892
  19.0 8.3 %collective-permute-start = (bf16[256,256]{1,0:T(8,128)(2,1)S(1)}, bf16[256,256]{1,0:T(8,128)(2,1)S(1)}, u32[]{:S(2)}, u32[]{:S(2)}) collective-permute-start(bf16[256,256]{1,0:T(8,128)(2,1)S(1)} %dynamic-slice_bitcast_fusion), channel_id=1, source_target_pairs={{0,496},{16,32},{32,16},{48,64},{64,48},{80,96},{96,80},{112,128},... | collective-permute-start | bytes 393224 | tf_op jit(solution)/shard_map/ppermute | solution.py:305
  21.5 1.0 copy-start.1
  41.9 3.8 %collective-permute-start.1 = (bf16[64,4096]{1,0:T(8,128)(2,1)S(1)}, bf16[64,4096]{1,0:T(8,128)(2,1)S(1)}, u32[]{:S(2)}, u32[]{:S(2)}) collective-permute-start(bf16[64,4096]{1,0:T(8,128)(2,1)S(1)} %bitcast.40), channel_id=1, source_target_pairs={{0,1},{1,0},{2,3},{3,2},{4,5},{5,4},{6,7},{7,6},{8,9},{9,8},{10,11... | collective-permute-start | bytes 1572872 | tf_op jit(solution)/shard_map/ppermute | solution.py:291
  46.8 3.8 %collective-permute-start.2 = (bf16[64,4096]{1,0:T(8,128)(2,1)S(1)}, bf16[64,4096]{1,0:T(8,128)(2,1)S(1)}, u32[]{:S(2)}, u32[]{:S(2)}) collective-permute-start(bf16[64,4096]{1,0:T(8,128)(2,1)S(1)} %get-tuple-element.59), channel_id=1, source_target_pairs={{0,1},{1,0},{2,3},{3,2},{4,5},{5,4},{6,7},{7,6},{8,9},{9,8},{10,11... | collective-permute-start | bytes 1572872 | tf_op jit(solution)/shard_map/ppermute | solution.py:291
  66.5 20.1 %all-to-all-start.3 = ((bf16[8,160,128]{2,1,0:T(8,128)(2,1)}), bf16[8,160,128]{2,1,0:T(8,128)(2,1)S(1)}, u32[]{:S(2)}, u32[]{:S(2)}) async-start(bf16[8,160,128]{2,1,0:T(8,128)(2,1)} %get-tuple-element.62), calls=%async_computation.3 | async-start | bytes 655360 | tf_op jit(solution)/shard_map/all_to_all | solution.py:329
  76.1 7.0 %collective-permute-start.3 = (bf16[8,2048]{1,0:T(8,128)(2,1)S(1)}, bf16[8,2048]{1,0:T(8,128)(2,1)S(1)}, u32[]{:S(2)}, u32[]{:S(2)}) collective-permute-start(bf16[8,2048]{1,0:T(8,128)(2,1)S(1)} %get-tuple-element.63.high), channel_id=1, source_target_pairs={{0,16},{16,32},{32,48},{48,64},{64,80},{80,96},{96,112},{112,128},... | collective-permute-start | bytes 98312 | tf_op jit(solution)/shard_map/ppermute | solution.py:280
  79.4 7.2 %collective-permute-start.4 = (bf16[8,2048]{1,0:T(8,128)(2,1)S(1)}, bf16[8,2048]{1,0:T(8,128)(2,1)S(1)}, u32[]{:S(2)}, u32[]{:S(2)}) collective-permute-start(bf16[8,2048]{1,0:T(8,128)(2,1)S(1)} %get-tuple-element.64.low), channel_id=1, source_target_pairs={{0,496},{16,0},{32,16},{48,32},{64,48},{80,64},{96,80},{112,96},{1... | collective-permute-start | bytes 98312 | tf_op jit(solution)/shard_map/ppermute | solution.py:280
  87.6 16.8 %all-to-all-start.4 = ((bf16[16,16,256]{2,1,0:T(8,128)(2,1)}), bf16[16,16,256]{2,1,0:T(8,128)(2,1)S(1)}, u32[]{:S(2)}, u32[]{:S(2)}) async-start(bf16[16,16,256]{2,1,0:T(8,128)(2,1)} %bitcast.22), calls=%async_computation.4 | async-start | bytes 262144 | tf_op jit(solution)/shard_map/all_to_all | solution.py:408
  94.6 9.9 %collective-permute-start.5 = (bf16[160,128]{1,0:T(8,128)(2,1)S(1)}, bf16[160,128]{1,0:T(8,128)(2,1)S(1)}, u32[]{:S(2)}, u32[]{:S(2)}) collective-permute-start(bf16[160,128]{1,0:T(8,128)(2,1)S(1)} %shard_map.118.one), channel_id=1, source_target_pairs={{0,128},{1,385},{2,130},{3,387},{4,132},{5,389},{6,134},{7,391},{8... | collective-permute-start | bytes 122888 | tf_op jit(solution)/shard_map/ppermute | solution.py:323
  104.5 10.0 %collective-permute-start.6 = (bf16[160,128]{1,0:T(8,128)(2,1)S(1)}, bf16[160,128]{1,0:T(8,128)(2,1)S(1)}, u32[]{:S(2)}, u32[]{:S(2)}) collective-permute-start(bf16[160,128]{1,0:T(8,128)(2,1)S(1)} %shard_map.119.one), channel_id=1, source_target_pairs={{0,384},{1,129},{2,386},{3,131},{4,388},{5,133},{6,390},{7,135},{8... | collective-permute-start | bytes 122888 | tf_op jit(solution)/shard_map/ppermute | solution.py:323

commit v8 on v7

--- a/solution.py
+++ b/solution.py
@@ -79,8 +79,9 @@
                     out[copy, :, col : col + LANE] = value
 
 
-def copies_kernel(field, out):
-    rows = field[...].astype(F32)
+def copies_kernel(field, out, local):
+    pltpu.sync_copy(field, local)
+    rows = local[...].astype(F32)
     plane = jnp.concatenate([rows[:, 0, :], rows[:, 1, :]], axis=1).astype(BF16)
     for i in range(out.shape[0]):
         out[i] = plane
@@ -334,7 +335,13 @@
     wide = lambda bias: jnp.broadcast_to(bias.astype(F32)[:, None], (8, LANE))
     core = lax.axis_index("filt") % 2
     odd = lax.axis_index("space") % 2
-    copies = vmem_call(copies_kernel, struct((32, 16, 256), BF16))(volume.reshape(16, 2, LANE))
+    copies = vmem_call(
+        copies_kernel,
+        struct((32, 16, 256), BF16),
+        [pltpu.VMEM((16, 2, LANE), BF16)],
+        [pl.BlockSpec(memory_space=pl.ANY)],
+        60 * 1024 * 1024,
+    )(volume.reshape(16, 2, LANE))
     pair = pair_gather(copies).reshape(2, 256, 256)
     given = (first_weight, wide(first_bias), second_weight, wide(second_bias), cotangent)
     pair, given = lax.optimization_barrier((pair, given))

time: 131 us -> 131 us (level)
  no operation moved by 1% of the time
where the time goes in v8:
time: 131 us; the launch traced here: 130 us
  starting transfers between devices  49.4 us (38%)
  blocking collectives  43 us (33%)
  waiting for transfers between devices  24.7 us (19%)
  Pallas kernels  9.53 us (7%)
  local copies, waits for them, and re-layouts  2.12 us (2%)
    all_to_all x2, blocking collectives, chip_exchange(): lax.all_to_all(value, 'filt', 0, 0, axis_index_groups=groups, tiled=True)  28.6 us
    all_to_all x1, blocking collectives, near_exchange(): lax.all_to_all(value, 'space', 0, 0, axis_index_groups=groups, tiled=True)  14.4 us
    ppermute x2, starting transfers between devices, partner(): return lax.ppermute(value, ('space', 'filt'), pairs)  11.9 us
    all_to_all x1, starting transfers between devices, near_exchange(): lax.all_to_all(value, 'space', 0, 0, axis_index_groups=groups, tiled=True)  9.57 us
    all_to_all x1, starting transfers between devices, pair_gather(): lax.all_to_all(copies, ('space', 'filt'), 0, 0, axis_index_groups=groups,...  9.27 us
    ppermute x2, waiting for transfers between devices, partner(): return lax.ppermute(value, ('space', 'filt'), pairs)  7.3 us
    all_to_all x1, waiting for transfers between devices, pair_gather(): lax.all_to_all(copies, ('space', 'filt'), 0, 0, axis_index_groups=groups,...  7.08 us
    all_to_all x1, starting transfers between devices, per_device(): share = lax.all_to_all(share.reshape(16, 16, 256), 'filt', 0, 0, tiled=True)  6.93 us
  transfers between devices with their start and end apart: 10, of which 7 were waited for; matrix products, arithmetic and copies ran while one was open for 1% of the time, Pallas kernels for 2%

profile of v8, /device:TPU:24, one launch (start us, length us, event | category | flops | bytes accessed | tf_op | source)
XLA Modules:
  0.0 129.9 jit_solution(2498517087111587419)
XLA Ops:
  0.6 1.4 %shard_map.109 = bf16[32,16,256]{2,1,0:T(8,128)(2,1)} custom-call(bf16[16,2,128]{2,1,0:T(2,128)(2,1)} %bitcast.56), custom_call_target="tpu_custom_call" | custom-call | tf_op jit(solution)/shard_map/pallas_call | solution.py:338
  2.1 9.3 %all-to-all-start = ((bf16[32,16,256]{2,1,0:T(8,128)(2,1)}), bf16[32,16,256]{2,1,0:T(8,128)(2,1)S(1)}, u32[]{:S(2)}, u32[]{:S(2)}) async-start(bf16[32,16,256]{2,1,0:T(8,128)(2,1)} %shard_map.109), calls=%async_computation | async-start | bytes 524288 | tf_op jit(solution)/shard_map/all_to_all | solution.py:300
  11.4 0.1 fusion.1
  11.5 0.0 copy-start.3
  11.5 0.0 copy-start.2
  11.5 0.0 copy-start.4
  11.5 7.1 %all-to-all-done = bf16[32,16,256]{2,1,0:T(8,128)(2,1)S(1)} async-done(((bf16[32,16,256]{2,1,0:T(8,128)(2,1)}), bf16[32,16,256]{2,1,0:T(8,128)(2,1)S(1)}, u32[]{:S(2)}, u32[]{:S(2)}) %all-to-all-start) | async-done | bytes 262176 | tf_op jit(solution)/shard_map/all_to_all | solution.py:300
  18.6 0.0 copy-done.3
  18.6 0.1 broadcast_in_dim.4.bias
  18.7 0.0 copy-done.4
  18.7 0.1 broadcast_in_dim.5.bias
  18.8 0.0 copy-done.2
  18.8 0.2 shard_map.110.cot
  19.0 0.0 copy-start.1
  19.0 1.9 %collective-permute-start = (bf16[256,256]{1,0:T(8,128)(2,1)S(1)}, bf16[256,256]{1,0:T(8,128)(2,1)S(1)}, u32[]{:S(2)}, u32[]{:S(2)}) collective-permute-start(bf16[256,256]{1,0:T(8,128)(2,1)S(1)} %dynamic-slice_bitcast_fusion), channel_id=1, source_target_pairs={{0,496},{16,32},{32,16},{48,64},{64,48},{80,96},{96,80},{112,128},... | collective-permute-start | bytes 393224 | tf_op jit(solution)/shard_map/ppermute | solution.py:306
  20.9 0.0 copy-done.1
  21.0 0.2 copy.18
  21.2 0.1 fusion
  21.3 0.2 copy.21
  21.5 0.0 copy-start
  21.5 0.2 copy.20
  21.7 0.8 copy-done
  22.4 0.1 copy.27
  22.6 0.2 copy.28
  22.8 4.6 %collective-permute-done.outer = bf16[256,256]{1,0:T(8,128)(2,1)S(1)} collective-permute-done((bf16[256,256]{1,0:T(8,128)(2,1)S(1)}, bf16[256,256]{1,0:T(8,128)(2,1)S(1)}, u32[]{:S(2)}, u32[]{:S(2)}) %collective-permute-start) | collective-permute-done | bytes 131104 | tf_op jit(solution)/shard_map/ppermute | solution.py:306
  27.3 0.5 shard_map.111
  27.8 14.1 %all_to_all.30 = bf16[8,8,4096]{2,1,0:T(8,128)(2,1)S(1)} all-to-all(bf16[8,8,4096]{2,1,0:T(8,128)(2,1)S(1)} %get-tuple-element.51), channel_id=1, replica_groups={{0,2,4,6,8,10,12,14},{1,3,5,7,9,11,13,15},{16,18,20,22,24,26,28,30},{17..., dimensions={0} | all-to-all | bytes 1048576 | tf_op jit(solution)/shard_map/all_to_all | solution.py:287
  41.9 1.9 %collective-permute-start.1 = (bf16[64,4096]{1,0:T(8,128)(2,1)S(1)}, bf16[64,4096]{1,0:T(8,128)(2,1)S(1)}, u32[]{:S(2)}, u32[]{:S(2)}) collective-permute-start(bf16[64,4096]{1,0:T(8,128)(2,1)S(1)} %bitcast.40), channel_id=1, source_target_pairs={{0,1},{1,0},{2,3},{3,2},{4,5},{5,4},{6,7},{7,6},{8,9},{9,8},{10,11... | collective-permute-start | bytes 1572872 | tf_op jit(solution)/shard_map/ppermute | solution.py:292
  43.8 0.1 copy.23.turned
  43.9 1.7 %collective-permute-done.1.across = bf16[64,4096]{1,0:T(8,128)(2,1)S(1)} collective-permute-done((bf16[64,4096]{1,0:T(8,128)(2,1)S(1)}, bf16[64,4096]{1,0:T(8,128)(2,1)S(1)}, u32[]{:S(2)}, u32[]{:S(2)}) %collective-permute-start.1) | collective-permute-done | bytes 524320 | tf_op jit(solution)/shard_map/ppermute | solution.py:292
  45.7 1.1 shard_map.112
  46.8 2.0 %collective-permute-start.2 = (bf16[64,4096]{1,0:T(8,128)(2,1)S(1)}, bf16[64,4096]{1,0:T(8,128)(2,1)S(1)}, u32[]{:S(2)}, u32[]{:S(2)}) collective-permute-start(bf16[64,4096]{1,0:T(8,128)(2,1)S(1)} %get-tuple-element.59), channel_id=1, source_target_pairs={{0,1},{1,0},{2,3},{3,2},{4,5},{5,4},{6,7},{7,6},{8,9},{9,8},{10,11... | collective-permute-start | bytes 1572872 | tf_op jit(solution)/shard_map/ppermute | solution.py:292
  48.8 1.3 shard_map.113
  50.1 0.5 collective-permute-done.2.other
  50.6 0.1 shard_map.114
  50.7 14.6 %all_to_all.31.parts = bf16[8,8,4096]{2,1,0:T(8,128)(2,1)S(1)} all-to-all(bf16[8,8,4096]{2,1,0:T(8,128)(2,1)S(1)} %bitcast.43), channel_id=1, replica_groups={{0,2,4,6,8,10,12,14},{1,3,5,7,9,11,13,15},{16,18,20,22,24,26,28,30},{17..., dimensions={0} | all-to-all | bytes 1048576 | tf_op jit(solution)/shard_map/all_to_all | solution.py:287
  65.3 1.2 shard_map.115
  66.5 9.6 %all-to-all-start.3 = ((bf16[8,160,128]{2,1,0:T(8,128)(2,1)}), bf16[8,160,128]{2,1,0:T(8,128)(2,1)S(1)}, u32[]{:S(2)}, u32[]{:S(2)}) async-start(bf16[8,160,128]{2,1,0:T(8,128)(2,1)} %get-tuple-element.62), calls=%async_computation.3 | async-start | bytes 655360 | tf_op jit(solution)/shard_map/all_to_all | solution.py:330
  76.1 3.4 %collective-permute-start.3 = (bf16[8,2048]{1,0:T(8,128)(2,1)S(1)}, bf16[8,2048]{1,0:T(8,128)(2,1)S(1)}, u32[]{:S(2)}, u32[]{:S(2)}) collective-permute-start(bf16[8,2048]{1,0:T(8,128)(2,1)S(1)} %get-tuple-element.63.high), channel_id=1, source_target_pairs={{0,16},{16,32},{32,48},{48,64},{64,80},{80,96},{96,112},{112,128},... | collective-permute-start | bytes 98312 | tf_op jit(solution)/shard_map/ppermute | solution.py:281
  79.4 2.5 %collective-permute-start.4 = (bf16[8,2048]{1,0:T(8,128)(2,1)S(1)}, bf16[8,2048]{1,0:T(8,128)(2,1)S(1)}, u32[]{:S(2)}, u32[]{:S(2)}) collective-permute-start(bf16[8,2048]{1,0:T(8,128)(2,1)S(1)} %get-tuple-element.64.low), channel_id=1, source_target_pairs={{0,496},{16,0},{32,16},{48,32},{64,48},{80,64},{96,80},{112,96},{1... | collective-permute-start | bytes 98312 | tf_op jit(solution)/shard_map/ppermute | solution.py:281
  81.9 0.1 copy.24.weight
  82.1 1.0 shard_map.116
  83.1 0.0 collective-permute-done.3.low_other
  83.1 3.5 %collective-permute-done.4.high_other = bf16[8,2048]{1,0:T(8,128)(2,1)S(1)} collective-permute-done((bf16[8,2048]{1,0:T(8,128)(2,1)S(1)}, bf16[8,2048]{1,0:T(8,128)(2,1)S(1)}, u32[]{:S(2)}, u32[]{:S(2)}) %collective-permute-start.4) | collective-permute-done | bytes 32800 | tf_op jit(solution)/shard_map/ppermute | solution.py:281
  86.6 0.0 all-to-all-done.3.parts
  86.7 1.0 shard_map.117
  87.6 6.9 %all-to-all-start.4 = ((bf16[16,16,256]{2,1,0:T(8,128)(2,1)}), bf16[16,16,256]{2,1,0:T(8,128)(2,1)S(1)}, u32[]{:S(2)}, u32[]{:S(2)}) async-start(bf16[16,16,256]{2,1,0:T(8,128)(2,1)} %bitcast.22), calls=%async_computation.4 | async-start | bytes 262144 | tf_op jit(solution)/shard_map/all_to_all | solution.py:415
  94.6 5.4 %collective-permute-start.5 = (bf16[160,128]{1,0:T(8,128)(2,1)S(1)}, bf16[160,128]{1,0:T(8,128)(2,1)S(1)}, u32[]{:S(2)}, u32[]{:S(2)}) collective-permute-start(bf16[160,128]{1,0:T(8,128)(2,1)S(1)} %shard_map.118.one), channel_id=1, source_target_pairs={{0,128},{1,385},{2,130},{3,387},{4,132},{5,389},{6,134},{7,391},{8... | collective-permute-start | bytes 122888 | tf_op jit(solution)/shard_map/ppermute | solution.py:324
  99.9 4.5 %collective-permute-done.5.other = bf16[160,128]{1,0:T(8,128)(2,1)S(1)} collective-permute-done((bf16[160,128]{1,0:T(8,128)(2,1)S(1)}, bf16[160,128]{1,0:T(8,128)(2,1)S(1)}, u32[]{:S(2)}, u32[]{:S(2)}) %collective-permute-start.5) | collective-permute-done | bytes 40992 | tf_op jit(solution)/shard_map/ppermute | solution.py:324
  104.5 0.0 all-to-all-done.4.parts
  104.5 6.6 %collective-permute-start.6 = (bf16[160,128]{1,0:T(8,128)(2,1)S(1)}, bf16[160,128]{1,0:T(8,128)(2,1)S(1)}, u32[]{:S(2)}, u32[]{:S(2)}) collective-permute-start(bf16[160,128]{1,0:T(8,128)(2,1)S(1)} %shard_map.119.one), channel_id=1, source_target_pairs={{0,384},{1,129},{2,386},{3,131},{4,388},{5,133},{6,390},{7,135},{8... | collective-permute-start | bytes 122888 | tf_op jit(solution)/shard_map/ppermute | solution.py:324
  111.1 0.6 shard_map.120
  111.7 2.8 %collective-permute-done.6.other = bf16[160,128]{1,0:T(8,128)(2,1)S(1)} collective-permute-done((bf16[160,128]{1,0:T(8,128)(2,1)S(1)}, bf16[160,128]{1,0:T(8,128)(2,1)S(1)}, u32[]{:S(2)}, u32[]{:S(2)}) %collective-permute-start.6) | collective-permute-done | bytes 40992 | tf_op jit(solution)/shard_map/ppermute | solution.py:324
  114.5 14.4 %all_to_all.32.refs_0_ = bf16[8,160,128]{2,1,0:T(8,128)(2,1)S(1)} all-to-all(bf16[8,160,128]{2,1,0:T(8,128)(2,1)S(1)} %shard_map.121), channel_id=1, replica_groups={{0,16,32,48,64,80,96,112},{128,144,160,176,192,208,224,240},{256,272,28..., dimensions={0} | all-to-all | bytes 655360 | tf_op jit(solution)/shard_map/all_to_all | solution.py:330
  128.9 1.0 shard_map.122
  (11 shorter events, 0.2 us)
Async XLA Ops:
  2.1 16.5 %all-to-all-start = ((bf16[32,16,256]{2,1,0:T(8,128)(2,1)}), bf16[32,16,256]{2,1,0:T(8,128)(2,1)S(1)}, u32[]{:S(2)}, u32[]{:S(2)}) async-start(bf16[32,16,256]{2,1,0:T(8,128)(2,1)} %shard_map.109), calls=%async_computation | async-start | bytes 524288 | tf_op jit(solution)/shard_map/all_to_all | solution.py:300
  11.5 7.1 %copy-start.3 = (bf16[8]{0:T(256)(128)(2,1)S(1)}, bf16[8]{0:T(256)(128)(2,1)}, u32[]{:S(2)}) copy-start(bf16[8]{0:T(256)(128)(2,1)} %param.8) | copy-start | bytes 52
  11.5 7.3 %copy-start.2 = (bf16[2,8,4,256]{3,2,1,0:T(4,128)(2,1)S(1)}, bf16[2,8,4,256]{3,2,1,0:T(4,128)(2,1)}, u32[]{:S(2)}) copy-start(bf16[2,8,4,256]{3,2,1,0:T(4,128)(2,1)} %param.11) | copy-start | bytes 98308
  11.5 7.2 %copy-start.4 = (bf16[8]{0:T(256)(128)(2,1)S(1)}, bf16[8]{0:T(256)(128)(2,1)}, u32[]{:S(2)}) copy-start(bf16[8]{0:T(256)(128)(2,1)} %param.10) | copy-start | bytes 52
  19.0 2.0 %copy-start.1 = (bf16[8,27,128]{2,0,1:T(8,128)(2,1)S(1)}, bf16[8,27,128]{2,0,1:T(8,128)(2,1)}, u32[]{:S(2)}) copy-start(bf16[8,27,128]{2,0,1:T(8,128)(2,1)} %param.9) | copy-start | bytes 165892
  19.0 8.3 %collective-permute-start = (bf16[256,256]{1,0:T(8,128)(2,1)S(1)}, bf16[256,256]{1,0:T(8,128)(2,1)S(1)}, u32[]{:S(2)}, u32[]{:S(2)}) collective-permute-start(bf16[256,256]{1,0:T(8,128)(2,1)S(1)} %dynamic-slice_bitcast_fusion), channel_id=1, source_target_pairs={{0,496},{16,32},{32,16},{48,64},{64,48},{80,96},{96,80},{112,128},... | collective-permute-start | bytes 393224 | tf_op jit(solution)/shard_map/ppermute | solution.py:306
  21.5 1.0 copy-start
  41.9 3.8 %collective-permute-start.1 = (bf16[64,4096]{1,0:T(8,128)(2,1)S(1)}, bf16[64,4096]{1,0:T(8,128)(2,1)S(1)}, u32[]{:S(2)}, u32[]{:S(2)}) collective-permute-start(bf16[64,4096]{1,0:T(8,128)(2,1)S(1)} %bitcast.40), channel_id=1, source_target_pairs={{0,1},{1,0},{2,3},{3,2},{4,5},{5,4},{6,7},{7,6},{8,9},{9,8},{10,11... | collective-permute-start | bytes 1572872 | tf_op jit(solution)/shard_map/ppermute | solution.py:292
  46.8 3.8 %collective-permute-start.2 = (bf16[64,4096]{1,0:T(8,128)(2,1)S(1)}, bf16[64,4096]{1,0:T(8,128)(2,1)S(1)}, u32[]{:S(2)}, u32[]{:S(2)}) collective-permute-start(bf16[64,4096]{1,0:T(8,128)(2,1)S(1)} %get-tuple-element.59), channel_id=1, source_target_pairs={{0,1},{1,0},{2,3},{3,2},{4,5},{5,4},{6,7},{7,6},{8,9},{9,8},{10,11... | collective-permute-start | bytes 1572872 | tf_op jit(solution)/shard_map/ppermute | solution.py:292
  66.5 20.1 %all-to-all-start.3 = ((bf16[8,160,128]{2,1,0:T(8,128)(2,1)}), bf16[8,160,128]{2,1,0:T(8,128)(2,1)S(1)}, u32[]{:S(2)}, u32[]{:S(2)}) async-start(bf16[8,160,128]{2,1,0:T(8,128)(2,1)} %get-tuple-element.62), calls=%async_computation.3 | async-start | bytes 655360 | tf_op jit(solution)/shard_map/all_to_all | solution.py:330
  76.1 7.0 %collective-permute-start.3 = (bf16[8,2048]{1,0:T(8,128)(2,1)S(1)}, bf16[8,2048]{1,0:T(8,128)(2,1)S(1)}, u32[]{:S(2)}, u32[]{:S(2)}) collective-permute-start(bf16[8,2048]{1,0:T(8,128)(2,1)S(1)} %get-tuple-element.63.high), channel_id=1, source_target_pairs={{0,16},{16,32},{32,48},{48,64},{64,80},{80,96},{96,112},{112,128},... | collective-permute-start | bytes 98312 | tf_op jit(solution)/shard_map/ppermute | solution.py:281
  79.4 7.2 %collective-permute-start.4 = (bf16[8,2048]{1,0:T(8,128)(2,1)S(1)}, bf16[8,2048]{1,0:T(8,128)(2,1)S(1)}, u32[]{:S(2)}, u32[]{:S(2)}) collective-permute-start(bf16[8,2048]{1,0:T(8,128)(2,1)S(1)} %get-tuple-element.64.low), channel_id=1, source_target_pairs={{0,496},{16,0},{32,16},{48,32},{64,48},{80,64},{96,80},{112,96},{1... | collective-permute-start | bytes 98312 | tf_op jit(solution)/shard_map/ppermute | solution.py:281
  87.6 16.8 %all-to-all-start.4 = ((bf16[16,16,256]{2,1,0:T(8,128)(2,1)}), bf16[16,16,256]{2,1,0:T(8,128)(2,1)S(1)}, u32[]{:S(2)}, u32[]{:S(2)}) async-start(bf16[16,16,256]{2,1,0:T(8,128)(2,1)} %bitcast.22), calls=%async_computation.4 | async-start | bytes 262144 | tf_op jit(solution)/shard_map/all_to_all | solution.py:415
  94.6 9.9 %collective-permute-start.5 = (bf16[160,128]{1,0:T(8,128)(2,1)S(1)}, bf16[160,128]{1,0:T(8,128)(2,1)S(1)}, u32[]{:S(2)}, u32[]{:S(2)}) collective-permute-start(bf16[160,128]{1,0:T(8,128)(2,1)S(1)} %shard_map.118.one), channel_id=1, source_target_pairs={{0,128},{1,385},{2,130},{3,387},{4,132},{5,389},{6,134},{7,391},{8... | collective-permute-start | bytes 122888 | tf_op jit(solution)/shard_map/ppermute | solution.py:324
  104.5 10.0 %collective-permute-start.6 = (bf16[160,128]{1,0:T(8,128)(2,1)S(1)}, bf16[160,128]{1,0:T(8,128)(2,1)S(1)}, u32[]{:S(2)}, u32[]{:S(2)}) collective-permute-start(bf16[160,128]{1,0:T(8,128)(2,1)S(1)} %shard_map.119.one), channel_id=1, source_target_pairs={{0,384},{1,129},{2,386},{3,131},{4,388},{5,133},{6,390},{7,135},{8... | collective-permute-start | bytes 122888 | tf_op jit(solution)/shard_map/ppermute | solution.py:324
